TPU v7x, 512 devices: a whole 4x4x16 slice. The times are simulated.
512 devices in a mesh: section: 2 (over core), dp: 32 (over x_lo, z), tensor: 8 (over y, x_hi).
Axes of the slice: x: 4 (x_hi: 2, x_lo: 2; x = x_hi * 2 + x_lo), y: 4, z: 16, core: 2. Of those that a mesh axis runs over, the one named last changes fastest.
Arguments:
- projections: bfloat16 [2, 3, 8192, 6144], P('section', None, 'dp', 'tensor'), may hold values from -5 to 5
- out_grad: bfloat16 [8192, 6144], P('dp', 'tensor'), may hold values from -6 to 6
Outputs:
- grads: bfloat16 [2, 3, 8192, 6144], P('section', None, 'dp', 'tensor')
All inputs are finite; a program needn't handle non-finite values.
Results may differ from a plain program's by a relative error of at most 0.01.
Values may be sent and summed in bfloat16 or wider, within the bound.
No kernel may reach another device: no remote copies, remote signals or barrier semaphores. Data moves between devices by JAX's collectives and lax.ppermute only.
A program may use at most 128 MiB of HBM per device.

v0:
```python
import math

import jax
import jax.numpy as jnp
from jax import lax
from jax.sharding import PartitionSpec as P

HD = 128


def passed_along(shard, axis, by):
    size = lax.axis_size(axis)
    pairs = [(i, i + by) for i in range(size) if 0 <= i + by < size]
    return lax.ppermute(shard, axis, pairs)


def swapped(value, axis, stride):
    mask = 2**stride
    pairs = [(source, source ^ mask) for source in range(lax.axis_size(axis))]
    return lax.ppermute(value, axis, pairs)


def split_heads(matrix):
    return matrix.reshape(matrix.shape[0], matrix.shape[1] // HD, HD).transpose(1, 0, 2)


def join_heads(stacked):
    return stacked.transpose(1, 0, 2).reshape(stacked.shape[1], stacked.shape[0] * HD)


def visible(query_rows, block_rows, offset, place):
    query_pos = lax.broadcasted_iota(jnp.int32, (query_rows, 4 * block_rows), 0) + offset
    key_pos = lax.broadcasted_iota(jnp.int32, (query_rows, 4 * block_rows), 1)
    block = key_pos // block_rows
    within = key_pos % block_rows
    return jnp.where(block == 0, within <= query_pos, block <= place)


def fetch_earlier(pair):
    blocks = [pair] + [passed_along(pair, "dp", step) for step in range(1, 4)]
    return jnp.stack(blocks)


def return_to_owners(terms, block_rows):
    pieces = [terms[:, block * block_rows : (block + 1) * block_rows] for block in range(4)]
    total = pieces[0].astype(jnp.float32)
    for step in range(1, 4):
        total = total + passed_along(pieces[step], "dp", -step).astype(jnp.float32)
    return total


def attend_forward(query, key_all, value_all, visible_mask, scale):

    def single(item):
        q_head, k_head, v_head = item
        scores = jnp.dot(q_head, k_head.T, preferred_element_type=jnp.float32) * scale
        scores = jnp.where(visible_mask, scores, -jnp.inf)
        top = jnp.max(scores, axis=1, keepdims=True)
        lse = top + jnp.log(jnp.sum(jnp.exp(scores - top), axis=1, keepdims=True))
        probs = jnp.exp(scores - lse).astype(jnp.bfloat16)
        out = jnp.dot(probs, v_head, preferred_element_type=jnp.float32).astype(jnp.bfloat16)
        return (out, lse)

    out, lse = lax.map(single, (split_heads(query), split_heads(key_all), split_heads(value_all)))
    return (join_heads(out), lse)


def attend_backward(query, key_all, value_all, out, lse, grad_out, visible_mask, scale):

    def single(item):
        q_head, k_head, v_head, o_head, lse_rows, g_head = item
        scores = jnp.dot(q_head, k_head.T, preferred_element_type=jnp.float32) * scale
        probs = jnp.exp(jnp.where(visible_mask, scores, -jnp.inf) - lse_rows)
        delta = jnp.sum(
            g_head.astype(jnp.float32) * o_head.astype(jnp.float32), axis=1, keepdims=True
        )
        dvals = jnp.dot(
            probs.astype(jnp.bfloat16).T, g_head, preferred_element_type=jnp.float32
        ).astype(jnp.bfloat16)
        dprobs = jnp.dot(g_head, v_head.T, preferred_element_type=jnp.float32)
        dscore = (probs * (dprobs - delta)).astype(jnp.bfloat16)
        dquery = (jnp.dot(dscore, k_head, preferred_element_type=jnp.float32) * scale).astype(
            jnp.bfloat16
        )
        dkeys = (jnp.dot(dscore.T, q_head, preferred_element_type=jnp.float32) * scale).astype(
            jnp.bfloat16
        )
        return (dquery, dkeys, dvals)

    items = (
        split_heads(query),
        split_heads(key_all),
        split_heads(value_all),
        split_heads(out),
        lse,
        split_heads(grad_out),
    )
    dquery, dkeys, dvals = lax.map(single, items)
    return (join_heads(dquery), jnp.stack([join_heads(dkeys), join_heads(dvals)]))


def body(projections, out_grad):
    is_first = lax.axis_index("section") == 0
    place = lax.axis_index("dp") % 4
    parity = lax.axis_index("tensor") % 2
    local = projections[0]
    rows, columns = (local.shape[1], local.shape[2])
    half_rows = rows // 2
    pair_width = 2 * columns
    scale = 1.0 / math.sqrt(HD)
    own_pair = local[1:3].reshape(2, half_rows, pair_width)
    partner_pair = swapped(own_pair, "tensor", 0)
    own_cols = local[1:3]
    partner_cols = partner_pair.reshape(2, rows, columns)
    block_first = jnp.where(
        parity == 0,
        jnp.concatenate([own_cols, partner_cols], axis=2),
        jnp.concatenate([partner_cols, own_cols], axis=2),
    )
    block_second = jnp.where(
        parity == 0,
        jnp.concatenate([own_pair, partner_pair], axis=1),
        jnp.concatenate([partner_pair, own_pair], axis=1),
    )
    gathered = fetch_earlier(jnp.where(is_first, block_first, block_second))
    key_all = gathered[:, 0].reshape(4 * rows, pair_width)
    value_all = gathered[:, 1].reshape(4 * rows, pair_width)
    key_first = lax.dynamic_slice_in_dim(key_all, parity * columns, columns, 1)
    value_first = lax.dynamic_slice_in_dim(value_all, parity * columns, columns, 1)
    mask_first = visible(rows, rows, 0, place)
    mask_second = visible(half_rows, rows, parity * half_rows, place)
    zero_out = jnp.zeros((rows, columns), jnp.bfloat16)
    zero_lse = jnp.zeros((columns // HD, rows, 1), jnp.float32)
    first_out, first_lse = lax.cond(
        is_first,
        lambda: attend_forward(local[0], key_first, value_first, mask_first, scale),
        lambda: (zero_out, zero_lse),
    )
    outgoing = lax.dynamic_slice_in_dim(first_out, (1 - parity) * half_rows, half_rows, 0)
    received = swapped(outgoing, "tensor", 0)
    kept = lax.dynamic_slice_in_dim(first_out, parity * half_rows, half_rows, 0)
    relayed = jnp.where(
        parity == 0,
        jnp.concatenate([kept, received], axis=1),
        jnp.concatenate([received, kept], axis=1),
    )
    arrived = passed_along(relayed, "section", 1)
    local_second = local.reshape(3, half_rows, pair_width)
    second_query = (local_second[0].astype(jnp.float32) + arrived.astype(jnp.float32)).astype(
        jnp.bfloat16
    )
    grad_second = out_grad.reshape(half_rows, pair_width)
    zero_half = jnp.zeros((half_rows, pair_width), jnp.bfloat16)
    zero_half_lse = jnp.zeros((pair_width // HD, half_rows, 1), jnp.float32)
    zero_terms = jnp.zeros((2, 4 * rows, pair_width), jnp.bfloat16)
    second_out, second_lse = lax.cond(
        is_first,
        lambda: (zero_half, zero_half_lse),
        lambda: attend_forward(second_query, key_all, value_all, mask_second, scale),
    )
    dq_two, terms_two = lax.cond(
        is_first,
        lambda: (zero_half, zero_terms),
        lambda: attend_backward(
            second_query,
            key_all,
            value_all,
            second_out,
            second_lse,
            grad_second,
            mask_second,
            scale,
        ),
    )
    returned = passed_along(dq_two, "section", -1)
    grad_outgoing = lax.dynamic_slice_in_dim(returned, (1 - parity) * columns, columns, 1)
    grad_received = swapped(grad_outgoing, "tensor", 0)
    grad_kept = lax.dynamic_slice_in_dim(returned, parity * columns, columns, 1)
    grad_first = jnp.where(
        parity == 0,
        jnp.concatenate([grad_kept, grad_received], axis=0),
        jnp.concatenate([grad_received, grad_kept], axis=0),
    )

    def first_backward():
        dquery, terms = attend_backward(
            local[0], key_first, value_first, first_out, first_lse, grad_first, mask_first, scale
        )
        blank = jnp.zeros_like(terms)
        padded = jnp.where(
            parity == 0,
            jnp.concatenate([terms, blank], axis=2),
            jnp.concatenate([blank, terms], axis=2),
        )
        return (dquery, padded)

    dq_one, terms_one = lax.cond(is_first, first_backward, lambda: (zero_out, zero_terms))
    total = return_to_owners(jnp.where(is_first, terms_one, terms_two), rows)
    owned_first = lax.dynamic_slice_in_dim(total, parity * columns, columns, 2).astype(jnp.bfloat16)
    sums_outgoing = lax.dynamic_slice_in_dim(total, (1 - parity) * half_rows, half_rows, 1)
    sums_received = swapped(
        jnp.where(is_first, jnp.zeros_like(sums_outgoing), sums_outgoing).astype(jnp.bfloat16),
        "tensor",
        0,
    ).astype(jnp.float32)
    sums_kept = lax.dynamic_slice_in_dim(total, parity * half_rows, half_rows, 1)
    owned_second = (sums_kept + sums_received).astype(jnp.bfloat16).reshape(2, rows, columns)
    result_first = jnp.concatenate([dq_one[None], owned_first])
    result_second = jnp.concatenate([dq_two.reshape(1, rows, columns), owned_second])
    return jnp.where(is_first, result_first, result_second)[None]


def solution(mesh):
    in_specs = (P("section", None, "dp", "tensor"), P("dp", "tensor"))
    out_specs = P("section", None, "dp", "tensor")
    return jax.shard_map(body, mesh=mesh, in_specs=in_specs, out_specs=out_specs, check_vma=False)
```

profile of v0, /device:TPU:108, one launch (start us, length us, event | category | flops | bytes accessed | tf_op | source)
XLA Modules:
  0.0 792.3 jit_solution(13962193862108735151)
XLA Ops:
  0.0 2.1 slice_bitcast_fusion
  3.3 2.4 collective-permute-start
  5.7 20.4 %collective-permute-done = bf16[2,128,1536]{2,1,0:T(8,128)(2,1)S(1)} collective-permute-done((bf16[2,128,1536]{2,1,0:T(8,128)(2,1)}, bf16[2,128,1536]{2,1,0:T(8,128)(2,1)S(1)}, u32[]{:S(2)}, u32[]{:S(2)}) %collective-permute-start) | collective-permute-done | bytes 786464 | tf_op jit(solution)/shard_map/ppermute | solution.py:20
  27.3 4.1 fusion.84
  31.4 7.7 collective-permute-start.3
  39.1 6.4 collective-permute-start.2
  45.5 2.9 collective-permute-start.1
  48.5 1.5 copy.71
  52.2 102.6 %collective-permute-done.3 = bf16[2,256,1536]{2,1,0:T(8,128)(2,1)} collective-permute-done((bf16[2,256,1536]{2,1,0:T(8,128)(2,1)}, bf16[2,256,1536]{2,1,0:T(8,128)(2,1)}, u32[]{:S(2)}, u32[]{:S(2)}) %collective-permute-start.3) | collective-permute-done | bytes 1572896 | tf_op jit(solution)/shard_map/ppermute | solution.py:14
  154.7 54.7 %collective-permute-done.2 = bf16[2,256,1536]{2,1,0:T(8,128)(2,1)} collective-permute-done((bf16[2,256,1536]{2,1,0:T(8,128)(2,1)}, bf16[2,256,1536]{2,1,0:T(8,128)(2,1)}, u32[]{:S(2)}, u32[]{:S(2)}) %collective-permute-start.2) | collective-permute-done | bytes 1572896 | tf_op jit(solution)/shard_map/ppermute | solution.py:14
  209.4 31.7 %collective-permute-done.1 = bf16[2,256,1536]{2,1,0:T(8,128)(2,1)} collective-permute-done((bf16[2,256,1536]{2,1,0:T(8,128)(2,1)}, bf16[2,256,1536]{2,1,0:T(8,128)(2,1)}, u32[]{:S(2)}, u32[]{:S(2)}) %collective-permute-start.1) | collective-permute-done | bytes 1572896 | tf_op jit(solution)/shard_map/ppermute | solution.py:14
  241.2 3.3 pad_maximum_fusion.2
  244.9 2.0 constant_dynamic-slice_fusion.9
  247.5 2.6 copy.126
  250.1 2.6 copy.125
  252.7 29.9 %conditional.4 = (bf16[256,768]{0,1:T(8,128)(2,1)}, f32[6,256,1]{1,2,0:T(1,128)}, bf16[256,768]{1,0:T(8,128)(2,1)}) conditional(s32[]{:T(128)} %convert_element_type.102, () %tuple.58, (bf16[3,256,768]{1,2,0:T(8,128)(2,1)}, bf16[1024,768]{0,1:T(8,128)(2,1)}, bf16[1024,768]{0,1:T(8,128)(2,1)}, pred[256,1024]{1,0:T(32,128)(4,1)S(1)}) %tuple.170), branch_computations={%region_0.1_spmd, %region_1.6_spmd} | conditional | flops 136085248 | bytes 5908681 | solution.py:134
  252.7 1.8 slice.24
  254.5 26.2 %while.48 = (s32[]{:T(128)}, bf16[6,256,128]{1,2,0:T(8,128)(2,1)}, f32[6,256,1]{1,2,0:T(1,128)}, bf16[6,256,128]{1,2,0:T(8,128)(2,1)}, bf16[6,1024,128]{1,2,0:T(...) while((s32[]{:T(128)}, bf16[6,256,128]{1,2,0:T(8,128)(2,1)}, ...), condition=%wide.region_5.5_spmd, body=%wide.region_2.4_spmd.sunk | while | flops 136085248 | bytes 4335721 | solution.py:64
  258.9 1.4 fusion.178
  276.4 1.4 fusion.178
  280.7 1.9 copy.87
  283.7 2.4 collective-permute-start.4
  286.1 6.6 collective-permute-done.4
  293.6 2.0 collective-permute-start.5
  295.7 1.9 slice_convert_fusion
  297.6 2.3 reshape.296
  300.7 2.1 add_convert_fusion.1
  303.6 3.1 conditional.6
  303.7 3.0 broadcast_in_dim.66.clone
  308.0 237.6 %collective-permute-done.6 = bf16[128,1536]{0,1:T(8,128)(2,1)S(1)} collective-permute-done((bf16[128,1536]{0,1:T(8,128)(2,1)S(1)}, bf16[128,1536]{0,1:T(8,128)(2,1)S(1)}, u32[]{:S(2)}, u32[]{:S(2)}) %collective-permute-start.6) | collective-permute-done | bytes 393248 | tf_op jit(solution)/shard_map/ppermute | solution.py:14
  545.7 2.4 collective-permute-start.7
  548.1 7.9 collective-permute-done.7
  556.1 66.1 %conditional.7 = (bf16[1,1,256,768]{3,2,1,0:T(8,128)(2,1)}, bf16[2,1024,1536]{2,1,0:T(8,128)(2,1)}) conditional(s32[]{:T(128)} %convert_element_type.102, () %tuple.57, (s32[]{:T(128)}, bf16[3,256,768]{1,2,0:T(8,128)(2,1)}, bf16[1024,768]{0,1:T(8,128)(2,1)}, bf16[1024,768]{0,1:T(8,128)(2,1)}, bf16[256,768]{0,1:T(8,128)(2,1)}, ...), branch_computations={%region_17.18_spmd, %region_18.22_spmd} | conditional | flops 342884096 | bytes 42277180 | solution.py:197
  557.2 46.9 %while.51 = (s32[]{:T(128)}, bf16[6,256,128]{1,2,0:T(8,128)(2,1)S(1)}, bf16[6,1024,128]{1,2,0:T(8,128)(2,1)}, bf16[6,1024,128]{1,2,0:T(8,128)(2,1)}, bf16[6,256,...) while((s32[]{:T(128)}, ...), condition=%wide.region_21.21_spmd, body=%wide.region_19.20_spmd.sunk | while | flops 337968896 | bytes 9640093 | solution.py:98
  604.8 2.2 pad_maximum_fusion.1
  607.0 1.9 copy.91
  608.9 4.6 pad_select_fusion
  613.6 8.6 %copy.93 = bf16[2,1024,1536]{2,1,0:T(8,128)(2,1)} copy(bf16[2,1024,1536]{1,2,0:T(8,128)(2,1)} %pad_select_fusion) | data formatting | bytes 12582912 | tf_op jit(solution)/shard_map/cond | solution.py:197
  622.2 3.4 broadcast_select_fusion.1
  626.2 1.9 collective-permute-start.8
  628.1 1.9 collective-permute-start.10
  630.1 1.9 collective-permute-start.9
  632.0 54.6 %collective-permute-done.8 = bf16[2,256,1536]{2,1,0:T(8,128)(2,1)S(1)} collective-permute-done((bf16[2,256,1536]{2,1,0:T(8,128)(2,1)S(1)}, bf16[2,256,1536]{2,1,0:T(8,128)(2,1)S(1)}, u32[]{:S(2)}, u32[]{:S(2)}) %collective-permute-start.8) | collective-permute-done | bytes 1572896 | tf_op jit(solution)/shard_map/ppermute | solution.py:14
  686.6 27.3 %collective-permute-done.10 = bf16[2,256,1536]{2,1,0:T(8,128)(2,1)S(1)} collective-permute-done((bf16[2,256,1536]{2,1,0:T(8,128)(2,1)S(1)}, bf16[2,256,1536]{2,1,0:T(8,128)(2,1)S(1)}, u32[]{:S(2)}, u32[]{:S(2)}) %collective-permute-start.10) | collective-permute-done | bytes 1572896 | tf_op jit(solution)/shard_map/ppermute | solution.py:14
  713.9 59.4 %collective-permute-done.9 = bf16[2,256,1536]{2,1,0:T(8,128)(2,1)S(1)} collective-permute-done((bf16[2,256,1536]{2,1,0:T(8,128)(2,1)S(1)}, bf16[2,256,1536]{2,1,0:T(8,128)(2,1)S(1)}, u32[]{:S(2)}, u32[]{:S(2)}) %collective-permute-start.9) | collective-permute-done | bytes 1572896 | tf_op jit(solution)/shard_map/ppermute | solution.py:14
  774.1 2.5 collective-permute-start.11
  776.8 12.9 %collective-permute-done.11 = bf16[2,128,1536]{2,1,0:T(8,128)(2,1)S(1)} collective-permute-done((bf16[2,128,1536]{2,1,0:T(8,128)(2,1)S(1)}, bf16[2,128,1536]{2,1,0:T(8,128)(2,1)S(1)}, u32[]{:S(2)}, u32[]{:S(2)}) %collective-permute-start.11) | collective-permute-done | bytes 786464 | tf_op jit(solution)/shard_map/ppermute | solution.py:20
  790.1 2.2 maximum_select_fusion.4
  (190 shorter events, 84.7 us)
Async XLA Ops:
  3.3 22.9 %collective-permute-start = (bf16[2,128,1536]{2,1,0:T(8,128)(2,1)}, bf16[2,128,1536]{2,1,0:T(8,128)(2,1)S(1)}, u32[]{:S(2)}, u32[]{:S(2)}) collective-permute-start(bf16[2,128,1536]{2,1,0:T(8,128)(2,1)} %reshape.292), channel_id=1, source_target_pairs={{0,1},{1,0},{2,3},{3,2},{4,5},{5,4},{6,7},{7,6},{8,9},{9,8},{10,11... | collective-permute-start | bytes 2359304 | tf_op jit(solution)/shard_map/ppermute | solution.py:20
  5.7 42.8 %copy-start.2 = (bf16[1,3,256,768]{3,2,1,0:T(8,128)(2,1)S(1)}, bf16[1,3,256,768]{3,2,1,0:T(8,128)(2,1)}, u32[]{:S(2)}) copy-start(bf16[1,3,256,768]{3,2,1,0:T(8,128)(2,1)} %param.18) | copy-start | bytes 3538948
  31.4 123.3 %collective-permute-start.3 = (bf16[2,256,1536]{2,1,0:T(8,128)(2,1)}, bf16[2,256,1536]{2,1,0:T(8,128)(2,1)}, u32[]{:S(2)}, u32[]{:S(2)}) collective-permute-start(bf16[2,256,1536]{2,1,0:T(8,128)(2,1)} %fusion.84), channel_id=1, source_target_pairs={{0,24},{8,32},{16,40},{24,48},{32,56},{40,64},{48,72},{56,80},{64,... | collective-permute-start | bytes 4718600 | tf_op jit(solution)/shard_map/ppermute | solution.py:14
  39.1 170.3 %collective-permute-start.2 = (bf16[2,256,1536]{2,1,0:T(8,128)(2,1)}, bf16[2,256,1536]{2,1,0:T(8,128)(2,1)}, u32[]{:S(2)}, u32[]{:S(2)}) collective-permute-start(bf16[2,256,1536]{2,1,0:T(8,128)(2,1)} %fusion.84), channel_id=1, source_target_pairs={{0,16},{8,24},{16,32},{24,40},{32,48},{40,56},{48,64},{56,72},{64,... | collective-permute-start | bytes 4718600 | tf_op jit(solution)/shard_map/ppermute | solution.py:14
  45.5 195.6 %collective-permute-start.1 = (bf16[2,256,1536]{2,1,0:T(8,128)(2,1)}, bf16[2,256,1536]{2,1,0:T(8,128)(2,1)}, u32[]{:S(2)}, u32[]{:S(2)}) collective-permute-start(bf16[2,256,1536]{2,1,0:T(8,128)(2,1)} %fusion.84), channel_id=1, source_target_pairs={{0,8},{8,16},{16,24},{24,32},{32,40},{40,48},{48,56},{56,64},{64,7... | collective-permute-start | bytes 4718600 | tf_op jit(solution)/shard_map/ppermute | solution.py:14
  50.3 0.5 copy-start.9
  50.3 0.6 copy-start.10
  50.3 0.6 copy-start.7
  244.9 2.6 copy-start
  282.6 17.2 %copy-start.8 = (s32[1024]{0:T(1024)S(1)}, s32[1024]{0:T(1024)}, u32[]{:S(2)}) copy-start(s32[1024]{0:T(1024)} %copy-done.7) | copy-start | bytes 12292
  283.7 9.1 %collective-permute-start.4 = (bf16[128,768]{1,0:T(8,128)(2,1)S(1)}, bf16[128,768]{1,0:T(8,128)(2,1)S(1)}, u32[]{:S(2)}, u32[]{:S(2)}) collective-permute-start(bf16[128,768]{1,0:T(8,128)(2,1)S(1)} %get-tuple-element.479), channel_id=1, source_target_pairs={{0,1},{1,0},{2,3},{3,2},{4,5},{5,4},{6,7},{7,6},{8,9},{9,8},{10,11... | collective-permute-start | bytes 589832 | tf_op jit(solution)/shard_map/ppermute | solution.py:20
  293.6 7.1 collective-permute-start.5
  306.7 249.3 %copy-start.4 = (bf16[1,1,256,768]{3,2,1,0:T(8,128)(2,1)}, bf16[1,1,256,768]{3,2,1,0:T(8,128)(2,1)S(1)}, u32[]{:S(2)}) copy-start(bf16[1,1,256,768]{3,2,1,0:T(8,128)(2,1)S(1)} %get-tuple-element.295) | copy-start | bytes 1179652
  306.7 238.9 %collective-permute-start.6 = (bf16[128,1536]{0,1:T(8,128)(2,1)S(1)}, bf16[128,1536]{0,1:T(8,128)(2,1)S(1)}, u32[]{:S(2)}, u32[]{:S(2)}) collective-permute-start(bf16[128,1536]{0,1:T(8,128)(2,1)S(1)} %get-tuple-element.290), channel_id=1, source_target_pairs={{256,0},{257,1},{258,2},{259,3},{260,4},{261,5},{262,6},{263,7},{2... | collective-permute-start | bytes 1179656 | tf_op jit(solution)/shard_map/ppermute | solution.py:14
  545.7 10.3 %collective-permute-start.7 = (bf16[128,768]{0,1:T(8,128)(2,1)S(1)}, bf16[128,768]{0,1:T(8,128)(2,1)S(1)}, u32[]{:S(2)}, u32[]{:S(2)}) collective-permute-start(bf16[128,768]{0,1:T(8,128)(2,1)S(1)} %get-tuple-element.477), channel_id=1, source_target_pairs={{0,1},{1,0},{2,3},{3,2},{4,5},{5,4},{6,7},{7,6},{8,9},{9,8},{10,11... | collective-permute-start | bytes 589832 | tf_op jit(solution)/shard_map/ppermute | solution.py:20
  604.1 0.7 copy-start.6
  626.2 60.4 %collective-permute-start.8 = (bf16[2,256,1536]{2,1,0:T(8,128)(2,1)S(1)}, bf16[2,256,1536]{2,1,0:T(8,128)(2,1)S(1)}, u32[]{:S(2)}, u32[]{:S(2)}) collective-permute-start(bf16[2,256,1536]{2,1,0:T(8,128)(2,1)S(1)} %get-tuple-element.467), channel_id=1, source_target_pairs={{8,0},{16,8},{24,16},{32,24},{40,32},{48,40},{56,48},{64,56},{72,6... | collective-permute-start | bytes 4718600 | tf_op jit(solution)/shard_map/ppermute | solution.py:14
  628.1 85.7 %collective-permute-start.10 = (bf16[2,256,1536]{2,1,0:T(8,128)(2,1)S(1)}, bf16[2,256,1536]{2,1,0:T(8,128)(2,1)S(1)}, u32[]{:S(2)}, u32[]{:S(2)}) collective-permute-start(bf16[2,256,1536]{2,1,0:T(8,128)(2,1)S(1)} %get-tuple-element.468), channel_id=1, source_target_pairs={{24,0},{32,8},{40,16},{48,24},{56,32},{64,40},{72,48},{80,56},{88,... | collective-permute-start | bytes 4718600 | tf_op jit(solution)/shard_map/ppermute | solution.py:14
  630.1 143.2 %collective-permute-start.9 = (bf16[2,256,1536]{2,1,0:T(8,128)(2,1)S(1)}, bf16[2,256,1536]{2,1,0:T(8,128)(2,1)S(1)}, u32[]{:S(2)}, u32[]{:S(2)}) collective-permute-start(bf16[2,256,1536]{2,1,0:T(8,128)(2,1)S(1)} %get-tuple-element.469), channel_id=1, source_target_pairs={{16,0},{24,8},{32,16},{40,24},{48,32},{56,40},{64,48},{72,56},{80,... | collective-permute-start | bytes 4718600 | tf_op jit(solution)/shard_map/ppermute | solution.py:14
  774.1 16.0 %copy-start.5 = (bf16[1,1,256,768]{3,2,1,0:T(8,128)(2,1)S(1)}, bf16[1,1,256,768]{3,2,1,0:T(8,128)(2,1)}, u32[]{:S(2)}) copy-start(bf16[1,1,256,768]{3,2,1,0:T(8,128)(2,1)} %copy-done.4) | copy-start | bytes 1179652
  774.1 15.5 %collective-permute-start.11 = (bf16[2,128,1536]{2,1,0:T(8,128)(2,1)S(1)}, bf16[2,128,1536]{2,1,0:T(8,128)(2,1)S(1)}, u32[]{:S(2)}, u32[]{:S(2)}) collective-permute-start(bf16[2,128,1536]{2,1,0:T(8,128)(2,1)S(1)} %select_convert_fusion), channel_id=1, source_target_pairs={{0,1},{1,0},{2,3},{3,2},{4,5},{5,4},{6,7},{7,6},{8,9},{9,8},{10,11... | collective-permute-start | bytes 2359304 | tf_op jit(solution)/shard_map/ppermute | solution.py:20
where the time goes:
time: 800 us; the launch traced here: 792 us
  waiting for transfers between devices  616 us (77%)
  local copies, waits for them, and re-layouts  65.3 us (8%)
  matrix products  44 us (6%)
  starting transfers between devices  35.9 us (4%)
  other arithmetic  30.3 us (4%)
    ppermute x8, waiting for transfers between devices, passed_along(): return lax.ppermute(shard, axis, pairs)  568 us
    ppermute x4, waiting for transfers between devices, swapped(): return lax.ppermute(value, axis, pairs)  47.9 us
    ppermute x8, starting transfers between devices, passed_along(): return lax.ppermute(shard, axis, pairs)  26.1 us
    dot_general x12, matrix products, single(): jnp.dot(q_head, k_head.T, preferred_element_type=jnp.float32) * scale  16.7 us
  transfers between devices with their start and end apart: 12, of which 11 were waited for; matrix products, arithmetic and copies ran while one was open for 1% of the time, Pallas kernels for 0%

commit v1 on v0

v1 whole, which is shorter than its diff:
```python
import math

import jax
import jax.numpy as jnp
from jax import lax
from jax.experimental import pallas as pl
from jax.experimental.pallas import tpu as pltpu
from jax.sharding import PartitionSpec as P

HD = 128
BLK = 256
LEN = 1024
SCALE = 1.0 / math.sqrt(HD)
SCALE2 = SCALE * math.log2(math.e)
AXES = ("section", "dp", "tensor")
BF = jnp.bfloat16
F32 = jnp.float32
VM = pl.BlockSpec(memory_space=pltpu.VMEM)
SM = pl.BlockSpec(memory_space=pltpu.SMEM)


def first_head(z):
    return jnp.where(z > 0, z + 1, 0)


def second_head(z):
    return jnp.where(z == 3, 5, 1)


def is_edge(z):
    return (z == 0) | (z == 3)


def head_cols(head):
    return pl.ds(pl.multiple_of(head * HD, HD), HD)


def rows_of(index, size):
    return pl.ds(pl.multiple_of(index * size, size), size)


def dot(a, b):
    return jnp.dot(a, b, preferred_element_type=F32)


def flip(x):
    return x.astype(F32).T.astype(BF)


def call(kernel, outs, args, scratch=(), flops=0):
    return pl.pallas_call(
        kernel,
        out_shape=[jax.ShapeDtypeStruct(s, d) for s, d in outs],
        in_specs=[SM] + [VM] * (len(args) - 1),
        out_specs=[VM] * len(outs),
        scratch_shapes=list(scratch),
        compiler_params=pltpu.CompilerParams(vmem_limit_bytes=48 * 1024 * 1024),
        cost_estimate=pl.CostEstimate(flops=flops, bytes_accessed=4000000, transcendentals=0),
    )(*args)


def pick_kernel(info, local, grad, *outs):
    z, h = info[0], info[1]
    for k in range(4):
        other = z ^ k
        outs[k][...] = local[:, :, head_cols(first_head(other))]
        outs[4 + k][...] = local[:, :, head_cols(second_head(other))]
    own, away = outs[8], outs[9]
    row = lax.broadcasted_iota(jnp.int32, (128, 256), 0)
    col = lax.broadcasted_iota(jnp.int32, (128, 256), 1)
    for out, a in ((own, h), (away, 1 - h)):
        take = jnp.where(col == 2 * row + a, 1.0, 0.0).astype(BF)
        for j in range(4):
            rows = grad[...] if j == 3 else local[j]
            out[j] = dot(take, rows).astype(BF)


def pick_second_kernel(info, own, came, *outs):
    z, h = info[0], info[1]
    mine, theirs = rows_of(h, 128), rows_of(1 - h, 128)
    for k in range(4):
        for slot, head in ((0, first_head(z ^ k)), (4, second_head(z ^ k))):
            outs[slot + k][:, mine, :] = own[:, :, head_cols(head)]
            outs[slot + k][:, theirs, :] = came[:, :, head_cols(head)]


def assemble(info, slot_a, slot_b, dst):
    z, s = info[0], info[2]

    @pl.when(s == 0)
    def _():
        for k in range(4):
            dst[:, rows_of(z ^ k, BLK), :] = slot_a[k][...]

    @pl.when(s == 1)
    def _():
        for k in range(4):
            dst[:, rows_of(z ^ k, BLK), :] = slot_b[k][...]


def score_block(keys, qt, i):
    n = (i + 1) * BLK
    st = dot(keys[0:n], qt[:, i * BLK : n]) * SCALE2
    key = lax.broadcasted_iota(jnp.int32, (BLK, BLK), 0)
    qry = lax.broadcasted_iota(jnp.int32, (BLK, BLK), 1)
    tail = jnp.where(key <= qry, st[n - BLK :], -jnp.inf)
    return tail if i == 0 else jnp.concatenate([st[: n - BLK], tail], axis=0)


def forward_kernel(info, *refs):
    slot_a, slot_b = refs[0:4], refs[4:8]
    qkv, ot, lse = refs[8:11]
    qt, vt = refs[11:]
    assemble(info, slot_a, slot_b, qkv)
    qt[...] = flip(qkv[0])
    vt[...] = flip(qkv[2])
    keys = qkv.at[1]
    for i in range(4):
        n = (i + 1) * BLK
        cols = slice(i * BLK, n)
        st = score_block(keys, qt, i)
        top = jnp.max(st, axis=0, keepdims=True)
        p = jnp.exp2(st - top)
        total = jnp.sum(p, axis=0, keepdims=True)
        ot[:, cols] = (dot(vt[:, 0:n], p.astype(BF)) / total).astype(BF)
        lse[:, cols] = jnp.broadcast_to(top + jnp.log2(total), (8, BLK))


def backward_block(i, p, keys_t, values, q, g, gt, delta, dqt, dk, dv):
    n = (i + 1) * BLK
    cols = slice(i * BLK, n)
    dp = dot(values[0:n], gt[:, cols])
    ds = (p * (dp - delta)).astype(BF)
    dqt[:, cols] = (dot(keys_t[:, 0:n], ds) * SCALE).astype(BF)
    add_k = dot(ds, q[cols])
    add_v = dot(p.astype(BF), g[cols])
    if i > 0:
        dk[0 : n - BLK] += add_k[: n - BLK]
        dv[0 : n - BLK] += add_v[: n - BLK]
    dk[n - BLK : n] = add_k[n - BLK :]
    dv[n - BLK : n] = add_v[n - BLK :]


def hand_out(info, outs, dq, dk, dv):
    z = info[0]
    for k in range(4):
        rows = rows_of(z ^ k, BLK)
        outs[k][0] = dq[rows]
        outs[k][1] = (dk[rows] * SCALE).astype(BF)
        outs[k][2] = dv[rows].astype(BF)


def second_kernel(info, *refs):
    slot_a, slot_b, ot1 = refs[0:4], refs[4:8], refs[8]
    outs, g1t = refs[9:13], refs[13]
    qkvg, qt, kt, vt, gt, dq, dk, dv = refs[14:]
    assemble(info, slot_a, slot_b, qkvg)
    q = qkvg[0].astype(F32) + ot1[...].astype(F32).T
    qkvg[0] = q.astype(BF)
    qt[...] = q.T.astype(BF)
    kt[...] = flip(qkvg[1])
    vt[...] = flip(qkvg[2])
    gt[...] = flip(qkvg[3])
    keys, values = qkvg.at[1], qkvg.at[2]
    for i in range(4):
        n = (i + 1) * BLK
        cols = slice(i * BLK, n)
        st = score_block(keys, qt, i)
        top = jnp.max(st, axis=0, keepdims=True)
        p = jnp.exp2(st - top)
        p = p * (1.0 / jnp.sum(p, axis=0, keepdims=True))
        o = dot(vt[:, 0:n], p.astype(BF)).astype(BF)
        delta = jnp.sum(gt[:, cols].astype(F32) * o.astype(F32), axis=0, keepdims=True)
        backward_block(i, p, kt, values, qkvg.at[0], qkvg.at[3], gt, delta, g1t, dk, dv)
    dq[...] = flip(g1t[...])
    hand_out(info, outs, dq, dk, dv)


def first_backward_kernel(info, *refs):
    qkv, ot, lse, gt = refs[0:4]
    outs = refs[4:8]
    g, qt, kt, dqt, dq, dk, dv = refs[8:]
    qt[...] = flip(qkv[0])
    kt[...] = flip(qkv[1])
    g[...] = flip(gt[...])
    keys, values = qkv.at[1], qkv.at[2]
    for i in range(4):
        cols = slice(i * BLK, (i + 1) * BLK)
        st = score_block(keys, qt, i)
        p = jnp.exp2(st - lse[0:1, cols])
        delta = jnp.sum(gt[:, cols].astype(F32) * ot[:, cols].astype(F32), axis=0, keepdims=True)
        backward_block(i, p, kt, values, qkv.at[0], g, gt, delta, dqt, dk, dv)
    dq[...] = flip(dqt[...])
    hand_out(info, outs, dq, dk, dv)


def place_heads(info, slot_a, slot_b, dst):
    z = info[0]
    for k in range(4):
        dst[:, :, head_cols(first_head(z ^ k))] = slot_a[k][...]

        @pl.when(is_edge(z ^ k))
        def _(k=k):
            dst[:, :, head_cols(second_head(z ^ k))] = slot_b[k][...]


def join_second_kernel(info, *refs):
    slot_a, slot_b = refs[0:4], refs[4:8]
    keep, away = refs[8:10]
    (full,) = refs[10:]
    h = info[1]
    place_heads(info, slot_a, slot_b, full)
    keep[...] = full[:, rows_of(h, 128), :]
    away[...] = full[:, rows_of(1 - h, 128), :]


def finish_kernel(info, *refs):
    slot_a, slot_b, keep, came = refs[0:4], refs[4:8], refs[8], refs[9]
    out = refs[10]
    h, s = info[1], info[2]

    @pl.when(s == 0)
    def _():
        place_heads(info, slot_a, slot_b, out)

    @pl.when(s == 1)
    def _():
        row = lax.broadcasted_iota(jnp.int32, (256, 128), 0)
        col = lax.broadcasted_iota(jnp.int32, (256, 128), 1)
        put_own = jnp.where(row == 2 * col + h, 1.0, 0.0).astype(BF)
        put_came = jnp.where(row == 2 * col + 1 - h, 1.0, 0.0).astype(BF)
        for j in range(3):
            out[j] = (dot(put_own, keep[j]) + dot(put_came, came[j])).astype(BF)


def build(n_dp, n_tensor):
    def index(s, d, t):
        return (s * n_dp + d) * n_tensor + t

    def everywhere(rule):
        pairs = []
        for d in range(n_dp):
            for t in range(n_tensor):
                pairs += rule(d, t)
        return pairs

    def send(value, pairs):
        return lax.ppermute(value, AXES, pairs)

    def inward(src, slot, k):
        return everywhere(
            lambda d, t: [(index(src, d, t), index(slot, d ^ k, t))]
            if slot == 0 or (d ^ k) % 4 in (0, 3)
            else []
        )

    def outward(dst, slot, k):
        return [(b, a) for a, b in inward(dst, slot, k)]

    def cross():
        return everywhere(lambda d, t: [(index(1, d, t), index(1, d, t ^ 1))])

    def body(projections, out_grad):
        s = lax.axis_index("section")
        z = lax.axis_index("dp") % 4
        h = lax.axis_index("tensor") % 2
        info = jnp.stack([z, h, s]).astype(jnp.int32)
        local = projections[0]
        rows, cols = local.shape[1:]
        chunk3 = ((3, BLK, HD), BF)
        chunk4 = ((4, BLK, HD), BF)
        half4 = ((4, rows // 2, cols), BF)
        half3 = ((3, rows // 2, cols), BF)
        vm = pltpu.VMEM
        tall, wide = vm((LEN, HD), BF), vm((HD, LEN), BF)
        acc = vm((LEN, HD), F32)

        picked = call(pick_kernel, [chunk3] * 8 + [half4] * 2, [info, local, out_grad])
        own, away = picked[8], picked[9]
        came = send(away, cross())
        first_a = {k: send(picked[k], inward(0, 0, k)) for k in (3, 2, 1)}
        first_b = {k: send(picked[4 + k], inward(0, 1, k)) for k in (3, 2, 1, 0)}
        first_a[0] = picked[0]

        picked2 = call(pick_second_kernel, [chunk4] * 8, [info, own, came])
        second_a = {k: send(picked2[k], inward(1, 0, k)) for k in (3, 2, 1, 0)}
        second_b = {k: send(picked2[4 + k], inward(1, 1, k)) for k in (3, 2, 1)}
        second_b[0] = picked2[4]

        def four(x):
            return [x[k] for k in range(4)]

        qkv, ot, lse = call(
            forward_kernel,
            [((3, LEN, HD), BF), ((HD, LEN), BF), ((8, LEN), F32)],
            [info] + four(first_a) + four(first_b),
            [wide, wide],
        )
        got = call(
            second_kernel,
            [chunk3] * 4 + [((HD, LEN), BF)],
            [info] + four(second_a) + four(second_b) + [ot],
            [vm((4, LEN, HD), BF)] + [wide] * 4 + [tall, acc, acc],
        )
        g1t = got[4]
        back_a = {k: send(got[k], outward(1, 0, k)) for k in (3, 2, 1, 0)}
        back_b = {k: send(got[k], outward(1, 1, k)) for k in (3, 2, 1)}
        back_b[0] = got[0]
        first = call(
            first_backward_kernel,
            [chunk3] * 4,
            [info, qkv, ot, lse, g1t],
            [tall, wide, wide, wide, tall, acc, acc],
        )
        keep, give = call(
            join_second_kernel,
            [half3] * 2,
            [info] + four(back_a) + four(back_b),
            [vm((3, rows, cols), BF)],
        )
        returned = send(give, cross())
        home_a = {k: send(first[k], outward(0, 0, k)) for k in (3, 2, 1)}
        home_b = {k: send(first[k], outward(0, 1, k)) for k in (3, 2, 1, 0)}
        home_a[0] = first[0]
        (out,) = call(
            finish_kernel,
            [((3, rows, cols), BF)],
            [info] + four(home_a) + four(home_b) + [keep, returned],
        )
        return out[None]

    return body


def solution(mesh):
    body = build(mesh.shape["dp"], mesh.shape["tensor"])
    in_specs = (P("section", None, "dp", "tensor"), P("dp", "tensor"))
    out_specs = P("section", None, "dp", "tensor")
    return jax.shard_map(body, mesh=mesh, in_specs=in_specs, out_specs=out_specs, check_vma=False)
```

time: 800 us -> 109 us (0.14)
  the two profiles are of different devices: /device:TPU:108 before, /device:TPU:32 now
where the time goes in v1:
time: 109 us; the launch traced here: 108 us
  starting transfers between devices  55.1 us (51%)
  waiting for transfers between devices  35.1 us (32%)
  Pallas kernels  15.2 us (14%)
  local copies, waits for them, and re-layouts  2.27 us (2%)
    ppermute x30, starting transfers between devices, send(): return lax.ppermute(value, AXES, pairs)  55.1 us
    ppermute x30, waiting for transfers between devices, send(): return lax.ppermute(value, AXES, pairs)  35.1 us
    pallas_call x7, Pallas kernels, call(): pl.pallas_call(kernel, out_shape=[jax.ShapeDtypeStruct(s, d) for s, d in...  15.2 us
    unnamed x4, local copies, waits for them, and re-layouts  2.27 us
  transfers between devices with their start and end apart: 30, of which 9 were waited for; matrix products, arithmetic and copies ran while one was open for 0% of the time, Pallas kernels for 6%

profile of v1, /device:TPU:32, one launch (start us, length us, event | category | flops | bytes accessed | tf_op | source)
XLA Modules:
  0.0 108.2 jit_solution(6626165847833778844)
XLA Ops:
  0.1 1.3 %copy-done = bf16[1,3,256,768]{3,2,1,0:T(8,128)(2,1)S(1)} copy-done((bf16[1,3,256,768]{3,2,1,0:T(8,128)(2,1)S(1)}, bf16[1,3,256,768]{3,2,1,0:T(8,128)(2,1)}, u32[]{:S(2)}) %copy-start) | copy-done | bytes 1179672
  1.4 1.0 copy-done.1
  2.3 1.4 %shard_map.28 = (bf16[3,256,128]{2,1,0:T(8,128)(2,1)S(1)}, bf16[3,256,128]{2,1,0:T(8,128)(2,1)S(1)}, bf16[3,256,128]{2,1,0:T(8,128)(2,1)S(1)}, bf16[3,256,128]{2...) custom-call(s32[3]{0:T(128)S(1)} %pad_add_fusion.info, ...), custom_call_target="tpu_custom_call" | custom-call | bytes 4000000 | tf_op jit(solution)/shard_map/pallas_call | solution.py:51
  3.7 0.7 collective-permute-start.7
  4.4 7.4 %collective-permute-start = (bf16[3,256,128]{2,1,0:T(8,128)(2,1)S(1)}, bf16[3,256,128]{2,1,0:T(8,128)(2,1)S(1)}, u32[]{:S(2)}, u32[]{:S(2)}) collective-permute-start(bf16[3,256,128]{2,1,0:T(8,128)(2,1)S(1)} %get-tuple-element.38), channel_id=1, source_target_pairs={{0,8},{1,9},{2,10},{3,11},{4,12},{5,13},{6,14},{7,15},{8,0},{9,1},... | collective-permute-start | bytes 589832 | tf_op jit(solution)/shard_map/ppermute | solution.py:248
  11.9 1.9 %collective-permute-start.1 = (bf16[3,256,128]{2,1,0:T(8,128)(2,1)S(1)}, bf16[3,256,128]{2,1,0:T(8,128)(2,1)S(1)}, u32[]{:S(2)}, u32[]{:S(2)}) collective-permute-start(bf16[3,256,128]{2,1,0:T(8,128)(2,1)S(1)} %get-tuple-element.39), channel_id=1, source_target_pairs={{0,16},{1,17},{2,18},{3,19},{4,20},{5,21},{6,22},{7,23},{8,24},{9,... | collective-permute-start | bytes 589832 | tf_op jit(solution)/shard_map/ppermute | solution.py:248
  13.8 3.4 %collective-permute-start.2 = (bf16[3,256,128]{2,1,0:T(8,128)(2,1)S(1)}, bf16[3,256,128]{2,1,0:T(8,128)(2,1)S(1)}, u32[]{:S(2)}, u32[]{:S(2)}) collective-permute-start(bf16[3,256,128]{2,1,0:T(8,128)(2,1)S(1)} %get-tuple-element.40), channel_id=1, source_target_pairs={{0,24},{1,25},{2,26},{3,27},{4,28},{5,29},{6,30},{7,31},{8,16},{9,... | collective-permute-start | bytes 589832 | tf_op jit(solution)/shard_map/ppermute | solution.py:248
  17.2 0.7 collective-permute-start.3
  17.8 0.9 shard_map.30
  18.8 1.3 %collective-permute-start.8 = (bf16[4,256,128]{2,1,0:T(8,128)(2,1)S(1)}, bf16[4,256,128]{2,1,0:T(8,128)(2,1)S(1)}, u32[]{:S(2)}, u32[]{:S(2)}) collective-permute-start(bf16[4,256,128]{2,1,0:T(8,128)(2,1)S(1)} %get-tuple-element.50), channel_id=1, source_target_pairs={{256,0},{257,1},{258,2},{259,3},{260,4},{261,5},{262,6},{263,7},{2... | collective-permute-start | bytes 786440 | tf_op jit(solution)/shard_map/ppermute | solution.py:248
  20.1 1.3 %collective-permute-start.9 = (bf16[4,256,128]{2,1,0:T(8,128)(2,1)S(1)}, bf16[4,256,128]{2,1,0:T(8,128)(2,1)S(1)}, u32[]{:S(2)}, u32[]{:S(2)}) collective-permute-start(bf16[4,256,128]{2,1,0:T(8,128)(2,1)S(1)} %get-tuple-element.51), channel_id=1, source_target_pairs={{256,8},{257,9},{258,10},{259,11},{260,12},{261,13},{262,14},{263,... | collective-permute-start | bytes 786440 | tf_op jit(solution)/shard_map/ppermute | solution.py:248
  21.4 6.2 %collective-permute-start.4 = (bf16[3,256,128]{2,1,0:T(8,128)(2,1)S(1)}, bf16[3,256,128]{2,1,0:T(8,128)(2,1)S(1)}, u32[]{:S(2)}, u32[]{:S(2)}) collective-permute-start(bf16[3,256,128]{2,1,0:T(8,128)(2,1)S(1)} %get-tuple-element.42), channel_id=1, source_target_pairs={{8,256},{9,257},{10,258},{11,259},{12,260},{13,261},{14,262},{15,2... | collective-permute-start | bytes 589832 | tf_op jit(solution)/shard_map/ppermute | solution.py:248
  27.6 1.3 %collective-permute-start.5 = (bf16[3,256,128]{2,1,0:T(8,128)(2,1)S(1)}, bf16[3,256,128]{2,1,0:T(8,128)(2,1)S(1)}, u32[]{:S(2)}, u32[]{:S(2)}) collective-permute-start(bf16[3,256,128]{2,1,0:T(8,128)(2,1)S(1)} %get-tuple-element.43), channel_id=1, source_target_pairs={{8,280},{9,281},{10,282},{11,283},{12,284},{13,285},{14,286},{15,2... | collective-permute-start | bytes 589832 | tf_op jit(solution)/shard_map/ppermute | solution.py:248
  28.9 0.7 collective-permute-start.6
  29.6 1.3 %collective-permute-done.4.refs_5_ = bf16[3,256,128]{2,1,0:T(8,128)(2,1)S(1)} collective-permute-done((bf16[3,256,128]{2,1,0:T(8,128)(2,1)S(1)}, bf16[3,256,128]{2,1,0:T(8,128)(2,1)S(1)}, u32[]{:S(2)}, u32[]{:S(2)}) %collective-permute-start.4) | collective-permute-done | bytes 196640 | tf_op jit(solution)/shard_map/ppermute | solution.py:248
  30.9 1.3 %collective-permute-start.10 = (bf16[4,256,128]{2,1,0:T(8,128)(2,1)S(1)}, bf16[4,256,128]{2,1,0:T(8,128)(2,1)S(1)}, u32[]{:S(2)}, u32[]{:S(2)}) collective-permute-start(bf16[4,256,128]{2,1,0:T(8,128)(2,1)S(1)} %get-tuple-element.52), channel_id=1, source_target_pairs={{256,16},{257,17},{258,18},{259,19},{260,20},{261,21},{262,22},{26... | collective-permute-start | bytes 786440 | tf_op jit(solution)/shard_map/ppermute | solution.py:248
  32.2 2.0 %collective-permute-done.5.refs_6_ = bf16[3,256,128]{2,1,0:T(8,128)(2,1)S(1)} collective-permute-done((bf16[3,256,128]{2,1,0:T(8,128)(2,1)S(1)}, bf16[3,256,128]{2,1,0:T(8,128)(2,1)S(1)}, u32[]{:S(2)}, u32[]{:S(2)}) %collective-permute-start.5) | collective-permute-done | bytes 196640 | tf_op jit(solution)/shard_map/ppermute | solution.py:248
  34.2 1.3 %collective-permute-start.11 = (bf16[4,256,128]{2,1,0:T(8,128)(2,1)S(1)}, bf16[4,256,128]{2,1,0:T(8,128)(2,1)S(1)}, u32[]{:S(2)}, u32[]{:S(2)}) collective-permute-start(bf16[4,256,128]{2,1,0:T(8,128)(2,1)S(1)} %get-tuple-element.53), channel_id=1, source_target_pairs={{256,24},{257,25},{258,26},{259,27},{260,28},{261,29},{262,30},{26... | collective-permute-start | bytes 786440 | tf_op jit(solution)/shard_map/ppermute | solution.py:248
  35.5 0.7 collective-permute-start.12
  36.2 0.7 collective-permute-start.13
  36.9 0.7 collective-permute-start.14
  37.6 2.4 %shard_map.29 = (bf16[3,1024,128]{2,1,0:T(8,128)(2,1)S(1)}, bf16[128,1024]{1,0:T(8,128)(2,1)S(1)}, f32[8,1024]{1,0:T(8,128)S(1)}) custom-call(s32[3]{0:T(128)S(1)} %pad_add_fusion.info, bf16[3,256,128]{2,1,0:T(8,128)(2,1)S(1)} %get-tuple-element.37.refs_0_, bf16[3,256,128]{2,1,0:T(8,128)(2,1)S(1)} %collective-permute-done.refs_1_, ...), custom_call_target="tpu_custom_call" | custom-call | bytes 4000000 | tf_op jit(solution)/shard_map/pallas_call | solution.py:51
  40.0 10.3 %collective-permute-done.11.refs_3_ = bf16[4,256,128]{2,1,0:T(8,128)(2,1)S(1)} collective-permute-done((bf16[4,256,128]{2,1,0:T(8,128)(2,1)S(1)}, bf16[4,256,128]{2,1,0:T(8,128)(2,1)S(1)}, u32[]{:S(2)}, u32[]{:S(2)}) %collective-permute-start.11) | collective-permute-done | bytes 262176 | tf_op jit(solution)/shard_map/ppermute | solution.py:248
  50.3 5.1 %shard_map.31 = (bf16[3,256,128]{2,1,0:T(8,128)(2,1)S(1)}, bf16[3,256,128]{2,1,0:T(8,128)(2,1)S(1)}, bf16[3,256,128]{2,1,0:T(8,128)(2,1)S(1)}, bf16[3,256,128]{2,1,0:T(8,128)(2,1)S(1)}, bf16[128,1024]{1,0:T(8,128)(2,1)S(1)}) custom-call(s32[3]{0:T(128)S(1)} %pad_add_fusion.info, bf16[4,256,128]{2,1,0:T(8,128)(2,1)S(1)} %collective-permute-done.8.refs_0_, ...), custom_call_target="tpu_custom_call" | custom-call | bytes 4000000 | tf_op jit(solution)/shard_map/pallas_call | solution.py:51
  55.4 3.0 %collective-permute-start.22 = (bf16[3,256,128]{2,1,0:T(8,128)(2,1)S(1)}, bf16[3,256,128]{2,1,0:T(8,128)(2,1)S(1)}, u32[]{:S(2)}, u32[]{:S(2)}) collective-permute-start(bf16[3,256,128]{2,1,0:T(8,128)(2,1)S(1)} %get-tuple-element.63.refs_4_), channel_id=1, source_target_pairs={{0,256},{1,257},{2,258},{3,259},{4,260},{5,261},{6,262},{7,263},{8... | collective-permute-start | bytes 589832 | tf_op jit(solution)/shard_map/ppermute | solution.py:248
  58.4 0.7 collective-permute-start.26
  59.1 4.5 %collective-permute-start.23 = (bf16[3,256,128]{2,1,0:T(8,128)(2,1)S(1)}, bf16[3,256,128]{2,1,0:T(8,128)(2,1)S(1)}, u32[]{:S(2)}, u32[]{:S(2)}) collective-permute-start(bf16[3,256,128]{2,1,0:T(8,128)(2,1)S(1)} %get-tuple-element.64), channel_id=1, source_target_pairs={{8,256},{9,257},{10,258},{11,259},{12,260},{13,261},{14,262},{15,2... | collective-permute-start | bytes 589832 | tf_op jit(solution)/shard_map/ppermute | solution.py:248
  63.7 0.7 collective-permute-start.27
  64.3 2.2 %collective-permute-start.24 = (bf16[3,256,128]{2,1,0:T(8,128)(2,1)S(1)}, bf16[3,256,128]{2,1,0:T(8,128)(2,1)S(1)}, u32[]{:S(2)}, u32[]{:S(2)}) collective-permute-start(bf16[3,256,128]{2,1,0:T(8,128)(2,1)S(1)} %get-tuple-element.65), channel_id=1, source_target_pairs={{16,256},{17,257},{18,258},{19,259},{20,260},{21,261},{22,262},{23... | collective-permute-start | bytes 589832 | tf_op jit(solution)/shard_map/ppermute | solution.py:248
  66.5 0.7 collective-permute-start.28
  67.2 1.3 %collective-permute-start.25 = (bf16[3,256,128]{2,1,0:T(8,128)(2,1)S(1)}, bf16[3,256,128]{2,1,0:T(8,128)(2,1)S(1)}, u32[]{:S(2)}, u32[]{:S(2)}) collective-permute-start(bf16[3,256,128]{2,1,0:T(8,128)(2,1)S(1)} %get-tuple-element.66), channel_id=1, source_target_pairs={{24,256},{25,257},{26,258},{27,259},{28,260},{29,261},{30,262},{31... | collective-permute-start | bytes 589832 | tf_op jit(solution)/shard_map/ppermute | solution.py:248
  68.6 8.1 %collective-permute-done.24.refs_2_ = bf16[3,256,128]{2,1,0:T(8,128)(2,1)S(1)} collective-permute-done((bf16[3,256,128]{2,1,0:T(8,128)(2,1)S(1)}, bf16[3,256,128]{2,1,0:T(8,128)(2,1)S(1)}, u32[]{:S(2)}, u32[]{:S(2)}) %collective-permute-start.24) | collective-permute-done | bytes 196640 | tf_op jit(solution)/shard_map/ppermute | solution.py:248
  76.7 2.1 %collective-permute-done.25.refs_3_ = bf16[3,256,128]{2,1,0:T(8,128)(2,1)S(1)} collective-permute-done((bf16[3,256,128]{2,1,0:T(8,128)(2,1)S(1)}, bf16[3,256,128]{2,1,0:T(8,128)(2,1)S(1)}, u32[]{:S(2)}, u32[]{:S(2)}) %collective-permute-start.25) | collective-permute-done | bytes 196640 | tf_op jit(solution)/shard_map/ppermute | solution.py:248
  78.8 0.8 shard_map.33
  79.6 0.7 collective-permute-start.29
  80.3 2.9 %shard_map.32 = (bf16[3,256,128]{2,1,0:T(8,128)(2,1)S(1)}, bf16[3,256,128]{2,1,0:T(8,128)(2,1)S(1)}, bf16[3,256,128]{2,1,0:T(8,128)(2,1)S(1)}, bf16[3,256,128]{2,1,0:T(8,128)(2,1)S(1)}) custom-call(s32[3]{0:T(128)S(1)} %pad_add_fusion.info, bf16[3,1024,128]{2,1,0:T(8,128)(2,1)S(1)} %get-tuple-element.45.refs_0_, ...), custom_call_target="tpu_custom_call" | custom-call | bytes 4000000 | tf_op jit(solution)/shard_map/pallas_call | solution.py:51
  83.2 0.7 collective-permute-start.18
  83.9 1.3 %collective-permute-start.19 = (bf16[3,256,128]{2,1,0:T(8,128)(2,1)S(1)}, bf16[3,256,128]{2,1,0:T(8,128)(2,1)S(1)}, u32[]{:S(2)}, u32[]{:S(2)}) collective-permute-start(bf16[3,256,128]{2,1,0:T(8,128)(2,1)S(1)} %get-tuple-element.60), channel_id=1, source_target_pairs={{256,8},{257,9},{258,10},{259,11},{260,12},{261,13},{262,14},{263,... | collective-permute-start | bytes 589832 | tf_op jit(solution)/shard_map/ppermute | solution.py:248
  85.2 1.9 %collective-permute-start.15 = (bf16[3,256,128]{2,1,0:T(8,128)(2,1)S(1)}, bf16[3,256,128]{2,1,0:T(8,128)(2,1)S(1)}, u32[]{:S(2)}, u32[]{:S(2)}) collective-permute-start(bf16[3,256,128]{2,1,0:T(8,128)(2,1)S(1)} %get-tuple-element.60), channel_id=1, source_target_pairs={{8,0},{9,1},{10,2},{11,3},{12,4},{13,5},{14,6},{15,7},{0,8},{1,9},... | collective-permute-start | bytes 589832 | tf_op jit(solution)/shard_map/ppermute | solution.py:248
  87.1 1.3 %collective-permute-start.20 = (bf16[3,256,128]{2,1,0:T(8,128)(2,1)S(1)}, bf16[3,256,128]{2,1,0:T(8,128)(2,1)S(1)}, u32[]{:S(2)}, u32[]{:S(2)}) collective-permute-start(bf16[3,256,128]{2,1,0:T(8,128)(2,1)S(1)} %get-tuple-element.61), channel_id=1, source_target_pairs={{280,8},{281,9},{282,10},{283,11},{284,12},{285,13},{286,14},{287,... | collective-permute-start | bytes 589832 | tf_op jit(solution)/shard_map/ppermute | solution.py:248
  88.4 3.5 %collective-permute-start.16 = (bf16[3,256,128]{2,1,0:T(8,128)(2,1)S(1)}, bf16[3,256,128]{2,1,0:T(8,128)(2,1)S(1)}, u32[]{:S(2)}, u32[]{:S(2)}) collective-permute-start(bf16[3,256,128]{2,1,0:T(8,128)(2,1)S(1)} %get-tuple-element.61), channel_id=1, source_target_pairs={{16,0},{17,1},{18,2},{19,3},{20,4},{21,5},{22,6},{23,7},{24,8},{25... | collective-permute-start | bytes 589832 | tf_op jit(solution)/shard_map/ppermute | solution.py:248
  91.9 0.8 collective-permute-done.19.refs_5_
  92.7 0.7 collective-permute-start.21
  93.3 1.5 %collective-permute-done.15.refs_1_ = bf16[3,256,128]{2,1,0:T(8,128)(2,1)S(1)} collective-permute-done((bf16[3,256,128]{2,1,0:T(8,128)(2,1)S(1)}, bf16[3,256,128]{2,1,0:T(8,128)(2,1)S(1)}, u32[]{:S(2)}, u32[]{:S(2)}) %collective-permute-start.15) | collective-permute-done | bytes 196640 | tf_op jit(solution)/shard_map/ppermute | solution.py:248
  94.8 2.6 %collective-permute-start.17 = (bf16[3,256,128]{2,1,0:T(8,128)(2,1)S(1)}, bf16[3,256,128]{2,1,0:T(8,128)(2,1)S(1)}, u32[]{:S(2)}, u32[]{:S(2)}) collective-permute-start(bf16[3,256,128]{2,1,0:T(8,128)(2,1)S(1)} %get-tuple-element.62), channel_id=1, source_target_pairs={{24,0},{25,1},{26,2},{27,3},{28,4},{29,5},{30,6},{31,7},{16,8},{17... | collective-permute-start | bytes 589832 | tf_op jit(solution)/shard_map/ppermute | solution.py:248
  97.5 5.3 %collective-permute-done.16.refs_2_ = bf16[3,256,128]{2,1,0:T(8,128)(2,1)S(1)} collective-permute-done((bf16[3,256,128]{2,1,0:T(8,128)(2,1)S(1)}, bf16[3,256,128]{2,1,0:T(8,128)(2,1)S(1)}, u32[]{:S(2)}, u32[]{:S(2)}) %collective-permute-start.16) | collective-permute-done | bytes 196640 | tf_op jit(solution)/shard_map/ppermute | solution.py:248
  102.8 3.6 %collective-permute-done.17.refs_3_ = bf16[3,256,128]{2,1,0:T(8,128)(2,1)S(1)} collective-permute-done((bf16[3,256,128]{2,1,0:T(8,128)(2,1)S(1)}, bf16[3,256,128]{2,1,0:T(8,128)(2,1)S(1)}, u32[]{:S(2)}, u32[]{:S(2)}) %collective-permute-start.17) | collective-permute-done | bytes 196640 | tf_op jit(solution)/shard_map/ppermute | solution.py:248
  106.4 1.8 %shard_map.34 = bf16[3,256,768]{2,1,0:T(8,128)(2,1)} custom-call(s32[3]{0:T(128)S(1)} %pad_add_fusion.info, bf16[3,256,128]{2,1,0:T(8,128)(2,1)S(1)} %get-tuple-element.59.refs_0_, bf16[3,256,128]{2,1,0:T(8,128)(2,1)S(1)} %collective-permute-done.15.refs_1_, bf16[3,256,128]{2,1,0:T(8,128)(2,1)S(1)} %collective-permute-done.16.refs_2_, ...), custom_call_target="tpu_custom_call" | custom-call | bytes 4000000 | tf_op jit(solution)/shard_map/pallas_call | solution.py:51
  (24 shorter events, 0.1 us)
Async XLA Ops:
  0.1 1.3 %copy-start = (bf16[1,3,256,768]{3,2,1,0:T(8,128)(2,1)S(1)}, bf16[1,3,256,768]{3,2,1,0:T(8,128)(2,1)}, u32[]{:S(2)}) copy-start(bf16[1,3,256,768]{3,2,1,0:T(8,128)(2,1)} %param.2) | copy-start | bytes 3538948
  1.3 1.0 copy-start.1
  3.7 14.1 %collective-permute-start.7 = (bf16[4,128,768]{2,1,0:T(8,128)(2,1)S(1)}, bf16[4,128,768]{2,1,0:T(8,128)(2,1)S(1)}, u32[]{:S(2)}, u32[]{:S(2)}) collective-permute-start(bf16[4,128,768]{2,1,0:T(8,128)(2,1)S(1)} %get-tuple-element.49), channel_id=1, source_target_pairs={{256,257},{257,256},{258,259},{259,258},{260,261},{261,260},{262,2... | collective-permute-start | bytes 2359304 | tf_op jit(solution)/shard_map/ppermute | solution.py:248
  4.4 15.6 %collective-permute-start = (bf16[3,256,128]{2,1,0:T(8,128)(2,1)S(1)}, bf16[3,256,128]{2,1,0:T(8,128)(2,1)S(1)}, u32[]{:S(2)}, u32[]{:S(2)}) collective-permute-start(bf16[3,256,128]{2,1,0:T(8,128)(2,1)S(1)} %get-tuple-element.38), channel_id=1, source_target_pairs={{0,8},{1,9},{2,10},{3,11},{4,12},{5,13},{6,14},{7,15},{8,0},{9,1},... | collective-permute-start | bytes 589832 | tf_op jit(solution)/shard_map/ppermute | solution.py:248
  11.9 9.5 %collective-permute-start.1 = (bf16[3,256,128]{2,1,0:T(8,128)(2,1)S(1)}, bf16[3,256,128]{2,1,0:T(8,128)(2,1)S(1)}, u32[]{:S(2)}, u32[]{:S(2)}) collective-permute-start(bf16[3,256,128]{2,1,0:T(8,128)(2,1)S(1)} %get-tuple-element.39), channel_id=1, source_target_pairs={{0,16},{1,17},{2,18},{3,19},{4,20},{5,21},{6,22},{7,23},{8,24},{9,... | collective-permute-start | bytes 589832 | tf_op jit(solution)/shard_map/ppermute | solution.py:248
  13.8 13.8 %collective-permute-start.2 = (bf16[3,256,128]{2,1,0:T(8,128)(2,1)S(1)}, bf16[3,256,128]{2,1,0:T(8,128)(2,1)S(1)}, u32[]{:S(2)}, u32[]{:S(2)}) collective-permute-start(bf16[3,256,128]{2,1,0:T(8,128)(2,1)S(1)} %get-tuple-element.40), channel_id=1, source_target_pairs={{0,24},{1,25},{2,26},{3,27},{4,28},{5,29},{6,30},{7,31},{8,16},{9,... | collective-permute-start | bytes 589832 | tf_op jit(solution)/shard_map/ppermute | solution.py:248
  17.2 11.8 %collective-permute-start.3 = (bf16[3,256,128]{2,1,0:T(8,128)(2,1)S(1)}, bf16[3,256,128]{2,1,0:T(8,128)(2,1)S(1)}, u32[]{:S(2)}, u32[]{:S(2)}) collective-permute-start(bf16[3,256,128]{2,1,0:T(8,128)(2,1)S(1)} %get-tuple-element.41), channel_id=1, source_target_pairs={{0,256},{1,257},{2,258},{3,259},{4,260},{5,261},{6,262},{7,263},{2... | collective-permute-start | bytes 589832 | tf_op jit(solution)/shard_map/ppermute | solution.py:248
  18.8 17.4 %collective-permute-start.8 = (bf16[4,256,128]{2,1,0:T(8,128)(2,1)S(1)}, bf16[4,256,128]{2,1,0:T(8,128)(2,1)S(1)}, u32[]{:S(2)}, u32[]{:S(2)}) collective-permute-start(bf16[4,256,128]{2,1,0:T(8,128)(2,1)S(1)} %get-tuple-element.50), channel_id=1, source_target_pairs={{256,0},{257,1},{258,2},{259,3},{260,4},{261,5},{262,6},{263,7},{2... | collective-permute-start | bytes 786440 | tf_op jit(solution)/shard_map/ppermute | solution.py:248
  20.1 16.8 %collective-permute-start.9 = (bf16[4,256,128]{2,1,0:T(8,128)(2,1)S(1)}, bf16[4,256,128]{2,1,0:T(8,128)(2,1)S(1)}, u32[]{:S(2)}, u32[]{:S(2)}) collective-permute-start(bf16[4,256,128]{2,1,0:T(8,128)(2,1)S(1)} %get-tuple-element.51), channel_id=1, source_target_pairs={{256,8},{257,9},{258,10},{259,11},{260,12},{261,13},{262,14},{263,... | collective-permute-start | bytes 786440 | tf_op jit(solution)/shard_map/ppermute | solution.py:248
  21.4 9.5 %collective-permute-start.4 = (bf16[3,256,128]{2,1,0:T(8,128)(2,1)S(1)}, bf16[3,256,128]{2,1,0:T(8,128)(2,1)S(1)}, u32[]{:S(2)}, u32[]{:S(2)}) collective-permute-start(bf16[3,256,128]{2,1,0:T(8,128)(2,1)S(1)} %get-tuple-element.42), channel_id=1, source_target_pairs={{8,256},{9,257},{10,258},{11,259},{12,260},{13,261},{14,262},{15,2... | collective-permute-start | bytes 589832 | tf_op jit(solution)/shard_map/ppermute | solution.py:248
  27.6 6.6 %collective-permute-start.5 = (bf16[3,256,128]{2,1,0:T(8,128)(2,1)S(1)}, bf16[3,256,128]{2,1,0:T(8,128)(2,1)S(1)}, u32[]{:S(2)}, u32[]{:S(2)}) collective-permute-start(bf16[3,256,128]{2,1,0:T(8,128)(2,1)S(1)} %get-tuple-element.43), channel_id=1, source_target_pairs={{8,280},{9,281},{10,282},{11,283},{12,284},{13,285},{14,286},{15,2... | collective-permute-start | bytes 589832 | tf_op jit(solution)/shard_map/ppermute | solution.py:248
  28.9 6.5 %collective-permute-start.6 = (bf16[3,256,128]{2,1,0:T(8,128)(2,1)S(1)}, bf16[3,256,128]{2,1,0:T(8,128)(2,1)S(1)}, u32[]{:S(2)}, u32[]{:S(2)}) collective-permute-start(bf16[3,256,128]{2,1,0:T(8,128)(2,1)S(1)} %get-tuple-element.44), channel_id=1, source_target_pairs={{0,280},{1,281},{2,282},{3,283},{4,284},{5,285},{6,286},{7,287},{2... | collective-permute-start | bytes 589832 | tf_op jit(solution)/shard_map/ppermute | solution.py:248
  30.9 9.0 %collective-permute-start.10 = (bf16[4,256,128]{2,1,0:T(8,128)(2,1)S(1)}, bf16[4,256,128]{2,1,0:T(8,128)(2,1)S(1)}, u32[]{:S(2)}, u32[]{:S(2)}) collective-permute-start(bf16[4,256,128]{2,1,0:T(8,128)(2,1)S(1)} %get-tuple-element.52), channel_id=1, source_target_pairs={{256,16},{257,17},{258,18},{259,19},{260,20},{261,21},{262,22},{26... | collective-permute-start | bytes 786440 | tf_op jit(solution)/shard_map/ppermute | solution.py:248
  34.2 16.1 %collective-permute-start.11 = (bf16[4,256,128]{2,1,0:T(8,128)(2,1)S(1)}, bf16[4,256,128]{2,1,0:T(8,128)(2,1)S(1)}, u32[]{:S(2)}, u32[]{:S(2)}) collective-permute-start(bf16[4,256,128]{2,1,0:T(8,128)(2,1)S(1)} %get-tuple-element.53), channel_id=1, source_target_pairs={{256,24},{257,25},{258,26},{259,27},{260,28},{261,29},{262,30},{26... | collective-permute-start | bytes 786440 | tf_op jit(solution)/shard_map/ppermute | solution.py:248
  35.5 14.8 %collective-permute-start.12 = (bf16[4,256,128]{2,1,0:T(8,128)(2,1)S(1)}, bf16[4,256,128]{2,1,0:T(8,128)(2,1)S(1)}, u32[]{:S(2)}, u32[]{:S(2)}) collective-permute-start(bf16[4,256,128]{2,1,0:T(8,128)(2,1)S(1)} %get-tuple-element.55), channel_id=1, source_target_pairs={{264,256},{265,257},{266,258},{267,259},{268,260},{269,261},{270,2... | collective-permute-start | bytes 786440 | tf_op jit(solution)/shard_map/ppermute | solution.py:248
  36.2 14.1 %collective-permute-start.13 = (bf16[4,256,128]{2,1,0:T(8,128)(2,1)S(1)}, bf16[4,256,128]{2,1,0:T(8,128)(2,1)S(1)}, u32[]{:S(2)}, u32[]{:S(2)}) collective-permute-start(bf16[4,256,128]{2,1,0:T(8,128)(2,1)S(1)} %get-tuple-element.56), channel_id=1, source_target_pairs={{264,280},{265,281},{266,282},{267,283},{268,284},{269,285},{270,2... | collective-permute-start | bytes 786440 | tf_op jit(solution)/shard_map/ppermute | solution.py:248
  36.9 13.4 %collective-permute-start.14 = (bf16[4,256,128]{2,1,0:T(8,128)(2,1)S(1)}, bf16[4,256,128]{2,1,0:T(8,128)(2,1)S(1)}, u32[]{:S(2)}, u32[]{:S(2)}) collective-permute-start(bf16[4,256,128]{2,1,0:T(8,128)(2,1)S(1)} %get-tuple-element.57), channel_id=1, source_target_pairs={{256,280},{257,281},{258,282},{259,283},{260,284},{261,285},{262,2... | collective-permute-start | bytes 786440 | tf_op jit(solution)/shard_map/ppermute | solution.py:248
  55.4 11.1 %collective-permute-start.22 = (bf16[3,256,128]{2,1,0:T(8,128)(2,1)S(1)}, bf16[3,256,128]{2,1,0:T(8,128)(2,1)S(1)}, u32[]{:S(2)}, u32[]{:S(2)}) collective-permute-start(bf16[3,256,128]{2,1,0:T(8,128)(2,1)S(1)} %get-tuple-element.63.refs_4_), channel_id=1, source_target_pairs={{0,256},{1,257},{2,258},{3,259},{4,260},{5,261},{6,262},{7,263},{8... | collective-permute-start | bytes 589832 | tf_op jit(solution)/shard_map/ppermute | solution.py:248
  58.4 8.8 %collective-permute-start.26 = (bf16[3,256,128]{2,1,0:T(8,128)(2,1)S(1)}, bf16[3,256,128]{2,1,0:T(8,128)(2,1)S(1)}, u32[]{:S(2)}, u32[]{:S(2)}) collective-permute-start(bf16[3,256,128]{2,1,0:T(8,128)(2,1)S(1)} %get-tuple-element.64), channel_id=1, source_target_pairs={{256,264},{257,265},{258,266},{259,267},{260,268},{261,269},{262,2... | collective-permute-start | bytes 589832 | tf_op jit(solution)/shard_map/ppermute | solution.py:248
  59.1 9.4 %collective-permute-start.23 = (bf16[3,256,128]{2,1,0:T(8,128)(2,1)S(1)}, bf16[3,256,128]{2,1,0:T(8,128)(2,1)S(1)}, u32[]{:S(2)}, u32[]{:S(2)}) collective-permute-start(bf16[3,256,128]{2,1,0:T(8,128)(2,1)S(1)} %get-tuple-element.64), channel_id=1, source_target_pairs={{8,256},{9,257},{10,258},{11,259},{12,260},{13,261},{14,262},{15,2... | collective-permute-start | bytes 589832 | tf_op jit(solution)/shard_map/ppermute | solution.py:248
  63.7 4.9 %collective-permute-start.27 = (bf16[3,256,128]{2,1,0:T(8,128)(2,1)S(1)}, bf16[3,256,128]{2,1,0:T(8,128)(2,1)S(1)}, u32[]{:S(2)}, u32[]{:S(2)}) collective-permute-start(bf16[3,256,128]{2,1,0:T(8,128)(2,1)S(1)} %get-tuple-element.65), channel_id=1, source_target_pairs={{280,264},{281,265},{282,266},{283,267},{284,268},{285,269},{286,2... | collective-permute-start | bytes 589832 | tf_op jit(solution)/shard_map/ppermute | solution.py:248
  64.3 12.3 %collective-permute-start.24 = (bf16[3,256,128]{2,1,0:T(8,128)(2,1)S(1)}, bf16[3,256,128]{2,1,0:T(8,128)(2,1)S(1)}, u32[]{:S(2)}, u32[]{:S(2)}) collective-permute-start(bf16[3,256,128]{2,1,0:T(8,128)(2,1)S(1)} %get-tuple-element.65), channel_id=1, source_target_pairs={{16,256},{17,257},{18,258},{19,259},{20,260},{21,261},{22,262},{23... | collective-permute-start | bytes 589832 | tf_op jit(solution)/shard_map/ppermute | solution.py:248
  66.5 10.1 %collective-permute-start.28 = (bf16[3,256,128]{2,1,0:T(8,128)(2,1)S(1)}, bf16[3,256,128]{2,1,0:T(8,128)(2,1)S(1)}, u32[]{:S(2)}, u32[]{:S(2)}) collective-permute-start(bf16[3,256,128]{2,1,0:T(8,128)(2,1)S(1)} %get-tuple-element.66), channel_id=1, source_target_pairs={{280,256},{281,257},{282,258},{283,259},{284,260},{285,261},{286,2... | collective-permute-start | bytes 589832 | tf_op jit(solution)/shard_map/ppermute | solution.py:248
  67.2 11.5 %collective-permute-start.25 = (bf16[3,256,128]{2,1,0:T(8,128)(2,1)S(1)}, bf16[3,256,128]{2,1,0:T(8,128)(2,1)S(1)}, u32[]{:S(2)}, u32[]{:S(2)}) collective-permute-start(bf16[3,256,128]{2,1,0:T(8,128)(2,1)S(1)} %get-tuple-element.66), channel_id=1, source_target_pairs={{24,256},{25,257},{26,258},{27,259},{28,260},{29,261},{30,262},{31... | collective-permute-start | bytes 589832 | tf_op jit(solution)/shard_map/ppermute | solution.py:248
  79.6 26.8 %collective-permute-start.29 = (bf16[3,128,768]{2,1,0:T(8,128)(2,1)S(1)}, bf16[3,128,768]{2,1,0:T(8,128)(2,1)S(1)}, u32[]{:S(2)}, u32[]{:S(2)}) collective-permute-start(bf16[3,128,768]{2,1,0:T(8,128)(2,1)S(1)} %get-tuple-element.68), channel_id=1, source_target_pairs={{256,257},{257,256},{258,259},{259,258},{260,261},{261,260},{262,2... | collective-permute-start | bytes 1769480 | tf_op jit(solution)/shard_map/ppermute | solution.py:248
  83.2 5.2 %collective-permute-start.18 = (bf16[3,256,128]{2,1,0:T(8,128)(2,1)S(1)}, bf16[3,256,128]{2,1,0:T(8,128)(2,1)S(1)}, u32[]{:S(2)}, u32[]{:S(2)}) collective-permute-start(bf16[3,256,128]{2,1,0:T(8,128)(2,1)S(1)} %get-tuple-element.59.refs_0_), channel_id=1, source_target_pairs={{256,0},{257,1},{258,2},{259,3},{260,4},{261,5},{262,6},{263,7},{2... | collective-permute-start | bytes 589832 | tf_op jit(solution)/shard_map/ppermute | solution.py:248
  83.9 8.8 %collective-permute-start.19 = (bf16[3,256,128]{2,1,0:T(8,128)(2,1)S(1)}, bf16[3,256,128]{2,1,0:T(8,128)(2,1)S(1)}, u32[]{:S(2)}, u32[]{:S(2)}) collective-permute-start(bf16[3,256,128]{2,1,0:T(8,128)(2,1)S(1)} %get-tuple-element.60), channel_id=1, source_target_pairs={{256,8},{257,9},{258,10},{259,11},{260,12},{261,13},{262,14},{263,... | collective-permute-start | bytes 589832 | tf_op jit(solution)/shard_map/ppermute | solution.py:248
  85.2 9.7 %collective-permute-start.15 = (bf16[3,256,128]{2,1,0:T(8,128)(2,1)S(1)}, bf16[3,256,128]{2,1,0:T(8,128)(2,1)S(1)}, u32[]{:S(2)}, u32[]{:S(2)}) collective-permute-start(bf16[3,256,128]{2,1,0:T(8,128)(2,1)S(1)} %get-tuple-element.60), channel_id=1, source_target_pairs={{8,0},{9,1},{10,2},{11,3},{12,4},{13,5},{14,6},{15,7},{0,8},{1,9},... | collective-permute-start | bytes 589832 | tf_op jit(solution)/shard_map/ppermute | solution.py:248
  87.1 10.4 %collective-permute-start.20 = (bf16[3,256,128]{2,1,0:T(8,128)(2,1)S(1)}, bf16[3,256,128]{2,1,0:T(8,128)(2,1)S(1)}, u32[]{:S(2)}, u32[]{:S(2)}) collective-permute-start(bf16[3,256,128]{2,1,0:T(8,128)(2,1)S(1)} %get-tuple-element.61), channel_id=1, source_target_pairs={{280,8},{281,9},{282,10},{283,11},{284,12},{285,13},{286,14},{287,... | collective-permute-start | bytes 589832 | tf_op jit(solution)/shard_map/ppermute | solution.py:248
  88.4 14.4 %collective-permute-start.16 = (bf16[3,256,128]{2,1,0:T(8,128)(2,1)S(1)}, bf16[3,256,128]{2,1,0:T(8,128)(2,1)S(1)}, u32[]{:S(2)}, u32[]{:S(2)}) collective-permute-start(bf16[3,256,128]{2,1,0:T(8,128)(2,1)S(1)} %get-tuple-element.61), channel_id=1, source_target_pairs={{16,0},{17,1},{18,2},{19,3},{20,4},{21,5},{22,6},{23,7},{24,8},{25... | collective-permute-start | bytes 589832 | tf_op jit(solution)/shard_map/ppermute | solution.py:248
  92.7 10.2 %collective-permute-start.21 = (bf16[3,256,128]{2,1,0:T(8,128)(2,1)S(1)}, bf16[3,256,128]{2,1,0:T(8,128)(2,1)S(1)}, u32[]{:S(2)}, u32[]{:S(2)}) collective-permute-start(bf16[3,256,128]{2,1,0:T(8,128)(2,1)S(1)} %get-tuple-element.62), channel_id=1, source_target_pairs={{280,0},{281,1},{282,2},{283,3},{284,4},{285,5},{286,6},{287,7},{2... | collective-permute-start | bytes 589832 | tf_op jit(solution)/shard_map/ppermute | solution.py:248
  94.8 11.6 %collective-permute-start.17 = (bf16[3,256,128]{2,1,0:T(8,128)(2,1)S(1)}, bf16[3,256,128]{2,1,0:T(8,128)(2,1)S(1)}, u32[]{:S(2)}, u32[]{:S(2)}) collective-permute-start(bf16[3,256,128]{2,1,0:T(8,128)(2,1)S(1)} %get-tuple-element.62), channel_id=1, source_target_pairs={{24,0},{25,1},{26,2},{27,3},{28,4},{29,5},{30,6},{31,7},{16,8},{17... | collective-permute-start | bytes 589832 | tf_op jit(solution)/shard_map/ppermute | solution.py:248

commit v2 on v1

v2 whole, which is shorter than its diff:
```python
import math

import jax
import jax.numpy as jnp
from jax import lax
from jax.experimental import pallas as pl
from jax.experimental.pallas import tpu as pltpu
from jax.sharding import PartitionSpec as P

HD = 128
BLK = 256
LEN = 1024
SCALE = 1.0 / math.sqrt(HD)
SCALE2 = SCALE * math.log2(math.e)
AXES = ("section", "dp", "tensor")
BF = jnp.bfloat16
F32 = jnp.float32
VM = pl.BlockSpec(memory_space=pltpu.VMEM)
SM = pl.BlockSpec(memory_space=pltpu.SMEM)


def first_head(z):
    return jnp.where(z > 0, z + 1, 0)


def second_head(z):
    return jnp.where(z == 3, 5, 1)


def is_edge(z):
    return (z == 0) | (z == 3)


def head_cols(head):
    return pl.ds(pl.multiple_of(head * HD, HD), HD)


def rows_of(index, size):
    return pl.ds(pl.multiple_of(index * size, size), size)


def dot(a, b):
    return jnp.dot(a, b, preferred_element_type=F32)


def flip(x):
    return x.astype(F32).T.astype(BF)


def call(kernel, outs, args, scratch=(), flops=0, spec=VM, limit=48):
    return pl.pallas_call(
        kernel,
        out_shape=[jax.ShapeDtypeStruct(s, d) for s, d in outs],
        in_specs=[SM] + [spec] * (len(args) - 1),
        out_specs=[VM] * len(outs),
        scratch_shapes=list(scratch),
        compiler_params=pltpu.CompilerParams(vmem_limit_bytes=limit * 1024 * 1024),
        cost_estimate=pl.CostEstimate(flops=flops, bytes_accessed=4000000, transcendentals=0),
    )(*args)


def selection(rows, cols, odd, spread):
    row = lax.broadcasted_iota(jnp.int32, (rows, cols), 0)
    col = lax.broadcasted_iota(jnp.int32, (rows, cols), 1)
    near, far = (col, row) if spread else (row, col)
    wanted = jnp.where(near < HD, 2 * near + odd, 2 * (near - HD) + 1 - odd)
    return jnp.where(far == wanted, 1.0, 0.0).astype(BF)


def pick_kernel(info, local_hbm, grad_hbm, *refs):
    outs, (local, sems) = refs[:-2], refs[-2:]
    z, s = info[0], info[2]
    copies = [pltpu.make_async_copy(local_hbm.at[j], local.at[j], sems.at[j]) for j in range(3)]
    copies += [pltpu.make_async_copy(grad_hbm, local.at[3], sems.at[3])]
    for copy in copies:
        copy.start()
    for copy in copies:
        copy.wait()

    def fill(out, head, parts):
        for j in range(parts):
            out[j * BLK : (j + 1) * BLK] = local[j, :, head_cols(head)]

    for k in (0, 1):
        heads = first_head(z ^ k), second_head(z ^ k)
        fill(outs[k], jnp.where(s == 0, heads[0], heads[1]), 4)
        fill(outs[2 + k], jnp.where(s == 0, heads[1], heads[0]), 4)

    @pl.when(s == 0)
    def _():
        for k in (2, 3):
            fill(outs[2 + k], first_head(z ^ k), 3)
            fill(outs[4 + k], second_head(z ^ k), 3)

    @pl.when(s == 1)
    def _():
        for k in (2, 3):
            fill(outs[6 + k], first_head(z ^ k), 4)
            fill(outs[8 + k], second_head(z ^ k), 4)


def part_kernel(info, c3, c2, d3, d2, cross1, same1, cross0, same0, own, away, near0, near1):
    z, h, s = info[0], info[1], info[2]
    take = selection(256, 256, h, False)

    def split(chunks):
        for k in range(4):
            rows = rows_of(z ^ k, HD)
            for j in range(4):
                both = dot(take, chunks[k][j * BLK : (j + 1) * BLK]).astype(BF)
                own[j, rows, :] = both[:HD]
                away[j, rows, :] = both[HD:]

    @pl.when(s == 0)
    def _():
        split((cross0, cross1, c2, c3))
        near0[...] = same0[0 : 3 * BLK]
        near1[...] = same1[0 : 3 * BLK]

    @pl.when(s == 1)
    def _():
        split((same0, same1, d2, d3))
        near0[...] = cross0[0 : 3 * BLK]
        near1[...] = cross1[0 : 3 * BLK]


def score_block(keys, qt, i):
    n = (i + 1) * BLK
    st = dot(keys[0:n], qt[:, i * BLK : n]) * SCALE2
    key = lax.broadcasted_iota(jnp.int32, (BLK, BLK), 0)
    qry = lax.broadcasted_iota(jnp.int32, (BLK, BLK), 1)
    tail = jnp.where(key <= qry, st[n - BLK :], -jnp.inf)
    return tail if i == 0 else jnp.concatenate([st[: n - BLK], tail], axis=0)


def backward_block(i, p, keys_t, values, q, g, gt, delta, dqt, dk, dv):
    n = (i + 1) * BLK
    cols = slice(i * BLK, n)
    dp = dot(values[0:n], gt[:, cols])
    ds = (p * (dp - delta)).astype(BF)
    dqt[:, cols] = (dot(keys_t[:, 0:n], ds) * SCALE).astype(BF)
    add_k = dot(ds, q[cols])
    add_v = dot(p.astype(BF), g[cols])
    if i > 0:
        dk[0 : n - BLK] += add_k[: n - BLK]
        dv[0 : n - BLK] += add_v[: n - BLK]
    dk[n - BLK : n] = add_k[n - BLK :]
    dv[n - BLK : n] = add_v[n - BLK :]


def hand_out(info, outs, dq, dk, dv):
    z = info[0]
    for k in range(4):
        rows = rows_of(z ^ k, BLK)
        outs[k][0] = dq[rows]
        outs[k][1] = (dk[rows] * SCALE).astype(BF)
        outs[k][2] = dv[rows].astype(BF)


def forward_kernel(info, a3, a2, b3, b2, near0, near1, qkv, ot, lse, qt, vt):
    z, s = info[0], info[2]

    def join(chunks):
        for k in range(4):
            for j in range(3):
                qkv[j, rows_of(z ^ k, BLK), :] = chunks[k][j * BLK : (j + 1) * BLK]

    @pl.when(s == 0)
    def _():
        join((near0, near1, a2, a3))

    @pl.when(s == 1)
    def _():
        join((near0, near1, b2, b3))

    qt[...] = flip(qkv[0])
    vt[...] = flip(qkv[2])
    keys = qkv.at[1]
    for i in range(4):
        n = (i + 1) * BLK
        cols = slice(i * BLK, n)
        st = score_block(keys, qt, i)
        top = jnp.max(st, axis=0, keepdims=True)
        p = jnp.exp2(st - top)
        total = jnp.sum(p, axis=0, keepdims=True)
        ot[:, cols] = (dot(vt[:, 0:n], p.astype(BF)) / total).astype(BF)
        lse[:, cols] = jnp.broadcast_to(top + jnp.log2(total), (8, BLK))


def second_kernel(info, own, came, ot1, keep, give, g1t, qkvg, qt, kt, vt, gt, dq, dk, dv):
    h = info[1]

    def block(b, part):
        return pl.ds(pl.multiple_of(b * BLK + part * HD, HD), HD)

    for j in range(4):
        for b in range(4):
            qkvg[j, block(b, h), :] = own[j, b * HD : (b + 1) * HD]
            qkvg[j, block(b, 1 - h), :] = came[j, b * HD : (b + 1) * HD]
    q = qkvg[0].astype(F32) + ot1[...].astype(F32).T
    qkvg[0] = q.astype(BF)
    qt[...] = q.T.astype(BF)
    kt[...] = flip(qkvg[1])
    vt[...] = flip(qkvg[2])
    gt[...] = flip(qkvg[3])
    keys, values = qkvg.at[1], qkvg.at[2]
    for i in range(4):
        n = (i + 1) * BLK
        cols = slice(i * BLK, n)
        st = score_block(keys, qt, i)
        top = jnp.max(st, axis=0, keepdims=True)
        p = jnp.exp2(st - top)
        p = p * (1.0 / jnp.sum(p, axis=0, keepdims=True))
        o = dot(vt[:, 0:n], p.astype(BF)).astype(BF)
        delta = jnp.sum(gt[:, cols].astype(F32) * o.astype(F32), axis=0, keepdims=True)
        backward_block(i, p, kt, values, qkvg.at[0], qkvg.at[3], gt, delta, g1t, dk, dv)
    dq[...] = flip(g1t[...])
    for b in range(4):
        rows = slice(b * HD, (b + 1) * HD)
        for out, part in ((keep, h), (give, 1 - h)):
            out[0, rows] = dq[block(b, part)]
            out[1, rows] = (dk[block(b, part)] * SCALE).astype(BF)
            out[2, rows] = dv[block(b, part)].astype(BF)


def first_backward_kernel(info, qkv, ot, lse, gt, *refs):
    outs = refs[0:4]
    g, qt, kt, dqt, dq, dk, dv = refs[4:]
    z = info[0]
    qt[...] = flip(qkv[0])
    kt[...] = flip(qkv[1])
    g[...] = flip(gt[...])
    keys, values = qkv.at[1], qkv.at[2]
    for i in range(4):
        cols = slice(i * BLK, (i + 1) * BLK)
        st = score_block(keys, qt, i)
        p = jnp.exp2(st - lse[0:1, cols])
        delta = jnp.sum(gt[:, cols].astype(F32) * ot[:, cols].astype(F32), axis=0, keepdims=True)
        backward_block(i, p, kt, values, qkv.at[0], g, gt, delta, dqt, dk, dv)
    dq[...] = flip(dqt[...])
    for k in range(4):
        rows = rows_of(z ^ k, BLK)
        outs[k][0] = dq[rows]
        outs[k][1] = (dk[rows] * SCALE).astype(BF)
        outs[k][2] = dv[rows].astype(BF)


def weave_kernel(info, keep, came, d0, d1, same0, same1, cross0, cross1, out2, out3):
    z, h, s = info[0], info[1], info[2]
    put = selection(256, 256, h, True)

    def weave(out, k):
        rows = rows_of(z ^ k, HD)
        for j in range(3):
            both = jnp.concatenate([keep[j, rows, :], came[j, rows, :]], axis=0)
            out[j] = dot(put, both).astype(BF)

    @pl.when(s == 0)
    def _():
        same0[...] = d0[...]
        same1[...] = d1[...]
        weave(cross0, 0)
        weave(cross1, 1)

    @pl.when(s == 1)
    def _():
        cross0[...] = d0[...]
        cross1[...] = d1[...]
        weave(same0, 0)
        weave(same1, 1)

    weave(out2, 2)
    weave(out3, 3)


def finish_kernel(info, a3, a2, b3, b2, c3, c2, d3, d2, *refs):
    cross1, same1, cross0, same0, out = refs
    z, s = info[0], info[2]

    def place(slot_a, slot_b):
        for k in range(4):
            out[:, :, head_cols(first_head(z ^ k))] = slot_a[k][...]

            @pl.when(is_edge(z ^ k))
            def _(k=k):
                out[:, :, head_cols(second_head(z ^ k))] = slot_b[k][...]

    @pl.when(s == 0)
    def _():
        place((same0, same1, a2, a3), (cross0, cross1, b2, b3))

    @pl.when(s == 1)
    def _():
        place((cross0, cross1, c2, c3), (same0, same1, d2, d3))


def build(n_dp, n_tensor):
    def index(s, d, t):
        return (s * n_dp + d) * n_tensor + t

    def everywhere(rule):
        pairs = []
        for d in range(n_dp):
            for t in range(n_tensor):
                pairs += rule(d, t)
        return pairs

    def send(value, pairs):
        return lax.ppermute(value, AXES, pairs)

    def inward(src, slot, k):
        return everywhere(
            lambda d, t: [(index(src, d, t), index(slot, d ^ k, t))]
            if slot == 0 or (d ^ k) % 4 in (0, 3)
            else []
        )

    def outward(dst, slot, k):
        return [(b, a) for a, b in inward(dst, slot, k)]

    def cross():
        return everywhere(
            lambda d, t: [
                (index(c, d, t), index(c, d, t ^ 1)) for c in range(2) if c == 0 or d % 4 in (0, 3)
            ]
        )

    def body(projections, out_grad):
        s = lax.axis_index("section")
        z = lax.axis_index("dp") % 4
        h = lax.axis_index("tensor") % 2
        info = jnp.stack([z, h, s]).astype(jnp.int32)
        local = projections[0]
        rows, cols = local.shape[1:]
        small, large = ((3 * BLK, HD), BF), ((4 * BLK, HD), BF)
        chunk = ((3, BLK, HD), BF)
        vm = pltpu.VMEM
        tall, wide = vm((LEN, HD), BF), vm((HD, LEN), BF)
        acc = vm((LEN, HD), F32)

        same0, same1, cross0, cross1, a2, a3, b2, b3, c2, c3, d2, d3 = call(
            pick_kernel,
            [large] * 4 + [small] * 4 + [large] * 4,
            [info, local, out_grad],
            [vm((4, rows, cols), BF), pltpu.SemaphoreType.DMA((4,))],
            spec=pl.BlockSpec(memory_space=pl.ANY),
            limit=51,
        )
        c3 = send(c3, inward(1, 0, 3))
        c2 = send(c2, inward(1, 0, 2))
        d3 = send(d3, inward(1, 1, 3))
        d2 = send(d2, inward(1, 1, 2))
        same1 = send(same1, inward(0, 0, 1) + inward(1, 1, 1))
        cross1 = send(cross1, inward(0, 1, 1) + inward(1, 0, 1))
        cross0 = send(cross0, inward(0, 1, 0) + inward(1, 0, 0))
        own, away, near0, near1 = call(
            part_kernel,
            [((4, 4 * HD, HD), BF)] * 2 + [small] * 2,
            [info, c3, c2, d3, d2, cross1, same1, cross0, same0],
        )
        came = send(away, cross())
        a3 = send(a3, inward(0, 0, 3))
        a2 = send(a2, inward(0, 0, 2))
        b3 = send(b3, inward(0, 1, 3))
        b2 = send(b2, inward(0, 1, 2))
        qkv, ot, lse = call(
            forward_kernel,
            [((3, LEN, HD), BF), ((HD, LEN), BF), ((8, LEN), F32)],
            [info, a3, a2, b3, b2, near0, near1],
            [wide, wide],
        )
        keep, give, g1t = call(
            second_kernel,
            [((3, 4 * HD, HD), BF)] * 2 + [((HD, LEN), BF)],
            [info, own, came, ot],
            [vm((4, LEN, HD), BF)] + [wide] * 4 + [tall, acc, acc],
        )
        came = send(give, cross())
        d0, d1, d2, d3 = call(
            first_backward_kernel,
            [chunk] * 4,
            [info, qkv, ot, lse, g1t],
            [tall, wide, wide, wide, tall, acc, acc],
        )
        a3 = send(d3, outward(0, 0, 3))
        a2 = send(d2, outward(0, 0, 2))
        b3 = send(d3, outward(0, 1, 3))
        b2 = send(d2, outward(0, 1, 2))
        same0, same1, cross0, cross1, c2, c3 = call(
            weave_kernel, [chunk] * 6, [info, keep, came, d0, d1]
        )
        d3 = send(c3, outward(1, 1, 3))
        d2 = send(c2, outward(1, 1, 2))
        c3 = send(c3, outward(1, 0, 3))
        c2 = send(c2, outward(1, 0, 2))
        same1 = send(same1, outward(0, 0, 1) + outward(1, 1, 1))
        cross1 = send(cross1, outward(0, 1, 1) + outward(1, 0, 1))
        cross0 = send(cross0, outward(0, 1, 0) + outward(1, 0, 0))
        (out,) = call(
            finish_kernel,
            [((3, rows, cols), BF)],
            [info, a3, a2, b3, b2, c3, c2, d3, d2, cross1, same1, cross0, same0],
        )
        return out[None]

    return body


def solution(mesh):
    body = build(mesh.shape["dp"], mesh.shape["tensor"])
    in_specs = (P("section", None, "dp", "tensor"), P("dp", "tensor"))
    out_specs = P("section", None, "dp", "tensor")
    return jax.shard_map(body, mesh=mesh, in_specs=in_specs, out_specs=out_specs, check_vma=False)
```

time: 109 us -> 112 us (1.028)
  the two profiles are of different devices: /device:TPU:32 before, /device:TPU:1 now
where the time goes in v2:
time: 112 us; the launch traced here: 111 us
  starting transfers between devices  61.5 us (55%)
  waiting for transfers between devices  32.2 us (29%)
  Pallas kernels  16.9 us (15%)
    ppermute x24, starting transfers between devices, send(): return lax.ppermute(value, AXES, pairs)  61.5 us
    ppermute x24, waiting for transfers between devices, send(): return lax.ppermute(value, AXES, pairs)  32.2 us
    pallas_call x7, Pallas kernels, call(): pl.pallas_call(kernel, out_shape=[jax.ShapeDtypeStruct(s, d) for s, d in...  16.9 us
  transfers between devices with their start and end apart: 24, of which 9 were waited for; matrix products, arithmetic and copies ran while one was open for 0% of the time, Pallas kernels for 6%

profile of v2, /device:TPU:1, one launch (start us, length us, event | category | flops | bytes accessed | tf_op | source)
XLA Modules:
  0.0 111.0 jit_solution(8750782749147978422)
XLA Ops:
  0.0 0.1 pad_add_fusion.info
  0.1 2.3 %shard_map.28 = (bf16[1024,128]{1,0:T(8,128)(2,1)S(1)}, bf16[1024,128]{1,0:T(8,128)(2,1)S(1)}, bf16[1024,128]{1,0:T(8,128)(2,1)S(1)}, bf16[1024,128]{1,0:T(8,128...) custom-call(s32[3]{0:T(128)S(1)} %pad_add_fusion.info, ...), custom_call_target="tpu_custom_call" | custom-call | bytes 4000000 | tf_op jit(solution)/shard_map/pallas_call | solution.py:51
  2.4 7.6 %collective-permute-start.4 = (bf16[1024,128]{1,0:T(8,128)(2,1)S(1)}, bf16[1024,128]{1,0:T(8,128)(2,1)S(1)}, u32[]{:S(2)}, u32[]{:S(2)}) collective-permute-start(bf16[1024,128]{1,0:T(8,128)(2,1)S(1)} %get-tuple-element.41), channel_id=1, source_target_pairs={{256,24},{257,25},{258,26},{259,27},{260,28},{261,29},{262,30},{26... | collective-permute-start | bytes 786440 | tf_op jit(solution)/shard_map/ppermute | solution.py:309
  10.0 1.3 %collective-permute-start.5 = (bf16[1024,128]{1,0:T(8,128)(2,1)S(1)}, bf16[1024,128]{1,0:T(8,128)(2,1)S(1)}, u32[]{:S(2)}, u32[]{:S(2)}) collective-permute-start(bf16[1024,128]{1,0:T(8,128)(2,1)S(1)} %get-tuple-element.42), channel_id=1, source_target_pairs={{256,16},{257,17},{258,18},{259,19},{260,20},{261,21},{262,22},{26... | collective-permute-start | bytes 786440 | tf_op jit(solution)/shard_map/ppermute | solution.py:309
  11.3 6.2 %collective-permute-start.6 = (bf16[1024,128]{1,0:T(8,128)(2,1)S(1)}, bf16[1024,128]{1,0:T(8,128)(2,1)S(1)}, u32[]{:S(2)}, u32[]{:S(2)}) collective-permute-start(bf16[1024,128]{1,0:T(8,128)(2,1)S(1)} %get-tuple-element.43), channel_id=1, source_target_pairs={{256,280},{257,281},{258,282},{259,283},{260,284},{261,285},{262,2... | collective-permute-start | bytes 786440 | tf_op jit(solution)/shard_map/ppermute | solution.py:309
  17.5 1.3 %collective-permute-start.7 = (bf16[1024,128]{1,0:T(8,128)(2,1)S(1)}, bf16[1024,128]{1,0:T(8,128)(2,1)S(1)}, u32[]{:S(2)}, u32[]{:S(2)}) collective-permute-start(bf16[1024,128]{1,0:T(8,128)(2,1)S(1)} %get-tuple-element.44), channel_id=1, source_target_pairs={{264,280},{265,281},{266,282},{267,283},{268,284},{269,285},{270,2... | collective-permute-start | bytes 786440 | tf_op jit(solution)/shard_map/ppermute | solution.py:309
  18.8 1.9 %collective-permute-start.8 = (bf16[1024,128]{1,0:T(8,128)(2,1)S(1)}, bf16[1024,128]{1,0:T(8,128)(2,1)S(1)}, u32[]{:S(2)}, u32[]{:S(2)}) collective-permute-start(bf16[1024,128]{1,0:T(8,128)(2,1)S(1)} %get-tuple-element.45), channel_id=1, source_target_pairs={{8,256},{9,257},{10,258},{11,259},{12,260},{13,261},{14,262},{15,2... | collective-permute-start | bytes 786440 | tf_op jit(solution)/shard_map/ppermute | solution.py:309
  20.8 0.0 collective-permute-done.4.c3
  20.8 1.3 %collective-permute-start.9 = (bf16[1024,128]{1,0:T(8,128)(2,1)S(1)}, bf16[1024,128]{1,0:T(8,128)(2,1)S(1)}, u32[]{:S(2)}, u32[]{:S(2)}) collective-permute-start(bf16[1024,128]{1,0:T(8,128)(2,1)S(1)} %get-tuple-element.46), channel_id=1, source_target_pairs={{0,8},{1,9},{2,10},{3,11},{4,12},{5,13},{6,14},{7,15},{8,0},{9,1},... | collective-permute-start | bytes 786440 | tf_op jit(solution)/shard_map/ppermute | solution.py:309
  22.1 0.0 collective-permute-done.5.c2
  22.1 7.1 %collective-permute-start.10 = (bf16[1024,128]{1,0:T(8,128)(2,1)S(1)}, bf16[1024,128]{1,0:T(8,128)(2,1)S(1)}, u32[]{:S(2)}, u32[]{:S(2)}) collective-permute-start(bf16[1024,128]{1,0:T(8,128)(2,1)S(1)} %get-tuple-element.47), channel_id=1, source_target_pairs={{0,256},{1,257},{2,258},{3,259},{4,260},{5,261},{6,262},{7,263},{2... | collective-permute-start | bytes 786440 | tf_op jit(solution)/shard_map/ppermute | solution.py:309
  29.1 0.0 collective-permute-done.6.d3
  29.1 0.2 collective-permute-done.7.d2
  29.4 5.7 %collective-permute-done.8.cross1 = bf16[1024,128]{1,0:T(8,128)(2,1)S(1)} collective-permute-done((bf16[1024,128]{1,0:T(8,128)(2,1)S(1)}, bf16[1024,128]{1,0:T(8,128)(2,1)S(1)}, u32[]{:S(2)}, u32[]{:S(2)}) %collective-permute-start.8) | collective-permute-done | bytes 262176 | tf_op jit(solution)/shard_map/ppermute | solution.py:309
  35.1 5.6 %collective-permute-done.9.same1 = bf16[1024,128]{1,0:T(8,128)(2,1)S(1)} collective-permute-done((bf16[1024,128]{1,0:T(8,128)(2,1)S(1)}, bf16[1024,128]{1,0:T(8,128)(2,1)S(1)}, u32[]{:S(2)}, u32[]{:S(2)}) %collective-permute-start.9) | collective-permute-done | bytes 262176 | tf_op jit(solution)/shard_map/ppermute | solution.py:309
  40.7 0.0 collective-permute-done.10.cross0
  40.7 1.3 %shard_map.29 = (bf16[4,512,128]{2,1,0:T(8,128)(2,1)S(1)}, bf16[4,512,128]{2,1,0:T(8,128)(2,1)S(1)}, bf16[768,128]{1,0:T(8,128)(2,1)S(1)}, bf16[768,128]{1,0:T(8,128)(2,1)S(1)}) custom-call(s32[3]{0:T(128)S(1)} %pad_add_fusion.info, bf16[1024,128]{1,0:T(8,128)(2,1)S(1)} %collective-permute-done.4.c3, bf16[1024,128]{1,0:T(8,128)(2,1)S(1)} %collective-permute-done.5.c2, ...), custom_call_target="tpu_custom_call" | custom-call | bytes 4000000 | tf_op jit(solution)/shard_map/pallas_call | solution.py:51
  42.0 1.9 %collective-permute-start.11 = (bf16[4,512,128]{2,1,0:T(8,128)(2,1)S(1)}, bf16[4,512,128]{2,1,0:T(8,128)(2,1)S(1)}, u32[]{:S(2)}, u32[]{:S(2)}) collective-permute-start(bf16[4,512,128]{2,1,0:T(8,128)(2,1)S(1)} %get-tuple-element.55), channel_id=1, source_target_pairs={{0,1},{256,257},{1,0},{257,256},{2,3},{258,259},{3,2},{259,258},{4... | collective-permute-start | bytes 1572872 | tf_op jit(solution)/shard_map/ppermute | solution.py:309
  43.9 0.7 collective-permute-start
  44.6 0.7 collective-permute-start.1
  45.3 1.3 %collective-permute-start.2 = (bf16[768,128]{1,0:T(8,128)(2,1)S(1)}, bf16[768,128]{1,0:T(8,128)(2,1)S(1)}, u32[]{:S(2)}, u32[]{:S(2)}) collective-permute-start(bf16[768,128]{1,0:T(8,128)(2,1)S(1)} %get-tuple-element.39), channel_id=1, source_target_pairs={{0,280},{1,281},{2,282},{3,283},{4,284},{5,285},{6,286},{7,287},{2... | collective-permute-start | bytes 589832 | tf_op jit(solution)/shard_map/ppermute | solution.py:309
  46.6 1.3 %collective-permute-start.3 = (bf16[768,128]{1,0:T(8,128)(2,1)S(1)}, bf16[768,128]{1,0:T(8,128)(2,1)S(1)}, u32[]{:S(2)}, u32[]{:S(2)}) collective-permute-start(bf16[768,128]{1,0:T(8,128)(2,1)S(1)} %get-tuple-element.40), channel_id=1, source_target_pairs={{8,280},{9,281},{10,282},{11,283},{12,284},{13,285},{14,286},{15,2... | collective-permute-start | bytes 589832 | tf_op jit(solution)/shard_map/ppermute | solution.py:309
  47.9 0.0 collective-permute-done.a3
  47.9 9.7 %collective-permute-done.2.b3 = bf16[768,128]{1,0:T(8,128)(2,1)S(1)} collective-permute-done((bf16[768,128]{1,0:T(8,128)(2,1)S(1)}, bf16[768,128]{1,0:T(8,128)(2,1)S(1)}, u32[]{:S(2)}, u32[]{:S(2)}) %collective-permute-start.2) | collective-permute-done | bytes 196640 | tf_op jit(solution)/shard_map/ppermute | solution.py:309
  57.6 3.9 %collective-permute-done.3.b2 = bf16[768,128]{1,0:T(8,128)(2,1)S(1)} collective-permute-done((bf16[768,128]{1,0:T(8,128)(2,1)S(1)}, bf16[768,128]{1,0:T(8,128)(2,1)S(1)}, u32[]{:S(2)}, u32[]{:S(2)}) %collective-permute-start.3) | collective-permute-done | bytes 196640 | tf_op jit(solution)/shard_map/ppermute | solution.py:309
  61.5 2.4 %shard_map.30 = (bf16[3,1024,128]{2,1,0:T(8,128)(2,1)S(1)}, bf16[128,1024]{1,0:T(8,128)(2,1)S(1)}, f32[8,1024]{1,0:T(8,128)S(1)}) custom-call(s32[3]{0:T(128)S(1)} %pad_add_fusion.info, bf16[768,128]{1,0:T(8,128)(2,1)S(1)} %collective-permute-done.a3, bf16[768,128]{1,0:T(8,128)(2,1)S(1)} %collective-permute-done.1.a2, ...), custom_call_target="tpu_custom_call" | custom-call | bytes 4000000 | tf_op jit(solution)/shard_map/pallas_call | solution.py:51
  63.9 5.0 %shard_map.31 = (bf16[3,512,128]{2,1,0:T(8,128)(2,1)S(1)}, bf16[3,512,128]{2,1,0:T(8,128)(2,1)S(1)}, bf16[128,1024]{1,0:T(8,128)(2,1)S(1)}) custom-call(s32[3]{0:T(128)S(1)} %pad_add_fusion.info, bf16[4,512,128]{2,1,0:T(8,128)(2,1)S(1)} %get-tuple-element.54.own, bf16[4,512,128]{2,1,0:T(8,128)(2,1)S(1)} %collective-permute-done.11.came, ...), custom_call_target="tpu_custom_call" | custom-call | bytes 4000000 | tf_op jit(solution)/shard_map/pallas_call | solution.py:51
  68.9 5.1 %collective-permute-start.16 = (bf16[3,512,128]{2,1,0:T(8,128)(2,1)S(1)}, bf16[3,512,128]{2,1,0:T(8,128)(2,1)S(1)}, u32[]{:S(2)}, u32[]{:S(2)}) collective-permute-start(bf16[3,512,128]{2,1,0:T(8,128)(2,1)S(1)} %get-tuple-element.60), channel_id=1, source_target_pairs={{0,1},{256,257},{1,0},{257,256},{2,3},{258,259},{3,2},{259,258},{4... | collective-permute-start | bytes 1179656 | tf_op jit(solution)/shard_map/ppermute | solution.py:309
  74.1 2.9 %shard_map.32 = (bf16[3,256,128]{2,1,0:T(8,128)(2,1)S(1)}, bf16[3,256,128]{2,1,0:T(8,128)(2,1)S(1)}, bf16[3,256,128]{2,1,0:T(8,128)(2,1)S(1)}, bf16[3,256,128]{2,1,0:T(8,128)(2,1)S(1)}) custom-call(s32[3]{0:T(128)S(1)} %pad_add_fusion.info, bf16[3,1024,128]{2,1,0:T(8,128)(2,1)S(1)} %get-tuple-element.51.qkv, bf16[128,1024]{1,0:T(8,128)(2,1)S(1)} %get-tuple-element.52.ot1.ot, ...), custom_call_target="tpu_custom_call" | custom-call | bytes 4000000 | tf_op jit(solution)/shard_map/pallas_call | solution.py:51
  76.9 1.3 %collective-permute-start.14 = (bf16[3,256,128]{2,1,0:T(8,128)(2,1)S(1)}, bf16[3,256,128]{2,1,0:T(8,128)(2,1)S(1)}, u32[]{:S(2)}, u32[]{:S(2)}) collective-permute-start(bf16[3,256,128]{2,1,0:T(8,128)(2,1)S(1)} %get-tuple-element.57), channel_id=1, source_target_pairs={{280,0},{281,1},{282,2},{283,3},{284,4},{285,5},{286,6},{287,7},{2... | collective-permute-start | bytes 589832 | tf_op jit(solution)/shard_map/ppermute | solution.py:309
  78.2 0.7 collective-permute-start.12
  78.9 2.7 %collective-permute-start.15 = (bf16[3,256,128]{2,1,0:T(8,128)(2,1)S(1)}, bf16[3,256,128]{2,1,0:T(8,128)(2,1)S(1)}, u32[]{:S(2)}, u32[]{:S(2)}) collective-permute-start(bf16[3,256,128]{2,1,0:T(8,128)(2,1)S(1)} %get-tuple-element.58), channel_id=1, source_target_pairs={{280,8},{281,9},{282,10},{283,11},{284,12},{285,13},{286,14},{287,... | collective-permute-start | bytes 589832 | tf_op jit(solution)/shard_map/ppermute | solution.py:309
  81.6 0.7 collective-permute-start.13
  82.3 0.1 collective-permute-done.16.came
  82.3 1.3 %shard_map.33 = (bf16[3,256,128]{2,1,0:T(8,128)(2,1)S(1)}, bf16[3,256,128]{2,1,0:T(8,128)(2,1)S(1)}, bf16[3,256,128]{2,1,0:T(8,128)(2,1)S(1)}, bf16[3,256,128]{2...) custom-call(s32[3]{0:T(128)S(1)} %pad_add_fusion.info, ...), custom_call_target="tpu_custom_call" | custom-call | bytes 4000000 | tf_op jit(solution)/shard_map/pallas_call | solution.py:51
  83.7 5.2 %collective-permute-start.21 = (bf16[3,256,128]{2,1,0:T(8,128)(2,1)S(1)}, bf16[3,256,128]{2,1,0:T(8,128)(2,1)S(1)}, u32[]{:S(2)}, u32[]{:S(2)}) collective-permute-start(bf16[3,256,128]{2,1,0:T(8,128)(2,1)S(1)} %get-tuple-element.65), channel_id=1, source_target_pairs={{256,8},{257,9},{258,10},{259,11},{260,12},{261,13},{262,14},{263,... | collective-permute-start | bytes 589832 | tf_op jit(solution)/shard_map/ppermute | solution.py:309
  88.9 1.3 %collective-permute-start.22 = (bf16[3,256,128]{2,1,0:T(8,128)(2,1)S(1)}, bf16[3,256,128]{2,1,0:T(8,128)(2,1)S(1)}, u32[]{:S(2)}, u32[]{:S(2)}) collective-permute-start(bf16[3,256,128]{2,1,0:T(8,128)(2,1)S(1)} %get-tuple-element.66), channel_id=1, source_target_pairs={{8,0},{9,1},{10,2},{11,3},{12,4},{13,5},{14,6},{15,7},{0,8},{1,9},... | collective-permute-start | bytes 589832 | tf_op jit(solution)/shard_map/ppermute | solution.py:309
  90.2 2.4 %collective-permute-start.19 = (bf16[3,256,128]{2,1,0:T(8,128)(2,1)S(1)}, bf16[3,256,128]{2,1,0:T(8,128)(2,1)S(1)}, u32[]{:S(2)}, u32[]{:S(2)}) collective-permute-start(bf16[3,256,128]{2,1,0:T(8,128)(2,1)S(1)} %get-tuple-element.63), channel_id=1, source_target_pairs={{280,256},{281,257},{282,258},{283,259},{284,260},{285,261},{286,2... | collective-permute-start | bytes 589832 | tf_op jit(solution)/shard_map/ppermute | solution.py:309
  92.6 1.3 %collective-permute-start.17 = (bf16[3,256,128]{2,1,0:T(8,128)(2,1)S(1)}, bf16[3,256,128]{2,1,0:T(8,128)(2,1)S(1)}, u32[]{:S(2)}, u32[]{:S(2)}) collective-permute-start(bf16[3,256,128]{2,1,0:T(8,128)(2,1)S(1)} %get-tuple-element.63), channel_id=1, source_target_pairs={{24,256},{25,257},{26,258},{27,259},{28,260},{29,261},{30,262},{31... | collective-permute-start | bytes 589832 | tf_op jit(solution)/shard_map/ppermute | solution.py:309
  93.9 0.0 collective-permute-done.13.a2
  94.0 5.7 %collective-permute-start.23 = (bf16[3,256,128]{2,1,0:T(8,128)(2,1)S(1)}, bf16[3,256,128]{2,1,0:T(8,128)(2,1)S(1)}, u32[]{:S(2)}, u32[]{:S(2)}) collective-permute-start(bf16[3,256,128]{2,1,0:T(8,128)(2,1)S(1)} %get-tuple-element.67), channel_id=1, source_target_pairs={{256,0},{257,1},{258,2},{259,3},{260,4},{261,5},{262,6},{263,7},{2... | collective-permute-start | bytes 589832 | tf_op jit(solution)/shard_map/ppermute | solution.py:309
  99.6 1.3 %collective-permute-start.20 = (bf16[3,256,128]{2,1,0:T(8,128)(2,1)S(1)}, bf16[3,256,128]{2,1,0:T(8,128)(2,1)S(1)}, u32[]{:S(2)}, u32[]{:S(2)}) collective-permute-start(bf16[3,256,128]{2,1,0:T(8,128)(2,1)S(1)} %get-tuple-element.64), channel_id=1, source_target_pairs={{280,264},{281,265},{282,266},{283,267},{284,268},{285,269},{286,2... | collective-permute-start | bytes 589832 | tf_op jit(solution)/shard_map/ppermute | solution.py:309
  100.9 1.3 %collective-permute-start.18 = (bf16[3,256,128]{2,1,0:T(8,128)(2,1)S(1)}, bf16[3,256,128]{2,1,0:T(8,128)(2,1)S(1)}, u32[]{:S(2)}, u32[]{:S(2)}) collective-permute-start(bf16[3,256,128]{2,1,0:T(8,128)(2,1)S(1)} %get-tuple-element.64), channel_id=1, source_target_pairs={{16,256},{17,257},{18,258},{19,259},{20,260},{21,261},{22,262},{23... | collective-permute-start | bytes 589832 | tf_op jit(solution)/shard_map/ppermute | solution.py:309
  102.3 0.0 collective-permute-done.19.d3
  102.3 1.1 collective-permute-done.17.c3
  103.3 1.4 %collective-permute-done.20.d2 = bf16[3,256,128]{2,1,0:T(8,128)(2,1)S(1)} collective-permute-done((bf16[3,256,128]{2,1,0:T(8,128)(2,1)S(1)}, bf16[3,256,128]{2,1,0:T(8,128)(2,1)S(1)}, u32[]{:S(2)}, u32[]{:S(2)}) %collective-permute-start.20) | collective-permute-done | bytes 196640 | tf_op jit(solution)/shard_map/ppermute | solution.py:309
  104.8 4.5 %collective-permute-done.18.c2 = bf16[3,256,128]{2,1,0:T(8,128)(2,1)S(1)} collective-permute-done((bf16[3,256,128]{2,1,0:T(8,128)(2,1)S(1)}, bf16[3,256,128]{2,1,0:T(8,128)(2,1)S(1)}, u32[]{:S(2)}, u32[]{:S(2)}) %collective-permute-start.18) | collective-permute-done | bytes 196640 | tf_op jit(solution)/shard_map/ppermute | solution.py:309
  109.2 1.8 %shard_map.34 = bf16[3,256,768]{2,1,0:T(8,128)(2,1)} custom-call(s32[3]{0:T(128)S(1)} %pad_add_fusion.info, bf16[3,256,128]{2,1,0:T(8,128)(2,1)S(1)} %collective-permute-done.12.a3, bf16[3,256,128]{2,1,0:T(8,128)(2,1)S(1)} %collective-permute-done.13.a2, bf16[3,256,128]{2,1,0:T(8,128)(2,1)S(1)} %collective-permute-done.14.b3, ...), custom_call_target="tpu_custom_call" | custom-call | bytes 4000000 | tf_op jit(solution)/shard_map/pallas_call | solution.py:51
  (8 shorter events, 0.0 us)
Async XLA Ops:
  2.4 18.4 %collective-permute-start.4 = (bf16[1024,128]{1,0:T(8,128)(2,1)S(1)}, bf16[1024,128]{1,0:T(8,128)(2,1)S(1)}, u32[]{:S(2)}, u32[]{:S(2)}) collective-permute-start(bf16[1024,128]{1,0:T(8,128)(2,1)S(1)} %get-tuple-element.41), channel_id=1, source_target_pairs={{256,24},{257,25},{258,26},{259,27},{260,28},{261,29},{262,30},{26... | collective-permute-start | bytes 786440 | tf_op jit(solution)/shard_map/ppermute | solution.py:309
  10.0 12.1 %collective-permute-start.5 = (bf16[1024,128]{1,0:T(8,128)(2,1)S(1)}, bf16[1024,128]{1,0:T(8,128)(2,1)S(1)}, u32[]{:S(2)}, u32[]{:S(2)}) collective-permute-start(bf16[1024,128]{1,0:T(8,128)(2,1)S(1)} %get-tuple-element.42), channel_id=1, source_target_pairs={{256,16},{257,17},{258,18},{259,19},{260,20},{261,21},{262,22},{26... | collective-permute-start | bytes 786440 | tf_op jit(solution)/shard_map/ppermute | solution.py:309
  11.3 17.8 %collective-permute-start.6 = (bf16[1024,128]{1,0:T(8,128)(2,1)S(1)}, bf16[1024,128]{1,0:T(8,128)(2,1)S(1)}, u32[]{:S(2)}, u32[]{:S(2)}) collective-permute-start(bf16[1024,128]{1,0:T(8,128)(2,1)S(1)} %get-tuple-element.43), channel_id=1, source_target_pairs={{256,280},{257,281},{258,282},{259,283},{260,284},{261,285},{262,2... | collective-permute-start | bytes 786440 | tf_op jit(solution)/shard_map/ppermute | solution.py:309
  17.5 11.8 %collective-permute-start.7 = (bf16[1024,128]{1,0:T(8,128)(2,1)S(1)}, bf16[1024,128]{1,0:T(8,128)(2,1)S(1)}, u32[]{:S(2)}, u32[]{:S(2)}) collective-permute-start(bf16[1024,128]{1,0:T(8,128)(2,1)S(1)} %get-tuple-element.44), channel_id=1, source_target_pairs={{264,280},{265,281},{266,282},{267,283},{268,284},{269,285},{270,2... | collective-permute-start | bytes 786440 | tf_op jit(solution)/shard_map/ppermute | solution.py:309
  18.8 16.2 %collective-permute-start.8 = (bf16[1024,128]{1,0:T(8,128)(2,1)S(1)}, bf16[1024,128]{1,0:T(8,128)(2,1)S(1)}, u32[]{:S(2)}, u32[]{:S(2)}) collective-permute-start(bf16[1024,128]{1,0:T(8,128)(2,1)S(1)} %get-tuple-element.45), channel_id=1, source_target_pairs={{8,256},{9,257},{10,258},{11,259},{12,260},{13,261},{14,262},{15,2... | collective-permute-start | bytes 786440 | tf_op jit(solution)/shard_map/ppermute | solution.py:309
  20.8 19.9 %collective-permute-start.9 = (bf16[1024,128]{1,0:T(8,128)(2,1)S(1)}, bf16[1024,128]{1,0:T(8,128)(2,1)S(1)}, u32[]{:S(2)}, u32[]{:S(2)}) collective-permute-start(bf16[1024,128]{1,0:T(8,128)(2,1)S(1)} %get-tuple-element.46), channel_id=1, source_target_pairs={{0,8},{1,9},{2,10},{3,11},{4,12},{5,13},{6,14},{7,15},{8,0},{9,1},... | collective-permute-start | bytes 786440 | tf_op jit(solution)/shard_map/ppermute | solution.py:309
  22.1 18.6 %collective-permute-start.10 = (bf16[1024,128]{1,0:T(8,128)(2,1)S(1)}, bf16[1024,128]{1,0:T(8,128)(2,1)S(1)}, u32[]{:S(2)}, u32[]{:S(2)}) collective-permute-start(bf16[1024,128]{1,0:T(8,128)(2,1)S(1)} %get-tuple-element.47), channel_id=1, source_target_pairs={{0,256},{1,257},{2,258},{3,259},{4,260},{5,261},{6,262},{7,263},{2... | collective-permute-start | bytes 786440 | tf_op jit(solution)/shard_map/ppermute | solution.py:309
  42.0 21.9 %collective-permute-start.11 = (bf16[4,512,128]{2,1,0:T(8,128)(2,1)S(1)}, bf16[4,512,128]{2,1,0:T(8,128)(2,1)S(1)}, u32[]{:S(2)}, u32[]{:S(2)}) collective-permute-start(bf16[4,512,128]{2,1,0:T(8,128)(2,1)S(1)} %get-tuple-element.55), channel_id=1, source_target_pairs={{0,1},{256,257},{1,0},{257,256},{2,3},{258,259},{3,2},{259,258},{4... | collective-permute-start | bytes 1572872 | tf_op jit(solution)/shard_map/ppermute | solution.py:309
  43.9 4.0 %collective-permute-start = (bf16[768,128]{1,0:T(8,128)(2,1)S(1)}, bf16[768,128]{1,0:T(8,128)(2,1)S(1)}, u32[]{:S(2)}, u32[]{:S(2)}) collective-permute-start(bf16[768,128]{1,0:T(8,128)(2,1)S(1)} %get-tuple-element.37), channel_id=1, source_target_pairs={{0,24},{1,25},{2,26},{3,27},{4,28},{5,29},{6,30},{7,31},{8,16},{9,... | collective-permute-start | bytes 589832 | tf_op jit(solution)/shard_map/ppermute | solution.py:309
  44.6 3.3 %collective-permute-start.1 = (bf16[768,128]{1,0:T(8,128)(2,1)S(1)}, bf16[768,128]{1,0:T(8,128)(2,1)S(1)}, u32[]{:S(2)}, u32[]{:S(2)}) collective-permute-start(bf16[768,128]{1,0:T(8,128)(2,1)S(1)} %get-tuple-element.38), channel_id=1, source_target_pairs={{0,16},{1,17},{2,18},{3,19},{4,20},{5,21},{6,22},{7,23},{8,24},{9,... | collective-permute-start | bytes 589832 | tf_op jit(solution)/shard_map/ppermute | solution.py:309
  45.3 12.4 %collective-permute-start.2 = (bf16[768,128]{1,0:T(8,128)(2,1)S(1)}, bf16[768,128]{1,0:T(8,128)(2,1)S(1)}, u32[]{:S(2)}, u32[]{:S(2)}) collective-permute-start(bf16[768,128]{1,0:T(8,128)(2,1)S(1)} %get-tuple-element.39), channel_id=1, source_target_pairs={{0,280},{1,281},{2,282},{3,283},{4,284},{5,285},{6,286},{7,287},{2... | collective-permute-start | bytes 589832 | tf_op jit(solution)/shard_map/ppermute | solution.py:309
  46.6 14.9 %collective-permute-start.3 = (bf16[768,128]{1,0:T(8,128)(2,1)S(1)}, bf16[768,128]{1,0:T(8,128)(2,1)S(1)}, u32[]{:S(2)}, u32[]{:S(2)}) collective-permute-start(bf16[768,128]{1,0:T(8,128)(2,1)S(1)} %get-tuple-element.40), channel_id=1, source_target_pairs={{8,280},{9,281},{10,282},{11,283},{12,284},{13,285},{14,286},{15,2... | collective-permute-start | bytes 589832 | tf_op jit(solution)/shard_map/ppermute | solution.py:309
  68.9 13.4 %collective-permute-start.16 = (bf16[3,512,128]{2,1,0:T(8,128)(2,1)S(1)}, bf16[3,512,128]{2,1,0:T(8,128)(2,1)S(1)}, u32[]{:S(2)}, u32[]{:S(2)}) collective-permute-start(bf16[3,512,128]{2,1,0:T(8,128)(2,1)S(1)} %get-tuple-element.60), channel_id=1, source_target_pairs={{0,1},{256,257},{1,0},{257,256},{2,3},{258,259},{3,2},{259,258},{4... | collective-permute-start | bytes 1179656 | tf_op jit(solution)/shard_map/ppermute | solution.py:309
  76.9 11.9 %collective-permute-start.14 = (bf16[3,256,128]{2,1,0:T(8,128)(2,1)S(1)}, bf16[3,256,128]{2,1,0:T(8,128)(2,1)S(1)}, u32[]{:S(2)}, u32[]{:S(2)}) collective-permute-start(bf16[3,256,128]{2,1,0:T(8,128)(2,1)S(1)} %get-tuple-element.57), channel_id=1, source_target_pairs={{280,0},{281,1},{282,2},{283,3},{284,4},{285,5},{286,6},{287,7},{2... | collective-permute-start | bytes 589832 | tf_op jit(solution)/shard_map/ppermute | solution.py:309
  78.2 11.9 %collective-permute-start.12 = (bf16[3,256,128]{2,1,0:T(8,128)(2,1)S(1)}, bf16[3,256,128]{2,1,0:T(8,128)(2,1)S(1)}, u32[]{:S(2)}, u32[]{:S(2)}) collective-permute-start(bf16[3,256,128]{2,1,0:T(8,128)(2,1)S(1)} %get-tuple-element.57), channel_id=1, source_target_pairs={{24,0},{25,1},{26,2},{27,3},{28,4},{29,5},{30,6},{31,7},{16,8},{17... | collective-permute-start | bytes 589832 | tf_op jit(solution)/shard_map/ppermute | solution.py:309
  78.9 13.7 %collective-permute-start.15 = (bf16[3,256,128]{2,1,0:T(8,128)(2,1)S(1)}, bf16[3,256,128]{2,1,0:T(8,128)(2,1)S(1)}, u32[]{:S(2)}, u32[]{:S(2)}) collective-permute-start(bf16[3,256,128]{2,1,0:T(8,128)(2,1)S(1)} %get-tuple-element.58), channel_id=1, source_target_pairs={{280,8},{281,9},{282,10},{283,11},{284,12},{285,13},{286,14},{287,... | collective-permute-start | bytes 589832 | tf_op jit(solution)/shard_map/ppermute | solution.py:309
  81.6 12.4 %collective-permute-start.13 = (bf16[3,256,128]{2,1,0:T(8,128)(2,1)S(1)}, bf16[3,256,128]{2,1,0:T(8,128)(2,1)S(1)}, u32[]{:S(2)}, u32[]{:S(2)}) collective-permute-start(bf16[3,256,128]{2,1,0:T(8,128)(2,1)S(1)} %get-tuple-element.58), channel_id=1, source_target_pairs={{16,0},{17,1},{18,2},{19,3},{20,4},{21,5},{22,6},{23,7},{24,8},{25... | collective-permute-start | bytes 589832 | tf_op jit(solution)/shard_map/ppermute | solution.py:309
  83.7 16.0 %collective-permute-start.21 = (bf16[3,256,128]{2,1,0:T(8,128)(2,1)S(1)}, bf16[3,256,128]{2,1,0:T(8,128)(2,1)S(1)}, u32[]{:S(2)}, u32[]{:S(2)}) collective-permute-start(bf16[3,256,128]{2,1,0:T(8,128)(2,1)S(1)} %get-tuple-element.65), channel_id=1, source_target_pairs={{256,8},{257,9},{258,10},{259,11},{260,12},{261,13},{262,14},{263,... | collective-permute-start | bytes 589832 | tf_op jit(solution)/shard_map/ppermute | solution.py:309
  88.9 12.1 %collective-permute-start.22 = (bf16[3,256,128]{2,1,0:T(8,128)(2,1)S(1)}, bf16[3,256,128]{2,1,0:T(8,128)(2,1)S(1)}, u32[]{:S(2)}, u32[]{:S(2)}) collective-permute-start(bf16[3,256,128]{2,1,0:T(8,128)(2,1)S(1)} %get-tuple-element.66), channel_id=1, source_target_pairs={{8,0},{9,1},{10,2},{11,3},{12,4},{13,5},{14,6},{15,7},{0,8},{1,9},... | collective-permute-start | bytes 589832 | tf_op jit(solution)/shard_map/ppermute | solution.py:309
  90.2 12.1 %collective-permute-start.19 = (bf16[3,256,128]{2,1,0:T(8,128)(2,1)S(1)}, bf16[3,256,128]{2,1,0:T(8,128)(2,1)S(1)}, u32[]{:S(2)}, u32[]{:S(2)}) collective-permute-start(bf16[3,256,128]{2,1,0:T(8,128)(2,1)S(1)} %get-tuple-element.63), channel_id=1, source_target_pairs={{280,256},{281,257},{282,258},{283,259},{284,260},{285,261},{286,2... | collective-permute-start | bytes 589832 | tf_op jit(solution)/shard_map/ppermute | solution.py:309
  92.6 10.7 %collective-permute-start.17 = (bf16[3,256,128]{2,1,0:T(8,128)(2,1)S(1)}, bf16[3,256,128]{2,1,0:T(8,128)(2,1)S(1)}, u32[]{:S(2)}, u32[]{:S(2)}) collective-permute-start(bf16[3,256,128]{2,1,0:T(8,128)(2,1)S(1)} %get-tuple-element.63), channel_id=1, source_target_pairs={{24,256},{25,257},{26,258},{27,259},{28,260},{29,261},{30,262},{31... | collective-permute-start | bytes 589832 | tf_op jit(solution)/shard_map/ppermute | solution.py:309
  94.0 8.3 %collective-permute-start.23 = (bf16[3,256,128]{2,1,0:T(8,128)(2,1)S(1)}, bf16[3,256,128]{2,1,0:T(8,128)(2,1)S(1)}, u32[]{:S(2)}, u32[]{:S(2)}) collective-permute-start(bf16[3,256,128]{2,1,0:T(8,128)(2,1)S(1)} %get-tuple-element.67), channel_id=1, source_target_pairs={{256,0},{257,1},{258,2},{259,3},{260,4},{261,5},{262,6},{263,7},{2... | collective-permute-start | bytes 589832 | tf_op jit(solution)/shard_map/ppermute | solution.py:309
  99.6 5.1 %collective-permute-start.20 = (bf16[3,256,128]{2,1,0:T(8,128)(2,1)S(1)}, bf16[3,256,128]{2,1,0:T(8,128)(2,1)S(1)}, u32[]{:S(2)}, u32[]{:S(2)}) collective-permute-start(bf16[3,256,128]{2,1,0:T(8,128)(2,1)S(1)} %get-tuple-element.64), channel_id=1, source_target_pairs={{280,264},{281,265},{282,266},{283,267},{284,268},{285,269},{286,2... | collective-permute-start | bytes 589832 | tf_op jit(solution)/shard_map/ppermute | solution.py:309
  100.9 8.3 %collective-permute-start.18 = (bf16[3,256,128]{2,1,0:T(8,128)(2,1)S(1)}, bf16[3,256,128]{2,1,0:T(8,128)(2,1)S(1)}, u32[]{:S(2)}, u32[]{:S(2)}) collective-permute-start(bf16[3,256,128]{2,1,0:T(8,128)(2,1)S(1)} %get-tuple-element.64), channel_id=1, source_target_pairs={{16,256},{17,257},{18,258},{19,259},{20,260},{21,261},{22,262},{23... | collective-permute-start | bytes 589832 | tf_op jit(solution)/shard_map/ppermute | solution.py:309

commit v3 on v2

v3 whole, which is shorter than its diff:
```python
import math

import jax
import jax.numpy as jnp
from jax import lax
from jax.experimental import pallas as pl
from jax.experimental.pallas import tpu as pltpu
from jax.sharding import PartitionSpec as P

HD = 128
BLK = 256
LEN = 1024
SCALE = 1.0 / math.sqrt(HD)
SCALE2 = SCALE * math.log2(math.e)
AXES = ("section", "dp", "tensor")
BF = jnp.bfloat16
F32 = jnp.float32
VM = pl.BlockSpec(memory_space=pltpu.VMEM)
SM = pl.BlockSpec(memory_space=pltpu.SMEM)
ANY = pl.BlockSpec(memory_space=pl.ANY)


def first_head(z):
    return 2 * z - jnp.where(z > 0, 1, 0)


def second_head(z):
    return jnp.where(z == 2, 4, 2)


def is_inner(z):
    return (z == 1) | (z == 2)


def head_cols(head):
    return pl.ds(pl.multiple_of(head * HD, HD), HD)


def rows_of(index, size):
    return pl.ds(pl.multiple_of(index * size, size), size)


def dot(a, b):
    return jnp.dot(a, b, preferred_element_type=F32)


def flip(x):
    return x.astype(F32).T.astype(BF)


def call(kernel, outs, args, scratch=(), flops=0, spec=VM, limit=48, after=()):
    first = len(args)

    def body(*refs):
        kernel(*refs[:first], *refs[first + len(after) :])

    return pl.pallas_call(
        body,
        out_shape=[jax.ShapeDtypeStruct(s, d) for s, d in outs],
        in_specs=[SM] + [spec] * (first - 1) + [ANY] * len(after),
        out_specs=[VM] * len(outs),
        scratch_shapes=list(scratch),
        compiler_params=pltpu.CompilerParams(vmem_limit_bytes=int(limit * 1024 * 1024)),
        cost_estimate=pl.CostEstimate(flops=flops, bytes_accessed=4000000, transcendentals=0),
    )(*args, *after)


CHUNK = 3 * BLK + HD


def selection(rows, cols, odd):
    row = lax.broadcasted_iota(jnp.int32, (rows, cols), 0)
    col = lax.broadcasted_iota(jnp.int32, (rows, cols), 1)
    return jnp.where(col == 2 * row + odd, 1.0, 0.0).astype(BF)


def fetch(local_hbm, grad_hbm, local, sems):
    copies = [pltpu.make_async_copy(local_hbm.at[j], local.at[j], sems.at[j]) for j in range(3)]
    copies += [pltpu.make_async_copy(grad_hbm, local.at[3], sems.at[3])]
    for copy in copies:
        copy.start()
    for copy in copies:
        copy.wait()


def fill_first(out, start, local, grad, head):
    cols = head_cols(head)
    for j in range(3):
        out[start + j * BLK : start + (j + 1) * BLK] = local[j, :, cols]
    out[start + 3 * BLK : start + CHUNK] = grad[:, cols]


def pick_far_kernel(info, local_hbm, grad_hbm, away, a3, a2, b3, b2, local, sems, grad):
    z, h, s = info[0], info[1], info[2]
    fetch(local_hbm, grad_hbm, local, sems)

    @pl.when(s == 0)
    def _():
        grad[...] = dot(selection(128, 256, h), local[3]).astype(BF)
        fill_first(a3, 0, local, grad, first_head(z ^ 3))
        fill_first(a2, 0, local, grad, first_head(z ^ 2))
        fill_first(b3, 0, local, grad, second_head(z ^ 3))
        fill_first(b2, 0, local, grad, second_head(z ^ 2))

    @pl.when(s == 1)
    def _():
        for j in range(4):
            away[j] = dot(selection(128, 256, 1 - h), local[j]).astype(BF)


def pick_near_kernel(info, local_hbm, grad_hbm, stash, local, sems, grad):
    z, h, s = info[0], info[1], info[2]
    fetch(local_hbm, grad_hbm, local, sems)

    @pl.when(s == 0)
    def _():
        grad[...] = dot(selection(128, 256, h), local[3]).astype(BF)
        for k in range(2):
            fill_first(stash, k * CHUNK, local, grad, second_head(z ^ k))
            fill_first(stash, (2 + k) * CHUNK, local, grad, first_head(z ^ k))

    @pl.when(s == 1)
    def _():
        for j in range(3):
            own = dot(selection(128, 256, h), local[j]).astype(BF)
            for head in range(6):
                start = (head * 3 + j) * HD
                stash[start : start + HD] = own[:, head * HD : (head + 1) * HD]


def pick_second_kernel(info, stash, came, *outs):
    z, h, s = info[0], info[1], info[2]

    def fill(out, head):
        cols = head_cols(head)
        for j in range(3):
            mine = pl.ds(pl.multiple_of(j * BLK + h * HD, HD), HD)
            theirs = pl.ds(pl.multiple_of(j * BLK + (1 - h) * HD, HD), HD)
            out[mine, :] = stash[rows_of(head * 3 + j, HD), :]
            out[theirs, :] = came[j, :, cols]
        out[3 * BLK :] = came[3, :, cols]

    @pl.when(s == 0)
    def _():
        for k in range(4):
            outs[k][...] = stash[k * CHUNK : (k + 1) * CHUNK]

    @pl.when(s == 1)
    def _():
        for k in range(2):
            fill(outs[k], first_head(z ^ k))
            fill(outs[2 + k], second_head(z ^ k))
            fill(outs[4 + k], first_head(z ^ (2 + k)))
            fill(outs[6 + k], second_head(z ^ (2 + k)))


def score_block(keys, qt, i):
    n = (i + 1) * BLK
    st = dot(keys[0:n], qt[:, i * BLK : n]) * SCALE2
    key = lax.broadcasted_iota(jnp.int32, (BLK, BLK), 0)
    qry = lax.broadcasted_iota(jnp.int32, (BLK, BLK), 1)
    tail = jnp.where(key <= qry, st[n - BLK :], -jnp.inf)
    return tail if i == 0 else jnp.concatenate([st[: n - BLK], tail], axis=0)


def backward_block(i, p, keys_t, values, q, g, gt, delta, dqt, dk, dv):
    n = (i + 1) * BLK
    cols = slice(i * BLK, n)
    dp = dot(values[0:n], gt[:, cols])
    ds = (p * (dp - delta)).astype(BF)
    dqt[:, cols] = (dot(keys_t[:, 0:n], ds) * SCALE).astype(BF)
    add_k = dot(ds, q[cols])
    add_v = dot(p.astype(BF), g[cols])
    if i > 0:
        dk[0 : n - BLK] += add_k[: n - BLK]
        dv[0 : n - BLK] += add_v[: n - BLK]
    dk[n - BLK : n] = add_k[n - BLK :]
    dv[n - BLK : n] = add_v[n - BLK :]


def hand_out(info, outs, dq, dk, dv):
    z = info[0]
    for k in range(4):
        rows = rows_of(z ^ k, BLK)
        outs[k][0] = dq[rows]
        outs[k][1] = (dk[rows] * SCALE).astype(BF)
        outs[k][2] = dv[rows].astype(BF)


def backward_block(i, p, keys_t, values, q, g, gt, delta, dqt, dk, dv):
    n = (i + 1) * BLK
    cols = slice(i * BLK, n)
    dp = dot(values[0:n], gt[:, cols])
    ds = (p * (dp - delta)).astype(BF)
    dqt[:, cols] = (dot(keys_t[:, 0:n], ds) * SCALE).astype(BF)
    add_k = dot(ds, q[cols])
    add_v = dot(p.astype(BF), g[cols])
    if i > 0:
        dk[0 : n - BLK] += add_k[: n - BLK]
        dv[0 : n - BLK] += add_v[: n - BLK]
    dk[n - BLK : n] = add_k[n - BLK :]
    dv[n - BLK : n] = add_v[n - BLK :]


def main_kernel(info, *refs):
    a3, a2, b3, b2, x3, x0, x1, same1, x2, d3, d2, here = refs[0:12]
    keep, give, out0, out1, to_a3, to_a2, to_b3, to_b2 = refs[12:20]
    qkv, qkvg, ot1, g1, qt, kt, vt, gt, p1, dq, dk, dv = refs[20:]
    z, h, s = info[0], info[1], info[2]

    def join(first, second):
        for k in range(4):
            rows = rows_of(z ^ k, BLK)
            for j in range(3):
                qkv[j, rows, :] = first[k][j * BLK : (j + 1) * BLK]
                qkvg[j, rows, :] = second[k][j * BLK : (j + 1) * BLK]
            for part, chunk in ((h, first[k]), (1 - h, second[k])):
                at = pl.ds(pl.multiple_of((z ^ k) * BLK + part * HD, HD), HD)
                qkvg[3, at, :] = chunk[3 * BLK :]

    @pl.when(s == 0)
    def _():
        join((here, same1, a2, a3), (x0, x1, x2, x3))

    @pl.when(s == 1)
    def _():
        join((x0, x1, b2, b3), (here, same1, d2, d3))

    qt[...] = flip(qkv[0])
    vt[...] = flip(qkv[2])
    keys = qkv.at[1]
    for i in range(4):
        n = (i + 1) * BLK
        cols = slice(i * BLK, n)
        st = score_block(keys, qt, i)
        top = jnp.max(st, axis=0, keepdims=True)
        p = jnp.exp2(st - top)
        p = p * (1.0 / jnp.sum(p, axis=0, keepdims=True))
        p1[0:n, cols] = p
        ot1[:, cols] = dot(vt[:, 0:n], p.astype(BF)).astype(BF)

    q = qkvg[0].astype(F32) + ot1[...].astype(F32).T
    qkvg[0] = q.astype(BF)
    qt[...] = q.T.astype(BF)
    kt[...] = flip(qkvg[1])
    vt[...] = flip(qkvg[2])
    gt[...] = flip(qkvg[3])
    keys, values = qkvg.at[1], qkvg.at[2]
    for i in range(4):
        n = (i + 1) * BLK
        cols = slice(i * BLK, n)
        st = score_block(keys, qt, i)
        top = jnp.max(st, axis=0, keepdims=True)
        p = jnp.exp2(st - top)
        p = p * (1.0 / jnp.sum(p, axis=0, keepdims=True))
        o = dot(vt[:, 0:n], p.astype(BF)).astype(BF)
        delta = jnp.sum(gt[:, cols].astype(F32) * o.astype(F32), axis=0, keepdims=True)
        backward_block(i, p, kt, values, qkvg.at[0], qkvg.at[3], gt, delta, g1, dk, dv)
    dq[...] = flip(g1[...])

    def block(b, part):
        return pl.ds(pl.multiple_of(b * BLK + part * HD, HD), HD)

    for b in range(4):
        rows = slice(b * HD, (b + 1) * HD)
        for out, part in ((keep, h), (give, 1 - h)):
            out[0, rows] = dq[block(b, part)]
            out[1, rows] = (dk[block(b, part)] * SCALE).astype(BF)
            out[2, rows] = dv[block(b, part)].astype(BF)

    kt[...] = flip(qkv[1])
    values = qkv.at[2]
    for i in range(4):
        cols = slice(i * BLK, (i + 1) * BLK)
        p = p1[0 : (i + 1) * BLK, cols]
        delta = jnp.sum(g1[:, cols].astype(F32) * ot1[:, cols].astype(F32), axis=0, keepdims=True)
        backward_block(i, p, kt, values, qkv.at[0], dq, g1, delta, gt, dk, dv)
    dq[...] = flip(gt[...])

    def hand_out(outs):
        for k, out in enumerate(outs):
            rows = rows_of(z ^ k, BLK)
            out[0] = dq[rows]
            out[1] = (dk[rows] * SCALE).astype(BF)
            out[2] = dv[rows].astype(BF)

    @pl.when(s == 0)
    def _():
        hand_out((out0, out1, to_a2, to_a3))

    @pl.when(s == 1)
    def _():
        hand_out((out0, out1, to_b2, to_b3))


def weave_kernel(info, keep, came, d0, d1, x3, x2, c3, c2, x1, same1, x0, here):
    z, h, s = info[0], info[1], info[2]
    row = lax.broadcasted_iota(jnp.int32, (256, 256), 0)
    col = lax.broadcasted_iota(jnp.int32, (256, 256), 1)
    wanted = jnp.where(col < HD, 2 * col + h, 2 * (col - HD) + 1 - h)
    put = jnp.where(row == wanted, 1.0, 0.0).astype(BF)

    def weave(out, k):
        rows = rows_of(z ^ k, HD)
        for j in range(3):
            both = jnp.concatenate([keep[j, rows, :], came[j, rows, :]], axis=0)
            out[j] = dot(put, both).astype(BF)

    @pl.when(s == 0)
    def _():
        here[...] = d0[...]
        same1[...] = d1[...]
        for k, out in enumerate((x0, x1, x2, x3)):
            weave(out, k)

    @pl.when(s == 1)
    def _():
        x0[...] = d0[...]
        x1[...] = d1[...]
        for k, out in enumerate((here, same1, c2, c3)):
            weave(out, k)


def finish_kernel(info, *refs):
    a3, a2, b3, b2, x3, x0, x1, same1, x2, c3, c2, here, out = refs
    z, s = info[0], info[2]

    def place(slot_a, slot_b):
        for k in range(4):
            out[:, :, head_cols(first_head(z ^ k))] = slot_a[k][...]

            @pl.when(is_inner(z ^ k))
            def _(k=k):
                out[:, :, head_cols(second_head(z ^ k))] = slot_b[k][...]

    @pl.when(s == 0)
    def _():
        place((here, same1, a2, a3), (x0, x1, b2, b3))

    @pl.when(s == 1)
    def _():
        place((x0, x1, x2, x3), (here, same1, c2, c3))


def build(n_dp, n_tensor):
    def index(s, d, t):
        return (s * n_dp + d) * n_tensor + t

    def everywhere(rule):
        pairs = []
        for d in range(n_dp):
            for t in range(n_tensor):
                pairs += rule(d, t)
        return pairs

    def send(value, pairs):
        return lax.ppermute(value, AXES, pairs)

    def inward(src, slot, k):
        return everywhere(
            lambda d, t: [(index(src, d, t), index(slot, d ^ k, t))]
            if slot == 0 or (d ^ k) % 4 in (1, 2)
            else []
        )

    def outward(dst, slot, k):
        return [(b, a) for a, b in inward(dst, slot, k)]

    def swap_lines(value, cores):
        return send(
            value,
            everywhere(
                lambda d, t: [
                    (index(c, d, t), index(c, d, t ^ 1))
                    for c in cores
                    if c == 1 and len(cores) == 1 or c == 0 or d % 4 in (1, 2)
                ]
            ),
        )

    def body(projections, out_grad):
        s = lax.axis_index("section")
        z = lax.axis_index("dp") % 4
        h = lax.axis_index("tensor") % 2
        info = jnp.stack([z, h, s]).astype(jnp.int32)
        local = projections[0]
        rows, cols = local.shape[1:]
        half = ((4, rows // 2, cols), BF)
        chunk_in = ((CHUNK, HD), BF)
        chunk = ((3, BLK, HD), BF)
        vm = pltpu.VMEM
        tall, wide = vm((LEN, HD), BF), vm((HD, LEN), BF)
        acc = vm((LEN, HD), F32)

        inputs = [info] + [
            pltpu.with_memory_space_constraint(x, pltpu.HBM) for x in (local, out_grad)
        ]
        hbm = pl.BlockSpec(memory_space=pltpu.HBM)
        staging = [vm((4, rows, cols), BF), pltpu.SemaphoreType.DMA((4,)), vm((HD, cols), BF)]
        away, a3, a2, b3, b2 = call(
            pick_far_kernel, [half] + [chunk_in] * 4, inputs, staging, spec=hbm
        )
        came = swap_lines(away, (1,))
        a3 = send(a3, inward(0, 0, 3))
        a2 = send(a2, inward(0, 0, 2))
        b3 = send(b3, inward(0, 1, 3))
        b2 = send(b2, inward(0, 1, 2))
        (stash,) = call(
            pick_near_kernel, [((4 * CHUNK, HD), BF)], inputs, staging, 0, hbm
        )
        x0, x1, here, same1, x2, x3, d2, d3 = call(
            pick_second_kernel, [chunk_in] * 8, [info, stash, came]
        )
        x3 = send(x3, inward(1, 0, 3))
        x2 = send(x2, inward(1, 0, 2))
        d3 = send(d3, inward(1, 1, 3))
        d2 = send(d2, inward(1, 1, 2))
        x1 = send(x1, inward(0, 1, 1) + inward(1, 0, 1))
        same1 = send(same1, inward(0, 0, 1) + inward(1, 1, 1))
        x0 = send(x0, inward(0, 1, 0) + inward(1, 0, 0))
        keep, give, d0, d1, a3, a2, b3, b2 = call(
            main_kernel,
            [((3, 4 * HD, HD), BF)] * 2 + [chunk] * 6,
            [info, a3, a2, b3, b2, x3, x0, x1, same1, x2, d3, d2, here],
            [vm((3, LEN, HD), BF), vm((4, LEN, HD), BF)]
            + [wide] * 6
            + [vm((LEN, LEN), F32), tall, acc, acc],
        )
        came = swap_lines(give, (0, 1))
        a3 = send(a3, outward(0, 0, 3))
        a2 = send(a2, outward(0, 0, 2))
        b3 = send(b3, outward(0, 1, 3))
        b2 = send(b2, outward(0, 1, 2))
        x3, x2, c3, c2, x1, same1, x0, here = call(
            weave_kernel, [chunk] * 8, [info, keep, came, d0, d1]
        )
        x3 = send(x3, outward(1, 0, 3))
        x2 = send(x2, outward(1, 0, 2))
        c3 = send(c3, outward(1, 1, 3))
        c2 = send(c2, outward(1, 1, 2))
        x1 = send(x1, outward(0, 1, 1) + outward(1, 0, 1))
        same1 = send(same1, outward(0, 0, 1) + outward(1, 1, 1))
        x0 = send(x0, outward(0, 1, 0) + outward(1, 0, 0))
        (out,) = call(
            finish_kernel,
            [((3, rows, cols), BF)],
            [info, a3, a2, b3, b2, x3, x0, x1, same1, x2, c3, c2, here],
        )
        return out[None]

    return body


def solution(mesh):
    body = build(mesh.shape["dp"], mesh.shape["tensor"])
    in_specs = (P("section", None, "dp", "tensor"), P("dp", "tensor"))
    out_specs = P("section", None, "dp", "tensor")
    return jax.shard_map(body, mesh=mesh, in_specs=in_specs, out_specs=out_specs, check_vma=False)
```

time: 112 us -> 95 us (0.85)
  starting transfers between devices: 61.5 us -> 45.8 us
  waiting for transfers between devices: 32.2 us -> 30.9 us
    ppermute x24, starting transfers between devices: 61.5 us -> 45.8 us  [send(): return lax.ppermute(value, AXES, pairs)]
    ppermute x24, waiting for transfers between devices: 32.2 us -> 30.9 us  [send(): return lax.ppermute(value, AXES, pairs)]
    pallas_call x7 -> x6, Pallas kernels: 16.9 us -> 17.3 us  [call(): pl.pallas_call(body, out_shape=[jax.ShapeDtypeStruct(s, d) for s, d in ou...]
  transfers between devices with their start and end apart: 24 -> 24, of which waited for: 9 -> 7; matrix products, arithmetic and copies ran while one was open for 0% -> 0% of each run, Pallas kernels for 6% -> 4%
where the time goes in v3:
time: 95 us; the launch traced here: 94.4 us
  starting transfers between devices  45.8 us (48%)
  waiting for transfers between devices  30.9 us (33%)
  Pallas kernels  17.3 us (18%)
    ppermute x24, starting transfers between devices, send(): return lax.ppermute(value, AXES, pairs)  45.8 us
    ppermute x24, waiting for transfers between devices, send(): return lax.ppermute(value, AXES, pairs)  30.9 us
    pallas_call x6, Pallas kernels, call(): pl.pallas_call(body, out_shape=[jax.ShapeDtypeStruct(s, d) for s, d in ou...  17.3 us
  transfers between devices with their start and end apart: 24, of which 7 were waited for; matrix products, arithmetic and copies ran while one was open for 0% of the time, Pallas kernels for 4%

profile of v3, /device:TPU:1, one launch (start us, length us, event | category | flops | bytes accessed | tf_op | source)
XLA Modules:
  0.0 94.4 jit_solution(11098828815662480905)
XLA Ops:
  0.0 0.1 pad_add_fusion.refs_0_
  0.1 2.3 %shard_map.28 = (bf16[4,128,768]{2,1,0:T(8,128)(2,1)S(1)}, bf16[896,128]{1,0:T(8,128)(2,1)S(1)}, bf16[896,128]{1,0:T(8,128)(2,1)S(1)}, bf16[896,128]{1,0:T(8,128)(2,1)S(1)}, bf16[896,128]{1,0:T(8,128)(2,1)S(1)}) custom-call(s32[3]{0:T(128)S(1)} %pad_add_fusion.refs_0_, bf16[3,256,768]{2,1,0:T(8,128)(2,1)} %bitcast.5, bf16[256,768]{1,0:T(8,128)(2,1)} %refs_2_.3), custom_call_target="tpu_custom_call" | custom-call | bytes 4000000 | tf_op jit(solution)/shard_map/pallas_call | solution.py:57
  2.4 5.5 %collective-permute-start.4 = (bf16[4,128,768]{2,1,0:T(8,128)(2,1)S(1)}, bf16[4,128,768]{2,1,0:T(8,128)(2,1)S(1)}, u32[]{:S(2)}, u32[]{:S(2)}) collective-permute-start(bf16[4,128,768]{2,1,0:T(8,128)(2,1)S(1)} %get-tuple-element.38), channel_id=1, source_target_pairs={{256,257},{257,256},{258,259},{259,258},{260,261},{261,260},{262,2... | collective-permute-start | bytes 2359304 | tf_op jit(solution)/shard_map/ppermute | solution.py:357
  7.9 0.7 collective-permute-start
  8.6 0.7 collective-permute-start.1
  9.2 0.7 collective-permute-start.2
  9.9 0.7 collective-permute-start.3
  10.6 2.3 %shard_map.29.refs_1_ = bf16[3584,128]{1,0:T(8,128)(2,1)S(1)} custom-call(s32[3]{0:T(128)S(1)} %pad_add_fusion.refs_0_, bf16[3,256,768]{2,1,0:T(8,128)(2,1)} %bitcast.6, bf16[256,768]{1,0:T(8,128)(2,1)} %refs_2_.3), custom_call_target="tpu_custom_call" | custom-call | bytes 4000000 | tf_op jit(solution)/shard_map/pallas_call | solution.py:57
  12.9 4.5 %collective-permute-done.4.refs_2_ = bf16[4,128,768]{2,1,0:T(8,128)(2,1)S(1)} collective-permute-done((bf16[4,128,768]{2,1,0:T(8,128)(2,1)S(1)}, bf16[4,128,768]{2,1,0:T(8,128)(2,1)S(1)}, u32[]{:S(2)}, u32[]{:S(2)}) %collective-permute-start.4) | collective-permute-done | bytes 786464 | tf_op jit(solution)/shard_map/ppermute | solution.py:357
  17.4 0.8 shard_map.30
  18.2 5.7 %collective-permute-start.5 = (bf16[896,128]{1,0:T(8,128)(2,1)S(1)}, bf16[896,128]{1,0:T(8,128)(2,1)S(1)}, u32[]{:S(2)}, u32[]{:S(2)}) collective-permute-start(bf16[896,128]{1,0:T(8,128)(2,1)S(1)} %get-tuple-element.39), channel_id=1, source_target_pairs={{256,24},{257,25},{258,26},{259,27},{260,28},{261,29},{262,30},{26... | collective-permute-start | bytes 688136 | tf_op jit(solution)/shard_map/ppermute | solution.py:357
  23.9 0.0 collective-permute-done.refs_1_
  23.9 1.3 %collective-permute-start.6 = (bf16[896,128]{1,0:T(8,128)(2,1)S(1)}, bf16[896,128]{1,0:T(8,128)(2,1)S(1)}, u32[]{:S(2)}, u32[]{:S(2)}) collective-permute-start(bf16[896,128]{1,0:T(8,128)(2,1)S(1)} %get-tuple-element.40), channel_id=1, source_target_pairs={{8,264},{9,265},{10,266},{11,267},{12,268},{13,269},{14,270},{15,2... | collective-permute-start | bytes 688136 | tf_op jit(solution)/shard_map/ppermute | solution.py:357
  25.2 2.5 %collective-permute-start.7 = (bf16[896,128]{1,0:T(8,128)(2,1)S(1)}, bf16[896,128]{1,0:T(8,128)(2,1)S(1)}, u32[]{:S(2)}, u32[]{:S(2)}) collective-permute-start(bf16[896,128]{1,0:T(8,128)(2,1)S(1)} %get-tuple-element.41), channel_id=1, source_target_pairs={{0,264},{1,265},{2,266},{3,267},{4,268},{5,269},{6,270},{7,271},{2... | collective-permute-start | bytes 688136 | tf_op jit(solution)/shard_map/ppermute | solution.py:357
  27.7 0.0 collective-permute-done.2.refs_3_
  27.7 8.1 %collective-permute-start.8 = (bf16[896,128]{1,0:T(8,128)(2,1)S(1)}, bf16[896,128]{1,0:T(8,128)(2,1)S(1)}, u32[]{:S(2)}, u32[]{:S(2)}) collective-permute-start(bf16[896,128]{1,0:T(8,128)(2,1)S(1)} %get-tuple-element.42), channel_id=1, source_target_pairs={{0,8},{1,9},{2,10},{3,11},{4,12},{5,13},{6,14},{7,15},{8,0},{9,1},... | collective-permute-start | bytes 688136 | tf_op jit(solution)/shard_map/ppermute | solution.py:357
  35.9 1.5 %collective-permute-start.9 = (bf16[896,128]{1,0:T(8,128)(2,1)S(1)}, bf16[896,128]{1,0:T(8,128)(2,1)S(1)}, u32[]{:S(2)}, u32[]{:S(2)}) collective-permute-start(bf16[896,128]{1,0:T(8,128)(2,1)S(1)} %get-tuple-element.43), channel_id=1, source_target_pairs={{256,16},{257,17},{258,18},{259,19},{260,20},{261,21},{262,22},{26... | collective-permute-start | bytes 688136 | tf_op jit(solution)/shard_map/ppermute | solution.py:357
  37.3 0.7 collective-permute-start.10
  38.0 0.0 collective-permute-done.6.refs_6_
  38.0 6.1 %collective-permute-start.11 = (bf16[896,128]{1,0:T(8,128)(2,1)S(1)}, bf16[896,128]{1,0:T(8,128)(2,1)S(1)}, u32[]{:S(2)}, u32[]{:S(2)}) collective-permute-start(bf16[896,128]{1,0:T(8,128)(2,1)S(1)} %get-tuple-element.45), channel_id=1, source_target_pairs={{256,272},{257,273},{258,274},{259,275},{260,276},{261,277},{262,2... | collective-permute-start | bytes 688136 | tf_op jit(solution)/shard_map/ppermute | solution.py:357
  44.1 0.0 collective-permute-done.7.refs_7_
  44.1 0.0 collective-permute-done.10.refs_10_
  44.2 2.9 %collective-permute-done.11.refs_11_ = bf16[896,128]{1,0:T(8,128)(2,1)S(1)} collective-permute-done((bf16[896,128]{1,0:T(8,128)(2,1)S(1)}, bf16[896,128]{1,0:T(8,128)(2,1)S(1)}, u32[]{:S(2)}, u32[]{:S(2)}) %collective-permute-start.11) | collective-permute-done | bytes 229408 | tf_op jit(solution)/shard_map/ppermute | solution.py:357
  47.1 8.9 %shard_map.31 = (bf16[3,512,128]{2,1,0:T(8,128)(2,1)S(1)}, bf16[3,512,128]{2,1,0:T(8,128)(2,1)S(1)}, bf16[3,256,128]{2,1,0:T(8,128)(2,1)S(1)}, bf16[3,256,128]{2...) custom-call(s32[3]{0:T(128)S(1)} %pad_add_fusion.refs_0_, ...), custom_call_target="tpu_custom_call" | custom-call | bytes 4000000 | tf_op jit(solution)/shard_map/pallas_call | solution.py:57
  56.1 0.7 collective-permute-start.16
  56.7 0.7 collective-permute-start.12
  57.4 0.7 collective-permute-start.13
  58.1 0.7 collective-permute-start.14
  58.8 0.7 collective-permute-start.15
  59.5 1.2 %shard_map.32 = (bf16[3,256,128]{2,1,0:T(8,128)(2,1)S(1)}, bf16[3,256,128]{2,1,0:T(8,128)(2,1)S(1)}, bf16[3,256,128]{2,1,0:T(8,128)(2,1)S(1)}, bf16[3,256,128]{2...) custom-call(s32[3]{0:T(128)S(1)} %pad_add_fusion.refs_0_, ...), custom_call_target="tpu_custom_call" | custom-call | bytes 4000000 | tf_op jit(solution)/shard_map/pallas_call | solution.py:57
  60.6 1.3 %collective-permute-start.17 = (bf16[3,256,128]{2,1,0:T(8,128)(2,1)S(1)}, bf16[3,256,128]{2,1,0:T(8,128)(2,1)S(1)}, u32[]{:S(2)}, u32[]{:S(2)}) collective-permute-start(bf16[3,256,128]{2,1,0:T(8,128)(2,1)S(1)} %get-tuple-element.55), channel_id=1, source_target_pairs={{24,256},{25,257},{26,258},{27,259},{28,260},{29,261},{30,262},{31... | collective-permute-start | bytes 589832 | tf_op jit(solution)/shard_map/ppermute | solution.py:357
  61.9 0.0 collective-permute-done.12.refs_1_
  62.0 1.3 %collective-permute-start.18 = (bf16[3,256,128]{2,1,0:T(8,128)(2,1)S(1)}, bf16[3,256,128]{2,1,0:T(8,128)(2,1)S(1)}, u32[]{:S(2)}, u32[]{:S(2)}) collective-permute-start(bf16[3,256,128]{2,1,0:T(8,128)(2,1)S(1)} %get-tuple-element.56), channel_id=1, source_target_pairs={{264,8},{265,9},{266,10},{267,11},{268,12},{269,13},{270,14},{271,... | collective-permute-start | bytes 589832 | tf_op jit(solution)/shard_map/ppermute | solution.py:357
  63.3 1.3 %collective-permute-start.19 = (bf16[3,256,128]{2,1,0:T(8,128)(2,1)S(1)}, bf16[3,256,128]{2,1,0:T(8,128)(2,1)S(1)}, u32[]{:S(2)}, u32[]{:S(2)}) collective-permute-start(bf16[3,256,128]{2,1,0:T(8,128)(2,1)S(1)} %get-tuple-element.57), channel_id=1, source_target_pairs={{264,0},{265,1},{266,2},{267,3},{268,4},{269,5},{270,6},{271,7},{2... | collective-permute-start | bytes 589832 | tf_op jit(solution)/shard_map/ppermute | solution.py:357
  64.6 0.0 collective-permute-done.14.refs_3_
  64.6 1.3 %collective-permute-start.20 = (bf16[3,256,128]{2,1,0:T(8,128)(2,1)S(1)}, bf16[3,256,128]{2,1,0:T(8,128)(2,1)S(1)}, u32[]{:S(2)}, u32[]{:S(2)}) collective-permute-start(bf16[3,256,128]{2,1,0:T(8,128)(2,1)S(1)} %get-tuple-element.58), channel_id=1, source_target_pairs={{8,0},{9,1},{10,2},{11,3},{12,4},{13,5},{14,6},{15,7},{0,8},{1,9},... | collective-permute-start | bytes 589832 | tf_op jit(solution)/shard_map/ppermute | solution.py:357
  65.9 0.0 collective-permute-done.15.refs_4_
  65.9 1.3 %collective-permute-start.21 = (bf16[3,256,128]{2,1,0:T(8,128)(2,1)S(1)}, bf16[3,256,128]{2,1,0:T(8,128)(2,1)S(1)}, u32[]{:S(2)}, u32[]{:S(2)}) collective-permute-start(bf16[3,256,128]{2,1,0:T(8,128)(2,1)S(1)} %get-tuple-element.59), channel_id=1, source_target_pairs={{16,256},{17,257},{18,258},{19,259},{20,260},{21,261},{22,262},{23... | collective-permute-start | bytes 589832 | tf_op jit(solution)/shard_map/ppermute | solution.py:357
  67.2 6.4 %collective-permute-done.17.refs_5_ = bf16[3,256,128]{2,1,0:T(8,128)(2,1)S(1)} collective-permute-done((bf16[3,256,128]{2,1,0:T(8,128)(2,1)S(1)}, bf16[3,256,128]{2,1,0:T(8,128)(2,1)S(1)}, u32[]{:S(2)}, u32[]{:S(2)}) %collective-permute-start.17) | collective-permute-done | bytes 196640 | tf_op jit(solution)/shard_map/ppermute | solution.py:357
  73.6 0.7 collective-permute-start.22
  74.3 0.0 collective-permute-done.18.refs_6_
  74.3 1.3 %collective-permute-start.23 = (bf16[3,256,128]{2,1,0:T(8,128)(2,1)S(1)}, bf16[3,256,128]{2,1,0:T(8,128)(2,1)S(1)}, u32[]{:S(2)}, u32[]{:S(2)}) collective-permute-start(bf16[3,256,128]{2,1,0:T(8,128)(2,1)S(1)} %get-tuple-element.61), channel_id=1, source_target_pairs={{272,256},{273,257},{274,258},{275,259},{276,260},{277,261},{278,2... | collective-permute-start | bytes 589832 | tf_op jit(solution)/shard_map/ppermute | solution.py:357
  75.6 7.0 %collective-permute-done.19.refs_7_ = bf16[3,256,128]{2,1,0:T(8,128)(2,1)S(1)} collective-permute-done((bf16[3,256,128]{2,1,0:T(8,128)(2,1)S(1)}, bf16[3,256,128]{2,1,0:T(8,128)(2,1)S(1)}, u32[]{:S(2)}, u32[]{:S(2)}) %collective-permute-start.19) | collective-permute-done | bytes 196640 | tf_op jit(solution)/shard_map/ppermute | solution.py:357
  82.6 4.6 %collective-permute-done.20.refs_8_ = bf16[3,256,128]{2,1,0:T(8,128)(2,1)S(1)} collective-permute-done((bf16[3,256,128]{2,1,0:T(8,128)(2,1)S(1)}, bf16[3,256,128]{2,1,0:T(8,128)(2,1)S(1)}, u32[]{:S(2)}, u32[]{:S(2)}) %collective-permute-start.20) | collective-permute-done | bytes 196640 | tf_op jit(solution)/shard_map/ppermute | solution.py:357
  87.2 3.0 %collective-permute-done.21.refs_9_ = bf16[3,256,128]{2,1,0:T(8,128)(2,1)S(1)} collective-permute-done((bf16[3,256,128]{2,1,0:T(8,128)(2,1)S(1)}, bf16[3,256,128]{2,1,0:T(8,128)(2,1)S(1)}, u32[]{:S(2)}, u32[]{:S(2)}) %collective-permute-start.21) | collective-permute-done | bytes 196640 | tf_op jit(solution)/shard_map/ppermute | solution.py:357
  90.2 0.0 collective-permute-done.22.refs_10_
  90.2 2.4 %collective-permute-done.23.refs_11_ = bf16[3,256,128]{2,1,0:T(8,128)(2,1)S(1)} collective-permute-done((bf16[3,256,128]{2,1,0:T(8,128)(2,1)S(1)}, bf16[3,256,128]{2,1,0:T(8,128)(2,1)S(1)}, u32[]{:S(2)}, u32[]{:S(2)}) %collective-permute-start.23) | collective-permute-done | bytes 196640 | tf_op jit(solution)/shard_map/ppermute | solution.py:357
  92.6 1.8 %shard_map.33 = bf16[3,256,768]{2,1,0:T(8,128)(2,1)} custom-call(s32[3]{0:T(128)S(1)} %pad_add_fusion.refs_0_, bf16[3,256,128]{2,1,0:T(8,128)(2,1)S(1)} %collective-permute-done.12.refs_1_, bf16[3,256,128]{2,1,0:T(8,128)(2,1)S(1)} %collective-permute-done.13.refs_2_, bf16[3,256,128]{2,1,0:T(8,128)(2,1)S(1)} %collective-permute-done.14.refs_3_, ...), custom_call_target="tpu_custom_call" | custom-call | bytes 4000000 | tf_op jit(solution)/shard_map/pallas_call | solution.py:57
  (7 shorter events, 0.0 us)
Async XLA Ops:
  2.4 15.0 %collective-permute-start.4 = (bf16[4,128,768]{2,1,0:T(8,128)(2,1)S(1)}, bf16[4,128,768]{2,1,0:T(8,128)(2,1)S(1)}, u32[]{:S(2)}, u32[]{:S(2)}) collective-permute-start(bf16[4,128,768]{2,1,0:T(8,128)(2,1)S(1)} %get-tuple-element.38), channel_id=1, source_target_pairs={{256,257},{257,256},{258,259},{259,258},{260,261},{261,260},{262,2... | collective-permute-start | bytes 2359304 | tf_op jit(solution)/shard_map/ppermute | solution.py:357
  7.9 16.0 %collective-permute-start = (bf16[896,128]{1,0:T(8,128)(2,1)S(1)}, bf16[896,128]{1,0:T(8,128)(2,1)S(1)}, u32[]{:S(2)}, u32[]{:S(2)}) collective-permute-start(bf16[896,128]{1,0:T(8,128)(2,1)S(1)} %get-tuple-element.34), channel_id=1, source_target_pairs={{0,24},{1,25},{2,26},{3,27},{4,28},{5,29},{6,30},{7,31},{8,16},{9,... | collective-permute-start | bytes 688136 | tf_op jit(solution)/shard_map/ppermute | solution.py:357
  8.6 16.7 %collective-permute-start.1 = (bf16[896,128]{1,0:T(8,128)(2,1)S(1)}, bf16[896,128]{1,0:T(8,128)(2,1)S(1)}, u32[]{:S(2)}, u32[]{:S(2)}) collective-permute-start(bf16[896,128]{1,0:T(8,128)(2,1)S(1)} %get-tuple-element.35), channel_id=1, source_target_pairs={{0,16},{1,17},{2,18},{3,19},{4,20},{5,21},{6,22},{7,23},{8,24},{9,... | collective-permute-start | bytes 688136 | tf_op jit(solution)/shard_map/ppermute | solution.py:357
  9.2 18.4 %collective-permute-start.2 = (bf16[896,128]{1,0:T(8,128)(2,1)S(1)}, bf16[896,128]{1,0:T(8,128)(2,1)S(1)}, u32[]{:S(2)}, u32[]{:S(2)}) collective-permute-start(bf16[896,128]{1,0:T(8,128)(2,1)S(1)} %get-tuple-element.36), channel_id=1, source_target_pairs={{8,272},{9,273},{10,274},{11,275},{12,276},{13,277},{14,278},{15,2... | collective-permute-start | bytes 688136 | tf_op jit(solution)/shard_map/ppermute | solution.py:357
  9.9 25.9 %collective-permute-start.3 = (bf16[896,128]{1,0:T(8,128)(2,1)S(1)}, bf16[896,128]{1,0:T(8,128)(2,1)S(1)}, u32[]{:S(2)}, u32[]{:S(2)}) collective-permute-start(bf16[896,128]{1,0:T(8,128)(2,1)S(1)} %get-tuple-element.37), channel_id=1, source_target_pairs={{0,272},{1,273},{2,274},{3,275},{4,276},{5,277},{6,278},{7,279},{2... | collective-permute-start | bytes 688136 | tf_op jit(solution)/shard_map/ppermute | solution.py:357
  18.2 19.1 %collective-permute-start.5 = (bf16[896,128]{1,0:T(8,128)(2,1)S(1)}, bf16[896,128]{1,0:T(8,128)(2,1)S(1)}, u32[]{:S(2)}, u32[]{:S(2)}) collective-permute-start(bf16[896,128]{1,0:T(8,128)(2,1)S(1)} %get-tuple-element.39), channel_id=1, source_target_pairs={{256,24},{257,25},{258,26},{259,27},{260,28},{261,29},{262,30},{26... | collective-permute-start | bytes 688136 | tf_op jit(solution)/shard_map/ppermute | solution.py:357
  23.9 14.1 %collective-permute-start.6 = (bf16[896,128]{1,0:T(8,128)(2,1)S(1)}, bf16[896,128]{1,0:T(8,128)(2,1)S(1)}, u32[]{:S(2)}, u32[]{:S(2)}) collective-permute-start(bf16[896,128]{1,0:T(8,128)(2,1)S(1)} %get-tuple-element.40), channel_id=1, source_target_pairs={{8,264},{9,265},{10,266},{11,267},{12,268},{13,269},{14,270},{15,2... | collective-permute-start | bytes 688136 | tf_op jit(solution)/shard_map/ppermute | solution.py:357
  25.2 18.9 %collective-permute-start.7 = (bf16[896,128]{1,0:T(8,128)(2,1)S(1)}, bf16[896,128]{1,0:T(8,128)(2,1)S(1)}, u32[]{:S(2)}, u32[]{:S(2)}) collective-permute-start(bf16[896,128]{1,0:T(8,128)(2,1)S(1)} %get-tuple-element.41), channel_id=1, source_target_pairs={{0,264},{1,265},{2,266},{3,267},{4,268},{5,269},{6,270},{7,271},{2... | collective-permute-start | bytes 688136 | tf_op jit(solution)/shard_map/ppermute | solution.py:357
  27.7 16.4 %collective-permute-start.8 = (bf16[896,128]{1,0:T(8,128)(2,1)S(1)}, bf16[896,128]{1,0:T(8,128)(2,1)S(1)}, u32[]{:S(2)}, u32[]{:S(2)}) collective-permute-start(bf16[896,128]{1,0:T(8,128)(2,1)S(1)} %get-tuple-element.42), channel_id=1, source_target_pairs={{0,8},{1,9},{2,10},{3,11},{4,12},{5,13},{6,14},{7,15},{8,0},{9,1},... | collective-permute-start | bytes 688136 | tf_op jit(solution)/shard_map/ppermute | solution.py:357
  35.9 8.3 %collective-permute-start.9 = (bf16[896,128]{1,0:T(8,128)(2,1)S(1)}, bf16[896,128]{1,0:T(8,128)(2,1)S(1)}, u32[]{:S(2)}, u32[]{:S(2)}) collective-permute-start(bf16[896,128]{1,0:T(8,128)(2,1)S(1)} %get-tuple-element.43), channel_id=1, source_target_pairs={{256,16},{257,17},{258,18},{259,19},{260,20},{261,21},{262,22},{26... | collective-permute-start | bytes 688136 | tf_op jit(solution)/shard_map/ppermute | solution.py:357
  37.3 6.8 %collective-permute-start.10 = (bf16[896,128]{1,0:T(8,128)(2,1)S(1)}, bf16[896,128]{1,0:T(8,128)(2,1)S(1)}, u32[]{:S(2)}, u32[]{:S(2)}) collective-permute-start(bf16[896,128]{1,0:T(8,128)(2,1)S(1)} %get-tuple-element.44), channel_id=1, source_target_pairs={{264,272},{265,273},{266,274},{267,275},{268,276},{269,277},{270,2... | collective-permute-start | bytes 688136 | tf_op jit(solution)/shard_map/ppermute | solution.py:357
  38.0 9.1 %collective-permute-start.11 = (bf16[896,128]{1,0:T(8,128)(2,1)S(1)}, bf16[896,128]{1,0:T(8,128)(2,1)S(1)}, u32[]{:S(2)}, u32[]{:S(2)}) collective-permute-start(bf16[896,128]{1,0:T(8,128)(2,1)S(1)} %get-tuple-element.45), channel_id=1, source_target_pairs={{256,272},{257,273},{258,274},{259,275},{260,276},{261,277},{262,2... | collective-permute-start | bytes 688136 | tf_op jit(solution)/shard_map/ppermute | solution.py:357
  56.1 3.4 %collective-permute-start.16 = (bf16[3,512,128]{2,1,0:T(8,128)(2,1)S(1)}, bf16[3,512,128]{2,1,0:T(8,128)(2,1)S(1)}, u32[]{:S(2)}, u32[]{:S(2)}) collective-permute-start(bf16[3,512,128]{2,1,0:T(8,128)(2,1)S(1)} %get-tuple-element.52), channel_id=1, source_target_pairs={{0,1},{1,0},{2,3},{3,2},{4,5},{5,4},{6,7},{7,6},{8,9},{264,265},{9... | collective-permute-start | bytes 1179656 | tf_op jit(solution)/shard_map/ppermute | solution.py:357
  56.7 5.2 %collective-permute-start.12 = (bf16[3,256,128]{2,1,0:T(8,128)(2,1)S(1)}, bf16[3,256,128]{2,1,0:T(8,128)(2,1)S(1)}, u32[]{:S(2)}, u32[]{:S(2)}) collective-permute-start(bf16[3,256,128]{2,1,0:T(8,128)(2,1)S(1)} %get-tuple-element.47), channel_id=1, source_target_pairs={{24,0},{25,1},{26,2},{27,3},{28,4},{29,5},{30,6},{31,7},{16,8},{17... | collective-permute-start | bytes 589832 | tf_op jit(solution)/shard_map/ppermute | solution.py:357
  57.4 5.8 %collective-permute-start.13 = (bf16[3,256,128]{2,1,0:T(8,128)(2,1)S(1)}, bf16[3,256,128]{2,1,0:T(8,128)(2,1)S(1)}, u32[]{:S(2)}, u32[]{:S(2)}) collective-permute-start(bf16[3,256,128]{2,1,0:T(8,128)(2,1)S(1)} %get-tuple-element.48), channel_id=1, source_target_pairs={{16,0},{17,1},{18,2},{19,3},{20,4},{21,5},{22,6},{23,7},{24,8},{25... | collective-permute-start | bytes 589832 | tf_op jit(solution)/shard_map/ppermute | solution.py:357
  58.1 6.5 %collective-permute-start.14 = (bf16[3,256,128]{2,1,0:T(8,128)(2,1)S(1)}, bf16[3,256,128]{2,1,0:T(8,128)(2,1)S(1)}, u32[]{:S(2)}, u32[]{:S(2)}) collective-permute-start(bf16[3,256,128]{2,1,0:T(8,128)(2,1)S(1)} %get-tuple-element.49), channel_id=1, source_target_pairs={{272,8},{273,9},{274,10},{275,11},{276,12},{277,13},{278,14},{279,... | collective-permute-start | bytes 589832 | tf_op jit(solution)/shard_map/ppermute | solution.py:357
  58.8 7.1 %collective-permute-start.15 = (bf16[3,256,128]{2,1,0:T(8,128)(2,1)S(1)}, bf16[3,256,128]{2,1,0:T(8,128)(2,1)S(1)}, u32[]{:S(2)}, u32[]{:S(2)}) collective-permute-start(bf16[3,256,128]{2,1,0:T(8,128)(2,1)S(1)} %get-tuple-element.50), channel_id=1, source_target_pairs={{272,0},{273,1},{274,2},{275,3},{276,4},{277,5},{278,6},{279,7},{2... | collective-permute-start | bytes 589832 | tf_op jit(solution)/shard_map/ppermute | solution.py:357
  60.6 12.9 %collective-permute-start.17 = (bf16[3,256,128]{2,1,0:T(8,128)(2,1)S(1)}, bf16[3,256,128]{2,1,0:T(8,128)(2,1)S(1)}, u32[]{:S(2)}, u32[]{:S(2)}) collective-permute-start(bf16[3,256,128]{2,1,0:T(8,128)(2,1)S(1)} %get-tuple-element.55), channel_id=1, source_target_pairs={{24,256},{25,257},{26,258},{27,259},{28,260},{29,261},{30,262},{31... | collective-permute-start | bytes 589832 | tf_op jit(solution)/shard_map/ppermute | solution.py:357
  62.0 12.3 %collective-permute-start.18 = (bf16[3,256,128]{2,1,0:T(8,128)(2,1)S(1)}, bf16[3,256,128]{2,1,0:T(8,128)(2,1)S(1)}, u32[]{:S(2)}, u32[]{:S(2)}) collective-permute-start(bf16[3,256,128]{2,1,0:T(8,128)(2,1)S(1)} %get-tuple-element.56), channel_id=1, source_target_pairs={{264,8},{265,9},{266,10},{267,11},{268,12},{269,13},{270,14},{271,... | collective-permute-start | bytes 589832 | tf_op jit(solution)/shard_map/ppermute | solution.py:357
  63.3 19.3 %collective-permute-start.19 = (bf16[3,256,128]{2,1,0:T(8,128)(2,1)S(1)}, bf16[3,256,128]{2,1,0:T(8,128)(2,1)S(1)}, u32[]{:S(2)}, u32[]{:S(2)}) collective-permute-start(bf16[3,256,128]{2,1,0:T(8,128)(2,1)S(1)} %get-tuple-element.57), channel_id=1, source_target_pairs={{264,0},{265,1},{266,2},{267,3},{268,4},{269,5},{270,6},{271,7},{2... | collective-permute-start | bytes 589832 | tf_op jit(solution)/shard_map/ppermute | solution.py:357
  64.6 22.6 %collective-permute-start.20 = (bf16[3,256,128]{2,1,0:T(8,128)(2,1)S(1)}, bf16[3,256,128]{2,1,0:T(8,128)(2,1)S(1)}, u32[]{:S(2)}, u32[]{:S(2)}) collective-permute-start(bf16[3,256,128]{2,1,0:T(8,128)(2,1)S(1)} %get-tuple-element.58), channel_id=1, source_target_pairs={{8,0},{9,1},{10,2},{11,3},{12,4},{13,5},{14,6},{15,7},{0,8},{1,9},... | collective-permute-start | bytes 589832 | tf_op jit(solution)/shard_map/ppermute | solution.py:357
  65.9 24.3 %collective-permute-start.21 = (bf16[3,256,128]{2,1,0:T(8,128)(2,1)S(1)}, bf16[3,256,128]{2,1,0:T(8,128)(2,1)S(1)}, u32[]{:S(2)}, u32[]{:S(2)}) collective-permute-start(bf16[3,256,128]{2,1,0:T(8,128)(2,1)S(1)} %get-tuple-element.59), channel_id=1, source_target_pairs={{16,256},{17,257},{18,258},{19,259},{20,260},{21,261},{22,262},{23... | collective-permute-start | bytes 589832 | tf_op jit(solution)/shard_map/ppermute | solution.py:357
  73.6 16.6 %collective-permute-start.22 = (bf16[3,256,128]{2,1,0:T(8,128)(2,1)S(1)}, bf16[3,256,128]{2,1,0:T(8,128)(2,1)S(1)}, u32[]{:S(2)}, u32[]{:S(2)}) collective-permute-start(bf16[3,256,128]{2,1,0:T(8,128)(2,1)S(1)} %get-tuple-element.60), channel_id=1, source_target_pairs={{272,264},{273,265},{274,266},{275,267},{276,268},{277,269},{278,2... | collective-permute-start | bytes 589832 | tf_op jit(solution)/shard_map/ppermute | solution.py:357
  74.3 18.4 %collective-permute-start.23 = (bf16[3,256,128]{2,1,0:T(8,128)(2,1)S(1)}, bf16[3,256,128]{2,1,0:T(8,128)(2,1)S(1)}, u32[]{:S(2)}, u32[]{:S(2)}) collective-permute-start(bf16[3,256,128]{2,1,0:T(8,128)(2,1)S(1)} %get-tuple-element.61), channel_id=1, source_target_pairs={{272,256},{273,257},{274,258},{275,259},{276,260},{277,261},{278,2... | collective-permute-start | bytes 589832 | tf_op jit(solution)/shard_map/ppermute | solution.py:357

commit v4 on v3

v4 whole, which is shorter than its diff:
```python
import math

import jax
import jax.numpy as jnp
from jax import lax
from jax.experimental import pallas as pl
from jax.experimental.pallas import tpu as pltpu
from jax.sharding import PartitionSpec as P

HD = 128
BLK = 256
LEN = 1024
SCALE = 1.0 / math.sqrt(HD)
SCALE2 = SCALE * math.log2(math.e)
AXES = ("section", "dp", "tensor")
BF = jnp.bfloat16
F32 = jnp.float32
VM = pl.BlockSpec(memory_space=pltpu.VMEM)
SM = pl.BlockSpec(memory_space=pltpu.SMEM)


def first_head(z):
    return 2 * z - jnp.where(z > 0, 1, 0)


def second_head(z):
    return jnp.where(z == 2, 4, 2)


def is_inner(z):
    return (z == 1) | (z == 2)


def head_cols(head):
    return pl.ds(pl.multiple_of(head * HD, HD), HD)


def rows_of(index, size):
    return pl.ds(pl.multiple_of(index * size, size), size)


def dot_nt(a, b):
    return lax.dot_general(a, b, (((1,), (1,)), ((), ())), preferred_element_type=F32)


def dot(a, b):
    return jnp.dot(a, b, preferred_element_type=F32)


def flip(x):
    return x.T


def call(kernel, outs, args, scratch=(), flops=0, spec=VM, out_spec=VM):
    return pl.pallas_call(
        kernel,
        out_shape=[jax.ShapeDtypeStruct(s, d) for s, d in outs],
        in_specs=[SM] + [spec] * (len(args) - 1),
        out_specs=[out_spec] * len(outs),
        scratch_shapes=list(scratch),
        compiler_params=pltpu.CompilerParams(vmem_limit_bytes=48 * 1024 * 1024),
        cost_estimate=pl.CostEstimate(flops=flops, bytes_accessed=4000000, transcendentals=0),
    )(*args)


CHUNK = 3 * BLK + HD


def selection(rows, cols, odd):
    row = lax.broadcasted_iota(jnp.int32, (rows, cols), 0)
    col = lax.broadcasted_iota(jnp.int32, (rows, cols), 1)
    return jnp.where(col == 2 * row + odd, 1.0, 0.0).astype(BF)


def fill_first(out, start, local, grad, head):
    cols = head_cols(head)
    for j in range(3):
        out[start + j * BLK : start + (j + 1) * BLK] = local[j, :, cols]
    out[start + 3 * BLK : start + CHUNK] = grad[:, cols]


def pick_far_kernel(info, local_hbm, grad_hbm, away, a2, a3, a1, near, local, sems, grad):
    z, h, s = info[0], info[1], info[2]
    sources = [grad_hbm] + [local_hbm.at[j] for j in range(3)]
    copies = [
        pltpu.make_async_copy(source, local.at[i], sems.at[i]) for i, source in enumerate(sources)
    ]
    for copy in copies:
        copy.start()

    @pl.when(s == 0)
    def _():
        copies[0].wait()
        grad[...] = dot(selection(128, 256, h), local[0]).astype(BF)
        for copy in copies[1:]:
            copy.wait()
        rows = local.at[1:4]
        fill_first(a3, 0, rows, grad, first_head(z ^ 3))
        fill_first(a2, 0, rows, grad, first_head(z ^ 2))
        fill_first(a1, 0, rows, grad, first_head(z ^ 1))
        for k in range(4):
            fill_first(near, k * CHUNK, rows, grad, second_head(z ^ k))
        fill_first(near, 4 * CHUNK, rows, grad, first_head(z))

    @pl.when(s == 1)
    def _():
        take = selection(128, 256, 1 - h)
        for i, copy in enumerate(copies):
            copy.wait()
            away[(i - 1) % 4] = dot(take, local[i]).astype(BF)


def pick_own_kernel(info, local_hbm, stash, local, sems):
    h, s = info[1], info[2]

    @pl.when(s == 1)
    def _():
        copies = [
            pltpu.make_async_copy(local_hbm.at[j], local.at[j], sems.at[j]) for j in range(3)
        ]
        for copy in copies:
            copy.start()
        for j, copy in enumerate(copies):
            copy.wait()
            own = dot(selection(128, 256, h), local[j]).astype(BF)
            for head in range(6):
                start = (head * 3 + j) * HD
                stash[start : start + HD] = own[:, head * HD : (head + 1) * HD]


def pick_second_kernel(info, near, stash, came, *outs):
    z, h, s = info[0], info[1], info[2]

    def fill(out, head):
        cols = head_cols(head)
        for j in range(3):
            mine = pl.ds(pl.multiple_of(j * BLK + h * HD, HD), HD)
            theirs = pl.ds(pl.multiple_of(j * BLK + (1 - h) * HD, HD), HD)
            out[mine, :] = stash[rows_of(head * 3 + j, HD), :]
            out[theirs, :] = came[j, :, cols]
        out[3 * BLK :] = came[3, :, cols]

    @pl.when(s == 0)
    def _():
        for k in range(5):
            outs[k][...] = near[k * CHUNK : (k + 1) * CHUNK]

    @pl.when(s == 1)
    def _():
        for k in range(4):
            fill(outs[k], first_head(z ^ k))
            fill(outs[4 + k], second_head(z ^ k))


def score_block(keys, q, i):
    n = (i + 1) * BLK
    st = dot_nt(keys[0:n], q[i * BLK : n]) * SCALE2
    key = lax.broadcasted_iota(jnp.int32, (BLK, BLK), 0)
    qry = lax.broadcasted_iota(jnp.int32, (BLK, BLK), 1)
    tail = jnp.where(key <= qry, st[n - BLK :], -jnp.inf)
    return tail if i == 0 else jnp.concatenate([st[: n - BLK], tail], axis=0)


def backward_block(i, p, dp, delta, keys_t, q, g, dqt, dk, dv):
    n = (i + 1) * BLK
    cols = slice(i * BLK, n)
    ds = (p * (dp - delta)).astype(BF)
    dqt[:, cols] = (dot(keys_t[:, 0:n], ds) * SCALE).astype(BF)
    add_k = dot(ds, q[cols])
    add_v = dot(p.astype(BF), g[cols])
    if i > 0:
        dk[0 : n - BLK] += add_k[: n - BLK]
        dv[0 : n - BLK] += add_v[: n - BLK]
    dk[n - BLK : n] = add_k[n - BLK :]
    dv[n - BLK : n] = add_v[n - BLK :]


def hand_out(info, outs, dq, dk, dv):
    z = info[0]
    for k in range(4):
        rows = rows_of(z ^ k, BLK)
        outs[k][0] = dq[rows]
        outs[k][1] = (dk[rows] * SCALE).astype(BF)
        outs[k][2] = dv[rows].astype(BF)


def backward_block(i, p, dp, delta, keys_t, q, g, dqt, dk, dv):
    n = (i + 1) * BLK
    cols = slice(i * BLK, n)
    ds = (p * (dp - delta)).astype(BF)
    dqt[:, cols] = (dot(keys_t[:, 0:n], ds) * SCALE).astype(BF)
    add_k = dot(ds, q[cols])
    add_v = dot(p.astype(BF), g[cols])
    if i > 0:
        dk[0 : n - BLK] += add_k[: n - BLK]
        dv[0 : n - BLK] += add_v[: n - BLK]
    dk[n - BLK : n] = add_k[n - BLK :]
    dv[n - BLK : n] = add_v[n - BLK :]


def main_kernel(info, *refs):
    a2, a3, a1, x3, x0, x1, d1, x2, d2, d3, here = refs[0:11]
    keep, give, out0, out1, out2, out3 = refs[11:17]
    first, second, ot1, g1, kt1, vt1, kt2, dqt1, p1, dq1, dq2, dk1, dv1, dk2, dv2 = refs[17:]
    z, h, s = info[0], info[1], info[2]

    def join(from_first, from_second):
        for k in range(4):
            rows = rows_of(z ^ k, BLK)
            for j in range(3):
                first[j, rows, :] = from_first[k][j * BLK : (j + 1) * BLK]
                second[j, rows, :] = from_second[k][j * BLK : (j + 1) * BLK]
            for part, chunk in ((h, from_first[k]), (1 - h, from_second[k])):
                at = pl.ds(pl.multiple_of((z ^ k) * BLK + part * HD, HD), HD)
                second[3, at, :] = chunk[3 * BLK :]

    @pl.when(s == 0)
    def _():
        join((here, a1, a2, a3), (x0, x1, x2, x3))

    @pl.when(s == 1)
    def _():
        join((x0, x1, x2, x3), (here, d1, d2, d3))

    vt1[...] = flip(first[2])
    kt2[...] = flip(second[1])
    kt1[...] = flip(first[1])

    def softmax(keys, q, i):
        st = score_block(keys, q, i)
        top = jnp.max(st, axis=0, keepdims=True)
        p = jnp.exp2(st - top)
        return p * (1.0 / jnp.sum(p, axis=0, keepdims=True))

    def forward(i):
        n = (i + 1) * BLK
        cols = slice(i * BLK, n)
        p = softmax(first.at[1], first.at[0], i)
        p1[0:n, cols] = p
        out = dot(vt1[:, 0:n], p.astype(BF)).astype(BF)
        ot1[:, cols] = out
        second[0, cols] = (second[0, cols].astype(F32) + out.astype(F32).T).astype(BF)

    def both(i):
        n = (i + 1) * BLK
        cols = slice(i * BLK, n)
        dp = dot_nt(second[2, 0:n], second[3, cols])
        st = score_block(second.at[1], second.at[0], i)
        top = jnp.max(st, axis=0, keepdims=True)
        p = jnp.exp2(st - top)
        share = 1.0 / jnp.sum(p, axis=0, keepdims=True)
        delta = jnp.sum(p * dp, axis=0, keepdims=True) * share
        p = p * share
        backward_block(i, p, dp, delta, kt2, second.at[0], second.at[3], g1, dk2, dv2)
        dq2[cols] = flip(g1[:, cols])

    def backward(i):
        n = (i + 1) * BLK
        cols = slice(i * BLK, n)
        delta = jnp.sum(g1[:, cols].astype(F32) * ot1[:, cols].astype(F32), axis=0, keepdims=True)
        dp = dot_nt(first[2, 0:n], dq2[cols])
        backward_block(i, p1[0:n, cols], dp, delta, kt1, first.at[0], dq2, dqt1, dk1, dv1)
        dq1[cols] = flip(dqt1[:, cols])

    for i in range(4):
        forward(i)
    for i in range(4):
        both(i)
    for i in range(4):
        backward(i)

    def block(b, part):
        return pl.ds(pl.multiple_of(b * BLK + part * HD, HD), HD)

    for b in range(4):
        rows = slice(b * HD, (b + 1) * HD)
        for out, part in ((keep, h), (give, 1 - h)):
            out[0, rows] = dq2[block(b, part)]
            out[1, rows] = (dk2[block(b, part)] * SCALE).astype(BF)
            out[2, rows] = dv2[block(b, part)].astype(BF)

    for k, out in enumerate((out0, out1, out2, out3)):
        rows = rows_of(z ^ k, BLK)
        out[0] = dq1[rows]
        out[1] = (dk1[rows] * SCALE).astype(BF)
        out[2] = dv1[rows].astype(BF)


def weave_kernel(info, keep, came, d0, d1, d2, d3, x3, x0, x1, c1, x2, c3, c2, here):
    z, h, s = info[0], info[1], info[2]
    row = lax.broadcasted_iota(jnp.int32, (256, 256), 0)
    col = lax.broadcasted_iota(jnp.int32, (256, 256), 1)
    wanted = jnp.where(col < HD, 2 * col + h, 2 * (col - HD) + 1 - h)
    put = jnp.where(row == wanted, 1.0, 0.0).astype(BF)

    def weave(out, k):
        rows = rows_of(z ^ k, HD)
        parts = [jnp.concatenate([x[j, rows, :] for j in range(3)], axis=1) for x in (keep, came)]
        woven = dot(put, jnp.concatenate(parts, axis=0)).astype(BF)
        for j in range(3):
            out[j] = woven[:, j * HD : (j + 1) * HD]

    @pl.when(s == 0)
    def _():
        here[...] = d0[...]
        for k, out in enumerate((x0, x1, x2, x3)):
            weave(out, k)

    @pl.when(s == 1)
    def _():
        for rows, out in ((d0, x0), (d1, x1), (d2, x2), (d3, x3)):
            out[...] = rows[...]
        for k, out in enumerate((here, c1, c2, c3)):
            weave(out, k)


def finish_kernel(info, *refs):
    a2, a3, a1, x3, x0, x1, c1, x2, c2, c3, here, out_hbm, out, sems = refs
    z, s = info[0], info[2]

    def place(slot_a, slot_b):
        for j in range(3):
            for k in range(4):
                out[j, :, head_cols(first_head(z ^ k))] = slot_a[k][j]

                @pl.when(is_inner(z ^ k))
                def _(k=k):
                    out[j, :, head_cols(second_head(z ^ k))] = slot_b[k][j]

            pltpu.make_async_copy(out.at[j], out_hbm.at[j], sems.at[j]).start()

    @pl.when(s == 0)
    def _():
        place((here, a1, a2, a3), (x0, x1, x2, x3))

    @pl.when(s == 1)
    def _():
        place((x0, x1, x2, x3), (here, c1, c2, c3))

    for j in range(3):
        pltpu.make_async_copy(out.at[j], out_hbm.at[j], sems.at[j]).wait()


def build(n_dp, n_tensor):
    def index(s, d, t):
        return (s * n_dp + d) * n_tensor + t

    def everywhere(rule):
        pairs = []
        for d in range(n_dp):
            for t in range(n_tensor):
                pairs += rule(d, t)
        return pairs

    def send(value, pairs):
        return lax.ppermute(value, AXES, pairs)

    def inward(src, slot, k):
        return everywhere(
            lambda d, t: [(index(src, d, t), index(slot, d ^ k, t))]
            if slot == 0 or (d ^ k) % 4 in (1, 2)
            else []
        )

    def outward(dst, slot, k):
        return [(b, a) for a, b in inward(dst, slot, k)]

    def swap_lines(value, cores):
        return send(
            value,
            everywhere(
                lambda d, t: [
                    (index(c, d, t), index(c, d, t ^ 1))
                    for c in cores
                    if c == 1 and len(cores) == 1 or c == 0 or d % 4 in (1, 2)
                ]
            ),
        )

    def body(projections, out_grad):
        s = lax.axis_index("section")
        z = lax.axis_index("dp") % 4
        h = lax.axis_index("tensor") % 2
        info = jnp.stack([z, h, s]).astype(jnp.int32)
        local = projections[0]
        rows, cols = local.shape[1:]
        half = ((4, rows // 2, cols), BF)
        chunk_in = ((CHUNK, HD), BF)
        chunk = ((3, BLK, HD), BF)
        vm = pltpu.VMEM
        tall, wide = vm((LEN, HD), BF), vm((HD, LEN), BF)
        acc = vm((LEN, HD), F32)

        inputs = [info] + [
            pltpu.with_memory_space_constraint(x, pltpu.HBM) for x in (local, out_grad)
        ]
        hbm = pl.BlockSpec(memory_space=pltpu.HBM)
        staging = [vm((4, rows, cols), BF), pltpu.SemaphoreType.DMA((4,)), vm((HD, cols), BF)]
        away, a2, a3, a1, near = call(
            pick_far_kernel,
            [half] + [chunk_in] * 3 + [((5 * CHUNK, HD), BF)],
            inputs,
            staging,
            spec=hbm,
        )
        came = swap_lines(away, (1,))
        a3 = send(a3, inward(0, 0, 3))
        a2 = send(a2, inward(0, 0, 2))
        a1 = send(a1, inward(0, 0, 1))
        (stash,) = call(
            pick_own_kernel, [((18 * HD, HD), BF)], inputs[:2], staging[:2], spec=hbm
        )
        x0, x1, x2, x3, here, d1, d2, d3 = call(
            pick_second_kernel, [chunk_in] * 8, [info, near, stash, came]
        )
        x3 = send(x3, inward(0, 1, 3) + inward(1, 0, 3))
        x0 = send(x0, inward(0, 1, 0) + inward(1, 0, 0))
        x1 = send(x1, inward(0, 1, 1) + inward(1, 0, 1))
        d1 = send(d1, inward(1, 1, 1))
        x2 = send(x2, inward(0, 1, 2) + inward(1, 0, 2))
        d3 = send(d3, inward(1, 1, 3))
        d2 = send(d2, inward(1, 1, 2))
        keep, give, d0, d1, d2, d3 = call(
            main_kernel,
            [((3, 4 * HD, HD), BF)] * 2 + [chunk] * 4,
            [info, a2, a3, a1, x3, x0, x1, d1, x2, d2, d3, here],
            [vm((3, LEN, HD), BF), vm((4, LEN, HD), BF)]
            + [wide] * 6
            + [vm((LEN, LEN), F32), tall, tall, acc, acc, acc, acc],
        )
        came = swap_lines(give, (0, 1))
        a3 = send(d3, outward(0, 0, 3))
        a2 = send(d2, outward(0, 0, 2))
        a1 = send(d1, outward(0, 0, 1))
        x3, x0, x1, c1, x2, c3, c2, here = call(
            weave_kernel, [chunk] * 8, [info, keep, came, d0, d1, d2, d3]
        )
        x3 = send(x3, outward(0, 1, 3) + outward(1, 0, 3))
        x0 = send(x0, outward(0, 1, 0) + outward(1, 0, 0))
        x1 = send(x1, outward(0, 1, 1) + outward(1, 0, 1))
        c1 = send(c1, outward(1, 1, 1))
        x2 = send(x2, outward(0, 1, 2) + outward(1, 0, 2))
        c3 = send(c3, outward(1, 1, 3))
        c2 = send(c2, outward(1, 1, 2))
        (out,) = call(
            finish_kernel,
            [((3, rows, cols), BF)],
            [info, a2, a3, a1, x3, x0, x1, c1, x2, c2, c3, here],
            [vm((3, rows, cols), BF), pltpu.SemaphoreType.DMA((3,))],
            out_spec=hbm,
        )
        return out[None]

    return body


def solution(mesh):
    body = build(mesh.shape["dp"], mesh.shape["tensor"])
    in_specs = (P("section", None, "dp", "tensor"), P("dp", "tensor"))
    out_specs = P("section", None, "dp", "tensor")
    return jax.shard_map(body, mesh=mesh, in_specs=in_specs, out_specs=out_specs, check_vma=False)
```

time: 95 us -> 89.7 us (0.944)
  starting transfers between devices: 45.8 us -> 36.1 us
  waiting for transfers between devices: 30.9 us -> 36.8 us
  Pallas kernels: 17.3 us -> 15.9 us
    ppermute x24 -> x22, starting transfers between devices: 45.8 us -> 36.1 us  [send(): return lax.ppermute(value, AXES, pairs)]
    ppermute x24 -> x22, waiting for transfers between devices: 30.9 us -> 36.8 us  [send(): return lax.ppermute(value, AXES, pairs)]
    pallas_call x6, Pallas kernels: 17.3 us -> 15.9 us  [call(): pl.pallas_call(kernel, out_shape=[jax.ShapeDtypeStruct(s, d) for s, d in...]
  transfers between devices with their start and end apart: 24 -> 22, of which waited for: 7 -> 7; matrix products, arithmetic and copies ran while one was open for 0% -> 0% of each run, Pallas kernels for 4% -> 5%
where the time goes in v4:
time: 89.7 us; the launch traced here: 89.1 us
  waiting for transfers between devices  36.8 us (41%)
  starting transfers between devices  36.1 us (40%)
  Pallas kernels  15.9 us (18%)
    ppermute x22, waiting for transfers between devices, send(): return lax.ppermute(value, AXES, pairs)  36.8 us
    ppermute x22, starting transfers between devices, send(): return lax.ppermute(value, AXES, pairs)  36.1 us
    pallas_call x6, Pallas kernels, call(): pl.pallas_call(kernel, out_shape=[jax.ShapeDtypeStruct(s, d) for s, d in...  15.9 us
  transfers between devices with their start and end apart: 22, of which 7 were waited for; matrix products, arithmetic and copies ran while one was open for 0% of the time, Pallas kernels for 5%

profile of v4, /device:TPU:1, one launch (start us, length us, event | category | flops | bytes accessed | tf_op | source)
XLA Modules:
  0.0 89.1 jit_solution(17839412273807914445)
XLA Ops:
  0.0 0.1 pad_add_fusion.info
  0.1 2.5 %shard_map.28 = (bf16[4,128,768]{2,1,0:T(8,128)(2,1)S(1)}, bf16[896,128]{1,0:T(8,128)(2,1)S(1)}, bf16[896,128]{1,0:T(8,128)(2,1)S(1)}, bf16[896,128]{1,0:T(8,128)(2,1)S(1)}, bf16[4480,128]{1,0:T(8,128)(2,1)S(1)}) custom-call(s32[3]{0:T(128)S(1)} %pad_add_fusion.info, bf16[3,256,768]{2,1,0:T(8,128)(2,1)} %bitcast.5, bf16[256,768]{1,0:T(8,128)(2,1)} %grad_hbm.1), custom_call_target="tpu_custom_call" | custom-call | bytes 4000000 | tf_op jit(solution)/shard_map/pallas_call | solution.py:55
  2.6 5.5 %collective-permute-start.3 = (bf16[4,128,768]{2,1,0:T(8,128)(2,1)S(1)}, bf16[4,128,768]{2,1,0:T(8,128)(2,1)S(1)}, u32[]{:S(2)}, u32[]{:S(2)}) collective-permute-start(bf16[4,128,768]{2,1,0:T(8,128)(2,1)S(1)} %get-tuple-element.36), channel_id=1, source_target_pairs={{256,257},{257,256},{258,259},{259,258},{260,261},{261,260},{262,2... | collective-permute-start | bytes 2359304 | tf_op jit(solution)/shard_map/ppermute | solution.py:356
  8.1 0.7 collective-permute-start
  8.7 0.7 collective-permute-start.1
  9.4 0.7 collective-permute-start.2
  10.1 2.2 %shard_map.29.stash = bf16[2304,128]{1,0:T(8,128)(2,1)S(1)} custom-call(s32[3]{0:T(128)S(1)} %pad_add_fusion.info, bf16[3,256,768]{2,1,0:T(8,128)(2,1)} %bitcast.6), custom_call_target="tpu_custom_call" | custom-call | bytes 4000000 | tf_op jit(solution)/shard_map/pallas_call | solution.py:55
  12.4 5.1 %collective-permute-done.3.came = bf16[4,128,768]{2,1,0:T(8,128)(2,1)S(1)} collective-permute-done((bf16[4,128,768]{2,1,0:T(8,128)(2,1)S(1)}, bf16[4,128,768]{2,1,0:T(8,128)(2,1)S(1)}, u32[]{:S(2)}, u32[]{:S(2)}) %collective-permute-start.3) | collective-permute-done | bytes 786464 | tf_op jit(solution)/shard_map/ppermute | solution.py:356
  17.4 0.8 shard_map.30
  18.2 4.6 %collective-permute-start.4 = (bf16[896,128]{1,0:T(8,128)(2,1)S(1)}, bf16[896,128]{1,0:T(8,128)(2,1)S(1)}, u32[]{:S(2)}, u32[]{:S(2)}) collective-permute-start(bf16[896,128]{1,0:T(8,128)(2,1)S(1)} %get-tuple-element.37), channel_id=1, source_target_pairs={{8,272},{9,273},{10,274},{11,275},{12,276},{13,277},{14,278},{15,2... | collective-permute-start | bytes 688136 | tf_op jit(solution)/shard_map/ppermute | solution.py:356
  22.9 1.3 %collective-permute-start.5 = (bf16[896,128]{1,0:T(8,128)(2,1)S(1)}, bf16[896,128]{1,0:T(8,128)(2,1)S(1)}, u32[]{:S(2)}, u32[]{:S(2)}) collective-permute-start(bf16[896,128]{1,0:T(8,128)(2,1)S(1)} %get-tuple-element.38), channel_id=1, source_target_pairs={{8,264},{9,265},{10,266},{11,267},{12,268},{13,269},{14,270},{15,2... | collective-permute-start | bytes 688136 | tf_op jit(solution)/shard_map/ppermute | solution.py:356
  24.2 0.0 collective-permute-done.refs_0_
  24.2 3.6 %collective-permute-start.6 = (bf16[896,128]{1,0:T(8,128)(2,1)S(1)}, bf16[896,128]{1,0:T(8,128)(2,1)S(1)}, u32[]{:S(2)}, u32[]{:S(2)}) collective-permute-start(bf16[896,128]{1,0:T(8,128)(2,1)S(1)} %get-tuple-element.39), channel_id=1, source_target_pairs={{0,264},{1,265},{2,266},{3,267},{4,268},{5,269},{6,270},{7,271},{2... | collective-permute-start | bytes 688136 | tf_op jit(solution)/shard_map/ppermute | solution.py:356
  27.8 0.0 collective-permute-done.1.refs_1_
  27.8 2.0 %collective-permute-start.7 = (bf16[896,128]{1,0:T(8,128)(2,1)S(1)}, bf16[896,128]{1,0:T(8,128)(2,1)S(1)}, u32[]{:S(2)}, u32[]{:S(2)}) collective-permute-start(bf16[896,128]{1,0:T(8,128)(2,1)S(1)} %get-tuple-element.40), channel_id=1, source_target_pairs={{256,264},{257,265},{258,266},{259,267},{260,268},{261,269},{262,2... | collective-permute-start | bytes 688136 | tf_op jit(solution)/shard_map/ppermute | solution.py:356
  29.8 0.0 collective-permute-done.2.refs_2_
  29.8 1.3 %collective-permute-start.8 = (bf16[896,128]{1,0:T(8,128)(2,1)S(1)}, bf16[896,128]{1,0:T(8,128)(2,1)S(1)}, u32[]{:S(2)}, u32[]{:S(2)}) collective-permute-start(bf16[896,128]{1,0:T(8,128)(2,1)S(1)} %get-tuple-element.41), channel_id=1, source_target_pairs={{0,272},{1,273},{2,274},{3,275},{4,276},{5,277},{6,278},{7,279},{2... | collective-permute-start | bytes 688136 | tf_op jit(solution)/shard_map/ppermute | solution.py:356
  31.2 0.0 collective-permute-done.4.refs_3_
  31.2 3.9 %collective-permute-start.9 = (bf16[896,128]{1,0:T(8,128)(2,1)S(1)}, bf16[896,128]{1,0:T(8,128)(2,1)S(1)}, u32[]{:S(2)}, u32[]{:S(2)}) collective-permute-start(bf16[896,128]{1,0:T(8,128)(2,1)S(1)} %get-tuple-element.42), channel_id=1, source_target_pairs={{256,272},{257,273},{258,274},{259,275},{260,276},{261,277},{262,2... | collective-permute-start | bytes 688136 | tf_op jit(solution)/shard_map/ppermute | solution.py:356
  35.1 0.0 collective-permute-done.5.refs_4_
  35.1 0.7 collective-permute-start.10
  35.8 0.0 collective-permute-done.6.refs_5_
  35.8 1.7 %collective-permute-done.7.refs_6_ = bf16[896,128]{1,0:T(8,128)(2,1)S(1)} collective-permute-done((bf16[896,128]{1,0:T(8,128)(2,1)S(1)}, bf16[896,128]{1,0:T(8,128)(2,1)S(1)}, u32[]{:S(2)}, u32[]{:S(2)}) %collective-permute-start.7) | collective-permute-done | bytes 229408 | tf_op jit(solution)/shard_map/ppermute | solution.py:356
  37.5 3.1 %collective-permute-done.8.refs_7_ = bf16[896,128]{1,0:T(8,128)(2,1)S(1)} collective-permute-done((bf16[896,128]{1,0:T(8,128)(2,1)S(1)}, bf16[896,128]{1,0:T(8,128)(2,1)S(1)}, u32[]{:S(2)}, u32[]{:S(2)}) %collective-permute-start.8) | collective-permute-done | bytes 229408 | tf_op jit(solution)/shard_map/ppermute | solution.py:356
  40.6 2.5 %collective-permute-done.9.refs_8_ = bf16[896,128]{1,0:T(8,128)(2,1)S(1)} collective-permute-done((bf16[896,128]{1,0:T(8,128)(2,1)S(1)}, bf16[896,128]{1,0:T(8,128)(2,1)S(1)}, u32[]{:S(2)}, u32[]{:S(2)}) %collective-permute-start.9) | collective-permute-done | bytes 229408 | tf_op jit(solution)/shard_map/ppermute | solution.py:356
  43.1 0.0 collective-permute-done.10.refs_9_
  43.1 7.6 %shard_map.31 = (bf16[3,512,128]{2,1,0:T(8,128)(2,1)S(1)}, bf16[3,512,128]{2,1,0:T(8,128)(2,1)S(1)}, bf16[3,256,128]{2,1,0:T(8,128)(2,1)S(1)}, bf16[3,256,128]{2...) custom-call(s32[3]{0:T(128)S(1)} %pad_add_fusion.info, ...), custom_call_target="tpu_custom_call" | custom-call | bytes 4000000 | tf_op jit(solution)/shard_map/pallas_call | solution.py:55
  50.7 0.7 collective-permute-start.14
  51.4 0.7 collective-permute-start.11
  52.1 0.7 collective-permute-start.12
  52.8 0.7 collective-permute-start.13
  53.4 0.0 collective-permute-done.14.came
  53.4 1.1 %shard_map.32 = (bf16[3,256,128]{2,1,0:T(8,128)(2,1)S(1)}, bf16[3,256,128]{2,1,0:T(8,128)(2,1)S(1)}, bf16[3,256,128]{2,1,0:T(8,128)(2,1)S(1)}, bf16[3,256,128]{2...) custom-call(s32[3]{0:T(128)S(1)} %pad_add_fusion.info, ...), custom_call_target="tpu_custom_call" | custom-call | bytes 4000000 | tf_op jit(solution)/shard_map/pallas_call | solution.py:55
  54.5 1.3 %collective-permute-start.15 = (bf16[3,256,128]{2,1,0:T(8,128)(2,1)S(1)}, bf16[3,256,128]{2,1,0:T(8,128)(2,1)S(1)}, u32[]{:S(2)}, u32[]{:S(2)}) collective-permute-start(bf16[3,256,128]{2,1,0:T(8,128)(2,1)S(1)} %get-tuple-element.51), channel_id=1, source_target_pairs={{272,8},{273,9},{274,10},{275,11},{276,12},{277,13},{278,14},{279,... | collective-permute-start | bytes 589832 | tf_op jit(solution)/shard_map/ppermute | solution.py:356
  55.8 1.3 %collective-permute-start.16 = (bf16[3,256,128]{2,1,0:T(8,128)(2,1)S(1)}, bf16[3,256,128]{2,1,0:T(8,128)(2,1)S(1)}, u32[]{:S(2)}, u32[]{:S(2)}) collective-permute-start(bf16[3,256,128]{2,1,0:T(8,128)(2,1)S(1)} %get-tuple-element.52), channel_id=1, source_target_pairs={{264,8},{265,9},{266,10},{267,11},{268,12},{269,13},{270,14},{271,... | collective-permute-start | bytes 589832 | tf_op jit(solution)/shard_map/ppermute | solution.py:356
  57.1 0.0 collective-permute-done.11.refs_0_
  57.1 1.3 %collective-permute-start.17 = (bf16[3,256,128]{2,1,0:T(8,128)(2,1)S(1)}, bf16[3,256,128]{2,1,0:T(8,128)(2,1)S(1)}, u32[]{:S(2)}, u32[]{:S(2)}) collective-permute-start(bf16[3,256,128]{2,1,0:T(8,128)(2,1)S(1)} %get-tuple-element.53), channel_id=1, source_target_pairs={{264,0},{265,1},{266,2},{267,3},{268,4},{269,5},{270,6},{271,7},{2... | collective-permute-start | bytes 589832 | tf_op jit(solution)/shard_map/ppermute | solution.py:356
  58.4 0.0 collective-permute-done.12.refs_1_
  58.4 1.3 %collective-permute-start.18 = (bf16[3,256,128]{2,1,0:T(8,128)(2,1)S(1)}, bf16[3,256,128]{2,1,0:T(8,128)(2,1)S(1)}, u32[]{:S(2)}, u32[]{:S(2)}) collective-permute-start(bf16[3,256,128]{2,1,0:T(8,128)(2,1)S(1)} %get-tuple-element.54), channel_id=1, source_target_pairs={{264,256},{265,257},{266,258},{267,259},{268,260},{269,261},{270,2... | collective-permute-start | bytes 589832 | tf_op jit(solution)/shard_map/ppermute | solution.py:356
  59.7 1.3 %collective-permute-start.19 = (bf16[3,256,128]{2,1,0:T(8,128)(2,1)S(1)}, bf16[3,256,128]{2,1,0:T(8,128)(2,1)S(1)}, u32[]{:S(2)}, u32[]{:S(2)}) collective-permute-start(bf16[3,256,128]{2,1,0:T(8,128)(2,1)S(1)} %get-tuple-element.55), channel_id=1, source_target_pairs={{272,0},{273,1},{274,2},{275,3},{276,4},{277,5},{278,6},{279,7},{2... | collective-permute-start | bytes 589832 | tf_op jit(solution)/shard_map/ppermute | solution.py:356
  61.0 10.9 %collective-permute-done.15.refs_3_ = bf16[3,256,128]{2,1,0:T(8,128)(2,1)S(1)} collective-permute-done((bf16[3,256,128]{2,1,0:T(8,128)(2,1)S(1)}, bf16[3,256,128]{2,1,0:T(8,128)(2,1)S(1)}, u32[]{:S(2)}, u32[]{:S(2)}) %collective-permute-start.15) | collective-permute-done | bytes 196640 | tf_op jit(solution)/shard_map/ppermute | solution.py:356
  72.0 1.3 %collective-permute-start.20 = (bf16[3,256,128]{2,1,0:T(8,128)(2,1)S(1)}, bf16[3,256,128]{2,1,0:T(8,128)(2,1)S(1)}, u32[]{:S(2)}, u32[]{:S(2)}) collective-permute-start(bf16[3,256,128]{2,1,0:T(8,128)(2,1)S(1)} %get-tuple-element.56), channel_id=1, source_target_pairs={{272,256},{273,257},{274,258},{275,259},{276,260},{277,261},{278,2... | collective-permute-start | bytes 589832 | tf_op jit(solution)/shard_map/ppermute | solution.py:356
  73.3 0.7 collective-permute-start.21
  73.9 8.1 %collective-permute-done.17.refs_5_ = bf16[3,256,128]{2,1,0:T(8,128)(2,1)S(1)} collective-permute-done((bf16[3,256,128]{2,1,0:T(8,128)(2,1)S(1)}, bf16[3,256,128]{2,1,0:T(8,128)(2,1)S(1)}, u32[]{:S(2)}, u32[]{:S(2)}) %collective-permute-start.17) | collective-permute-done | bytes 196640 | tf_op jit(solution)/shard_map/ppermute | solution.py:356
  82.1 5.4 %collective-permute-done.18.refs_6_ = bf16[3,256,128]{2,1,0:T(8,128)(2,1)S(1)} collective-permute-done((bf16[3,256,128]{2,1,0:T(8,128)(2,1)S(1)}, bf16[3,256,128]{2,1,0:T(8,128)(2,1)S(1)}, u32[]{:S(2)}, u32[]{:S(2)}) %collective-permute-start.18) | collective-permute-done | bytes 196640 | tf_op jit(solution)/shard_map/ppermute | solution.py:356
  87.5 0.0 collective-permute-done.20.refs_8_
  87.5 0.0 collective-permute-done.21.refs_9_
  87.5 1.7 %shard_map.33 = bf16[3,256,768]{2,1,0:T(8,128)(2,1)} custom-call(s32[3]{0:T(128)S(1)} %pad_add_fusion.info, bf16[3,256,128]{2,1,0:T(8,128)(2,1)S(1)} %collective-permute-done.11.refs_0_, bf16[3,256,128]{2,1,0:T(8,128)(2,1)S(1)} %collective-permute-done.12.refs_1_, bf16[3,256,128]{2,1,0:T(8,128)(2,1)S(1)} %collective-permute-done.13.refs_2_, ...), custom_call_target="tpu_custom_call" | custom-call | bytes 4000000 | tf_op jit(solution)/shard_map/pallas_call | solution.py:55
  (3 shorter events, 0.0 us)
Async XLA Ops:
  2.6 14.9 %collective-permute-start.3 = (bf16[4,128,768]{2,1,0:T(8,128)(2,1)S(1)}, bf16[4,128,768]{2,1,0:T(8,128)(2,1)S(1)}, u32[]{:S(2)}, u32[]{:S(2)}) collective-permute-start(bf16[4,128,768]{2,1,0:T(8,128)(2,1)S(1)} %get-tuple-element.36), channel_id=1, source_target_pairs={{256,257},{257,256},{258,259},{259,258},{260,261},{261,260},{262,2... | collective-permute-start | bytes 2359304 | tf_op jit(solution)/shard_map/ppermute | solution.py:356
  8.1 16.1 %collective-permute-start = (bf16[896,128]{1,0:T(8,128)(2,1)S(1)}, bf16[896,128]{1,0:T(8,128)(2,1)S(1)}, u32[]{:S(2)}, u32[]{:S(2)}) collective-permute-start(bf16[896,128]{1,0:T(8,128)(2,1)S(1)} %get-tuple-element.32), channel_id=1, source_target_pairs={{0,16},{1,17},{2,18},{3,19},{4,20},{5,21},{6,22},{7,23},{8,24},{9,... | collective-permute-start | bytes 688136 | tf_op jit(solution)/shard_map/ppermute | solution.py:356
  8.7 19.1 %collective-permute-start.1 = (bf16[896,128]{1,0:T(8,128)(2,1)S(1)}, bf16[896,128]{1,0:T(8,128)(2,1)S(1)}, u32[]{:S(2)}, u32[]{:S(2)}) collective-permute-start(bf16[896,128]{1,0:T(8,128)(2,1)S(1)} %get-tuple-element.33), channel_id=1, source_target_pairs={{0,24},{1,25},{2,26},{3,27},{4,28},{5,29},{6,30},{7,31},{8,16},{9,... | collective-permute-start | bytes 688136 | tf_op jit(solution)/shard_map/ppermute | solution.py:356
  9.4 20.4 %collective-permute-start.2 = (bf16[896,128]{1,0:T(8,128)(2,1)S(1)}, bf16[896,128]{1,0:T(8,128)(2,1)S(1)}, u32[]{:S(2)}, u32[]{:S(2)}) collective-permute-start(bf16[896,128]{1,0:T(8,128)(2,1)S(1)} %get-tuple-element.34), channel_id=1, source_target_pairs={{0,8},{1,9},{2,10},{3,11},{4,12},{5,13},{6,14},{7,15},{8,0},{9,1},... | collective-permute-start | bytes 688136 | tf_op jit(solution)/shard_map/ppermute | solution.py:356
  18.2 12.9 %collective-permute-start.4 = (bf16[896,128]{1,0:T(8,128)(2,1)S(1)}, bf16[896,128]{1,0:T(8,128)(2,1)S(1)}, u32[]{:S(2)}, u32[]{:S(2)}) collective-permute-start(bf16[896,128]{1,0:T(8,128)(2,1)S(1)} %get-tuple-element.37), channel_id=1, source_target_pairs={{8,272},{9,273},{10,274},{11,275},{12,276},{13,277},{14,278},{15,2... | collective-permute-start | bytes 688136 | tf_op jit(solution)/shard_map/ppermute | solution.py:356
  22.9 12.2 %collective-permute-start.5 = (bf16[896,128]{1,0:T(8,128)(2,1)S(1)}, bf16[896,128]{1,0:T(8,128)(2,1)S(1)}, u32[]{:S(2)}, u32[]{:S(2)}) collective-permute-start(bf16[896,128]{1,0:T(8,128)(2,1)S(1)} %get-tuple-element.38), channel_id=1, source_target_pairs={{8,264},{9,265},{10,266},{11,267},{12,268},{13,269},{14,270},{15,2... | collective-permute-start | bytes 688136 | tf_op jit(solution)/shard_map/ppermute | solution.py:356
  24.2 11.6 %collective-permute-start.6 = (bf16[896,128]{1,0:T(8,128)(2,1)S(1)}, bf16[896,128]{1,0:T(8,128)(2,1)S(1)}, u32[]{:S(2)}, u32[]{:S(2)}) collective-permute-start(bf16[896,128]{1,0:T(8,128)(2,1)S(1)} %get-tuple-element.39), channel_id=1, source_target_pairs={{0,264},{1,265},{2,266},{3,267},{4,268},{5,269},{6,270},{7,271},{2... | collective-permute-start | bytes 688136 | tf_op jit(solution)/shard_map/ppermute | solution.py:356
  27.8 9.7 %collective-permute-start.7 = (bf16[896,128]{1,0:T(8,128)(2,1)S(1)}, bf16[896,128]{1,0:T(8,128)(2,1)S(1)}, u32[]{:S(2)}, u32[]{:S(2)}) collective-permute-start(bf16[896,128]{1,0:T(8,128)(2,1)S(1)} %get-tuple-element.40), channel_id=1, source_target_pairs={{256,264},{257,265},{258,266},{259,267},{260,268},{261,269},{262,2... | collective-permute-start | bytes 688136 | tf_op jit(solution)/shard_map/ppermute | solution.py:356
  29.8 10.8 %collective-permute-start.8 = (bf16[896,128]{1,0:T(8,128)(2,1)S(1)}, bf16[896,128]{1,0:T(8,128)(2,1)S(1)}, u32[]{:S(2)}, u32[]{:S(2)}) collective-permute-start(bf16[896,128]{1,0:T(8,128)(2,1)S(1)} %get-tuple-element.41), channel_id=1, source_target_pairs={{0,272},{1,273},{2,274},{3,275},{4,276},{5,277},{6,278},{7,279},{2... | collective-permute-start | bytes 688136 | tf_op jit(solution)/shard_map/ppermute | solution.py:356
  31.2 11.9 %collective-permute-start.9 = (bf16[896,128]{1,0:T(8,128)(2,1)S(1)}, bf16[896,128]{1,0:T(8,128)(2,1)S(1)}, u32[]{:S(2)}, u32[]{:S(2)}) collective-permute-start(bf16[896,128]{1,0:T(8,128)(2,1)S(1)} %get-tuple-element.42), channel_id=1, source_target_pairs={{256,272},{257,273},{258,274},{259,275},{260,276},{261,277},{262,2... | collective-permute-start | bytes 688136 | tf_op jit(solution)/shard_map/ppermute | solution.py:356
  35.1 8.0 %collective-permute-start.10 = (bf16[896,128]{1,0:T(8,128)(2,1)S(1)}, bf16[896,128]{1,0:T(8,128)(2,1)S(1)}, u32[]{:S(2)}, u32[]{:S(2)}) collective-permute-start(bf16[896,128]{1,0:T(8,128)(2,1)S(1)} %get-tuple-element.43), channel_id=1, source_target_pairs={{264,272},{265,273},{266,274},{267,275},{268,276},{269,277},{270,2... | collective-permute-start | bytes 688136 | tf_op jit(solution)/shard_map/ppermute | solution.py:356
  50.7 2.7 %collective-permute-start.14 = (bf16[3,512,128]{2,1,0:T(8,128)(2,1)S(1)}, bf16[3,512,128]{2,1,0:T(8,128)(2,1)S(1)}, u32[]{:S(2)}, u32[]{:S(2)}) collective-permute-start(bf16[3,512,128]{2,1,0:T(8,128)(2,1)S(1)} %get-tuple-element.49), channel_id=1, source_target_pairs={{0,1},{1,0},{2,3},{3,2},{4,5},{5,4},{6,7},{7,6},{8,9},{264,265},{9... | collective-permute-start | bytes 1179656 | tf_op jit(solution)/shard_map/ppermute | solution.py:356
  51.4 5.7 %collective-permute-start.11 = (bf16[3,256,128]{2,1,0:T(8,128)(2,1)S(1)}, bf16[3,256,128]{2,1,0:T(8,128)(2,1)S(1)}, u32[]{:S(2)}, u32[]{:S(2)}) collective-permute-start(bf16[3,256,128]{2,1,0:T(8,128)(2,1)S(1)} %get-tuple-element.45.d2), channel_id=1, source_target_pairs={{16,0},{17,1},{18,2},{19,3},{20,4},{21,5},{22,6},{23,7},{24,8},{25... | collective-permute-start | bytes 589832 | tf_op jit(solution)/shard_map/ppermute | solution.py:356
  52.1 6.3 %collective-permute-start.12 = (bf16[3,256,128]{2,1,0:T(8,128)(2,1)S(1)}, bf16[3,256,128]{2,1,0:T(8,128)(2,1)S(1)}, u32[]{:S(2)}, u32[]{:S(2)}) collective-permute-start(bf16[3,256,128]{2,1,0:T(8,128)(2,1)S(1)} %get-tuple-element.46.d3), channel_id=1, source_target_pairs={{24,0},{25,1},{26,2},{27,3},{28,4},{29,5},{30,6},{31,7},{16,8},{17... | collective-permute-start | bytes 589832 | tf_op jit(solution)/shard_map/ppermute | solution.py:356
  52.8 7.0 %collective-permute-start.13 = (bf16[3,256,128]{2,1,0:T(8,128)(2,1)S(1)}, bf16[3,256,128]{2,1,0:T(8,128)(2,1)S(1)}, u32[]{:S(2)}, u32[]{:S(2)}) collective-permute-start(bf16[3,256,128]{2,1,0:T(8,128)(2,1)S(1)} %get-tuple-element.47.d1), channel_id=1, source_target_pairs={{8,0},{9,1},{10,2},{11,3},{12,4},{13,5},{14,6},{15,7},{0,8},{1,9},... | collective-permute-start | bytes 589832 | tf_op jit(solution)/shard_map/ppermute | solution.py:356
  54.5 17.5 %collective-permute-start.15 = (bf16[3,256,128]{2,1,0:T(8,128)(2,1)S(1)}, bf16[3,256,128]{2,1,0:T(8,128)(2,1)S(1)}, u32[]{:S(2)}, u32[]{:S(2)}) collective-permute-start(bf16[3,256,128]{2,1,0:T(8,128)(2,1)S(1)} %get-tuple-element.51), channel_id=1, source_target_pairs={{272,8},{273,9},{274,10},{275,11},{276,12},{277,13},{278,14},{279,... | collective-permute-start | bytes 589832 | tf_op jit(solution)/shard_map/ppermute | solution.py:356
  55.8 17.5 %collective-permute-start.16 = (bf16[3,256,128]{2,1,0:T(8,128)(2,1)S(1)}, bf16[3,256,128]{2,1,0:T(8,128)(2,1)S(1)}, u32[]{:S(2)}, u32[]{:S(2)}) collective-permute-start(bf16[3,256,128]{2,1,0:T(8,128)(2,1)S(1)} %get-tuple-element.52), channel_id=1, source_target_pairs={{264,8},{265,9},{266,10},{267,11},{268,12},{269,13},{270,14},{271,... | collective-permute-start | bytes 589832 | tf_op jit(solution)/shard_map/ppermute | solution.py:356
  57.1 25.0 %collective-permute-start.17 = (bf16[3,256,128]{2,1,0:T(8,128)(2,1)S(1)}, bf16[3,256,128]{2,1,0:T(8,128)(2,1)S(1)}, u32[]{:S(2)}, u32[]{:S(2)}) collective-permute-start(bf16[3,256,128]{2,1,0:T(8,128)(2,1)S(1)} %get-tuple-element.53), channel_id=1, source_target_pairs={{264,0},{265,1},{266,2},{267,3},{268,4},{269,5},{270,6},{271,7},{2... | collective-permute-start | bytes 589832 | tf_op jit(solution)/shard_map/ppermute | solution.py:356
  58.4 29.0 %collective-permute-start.18 = (bf16[3,256,128]{2,1,0:T(8,128)(2,1)S(1)}, bf16[3,256,128]{2,1,0:T(8,128)(2,1)S(1)}, u32[]{:S(2)}, u32[]{:S(2)}) collective-permute-start(bf16[3,256,128]{2,1,0:T(8,128)(2,1)S(1)} %get-tuple-element.54), channel_id=1, source_target_pairs={{264,256},{265,257},{266,258},{267,259},{268,260},{269,261},{270,2... | collective-permute-start | bytes 589832 | tf_op jit(solution)/shard_map/ppermute | solution.py:356
  59.7 27.7 %collective-permute-start.19 = (bf16[3,256,128]{2,1,0:T(8,128)(2,1)S(1)}, bf16[3,256,128]{2,1,0:T(8,128)(2,1)S(1)}, u32[]{:S(2)}, u32[]{:S(2)}) collective-permute-start(bf16[3,256,128]{2,1,0:T(8,128)(2,1)S(1)} %get-tuple-element.55), channel_id=1, source_target_pairs={{272,0},{273,1},{274,2},{275,3},{276,4},{277,5},{278,6},{279,7},{2... | collective-permute-start | bytes 589832 | tf_op jit(solution)/shard_map/ppermute | solution.py:356
  72.0 15.5 %collective-permute-start.20 = (bf16[3,256,128]{2,1,0:T(8,128)(2,1)S(1)}, bf16[3,256,128]{2,1,0:T(8,128)(2,1)S(1)}, u32[]{:S(2)}, u32[]{:S(2)}) collective-permute-start(bf16[3,256,128]{2,1,0:T(8,128)(2,1)S(1)} %get-tuple-element.56), channel_id=1, source_target_pairs={{272,256},{273,257},{274,258},{275,259},{276,260},{277,261},{278,2... | collective-permute-start | bytes 589832 | tf_op jit(solution)/shard_map/ppermute | solution.py:356
  73.3 14.2 %collective-permute-start.21 = (bf16[3,256,128]{2,1,0:T(8,128)(2,1)S(1)}, bf16[3,256,128]{2,1,0:T(8,128)(2,1)S(1)}, u32[]{:S(2)}, u32[]{:S(2)}) collective-permute-start(bf16[3,256,128]{2,1,0:T(8,128)(2,1)S(1)} %get-tuple-element.57), channel_id=1, source_target_pairs={{272,264},{273,265},{274,266},{275,267},{276,268},{277,269},{278,2... | collective-permute-start | bytes 589832 | tf_op jit(solution)/shard_map/ppermute | solution.py:356
